TPU v7x, 512 devices: a whole 4x8x8 slice. The times are simulated.
512 devices in a mesh: seq: 32 (over z_lo, y, core), head: 16 (over z_hi, x).
Axes of the slice: x: 4, y: 8, z: 8 (z_hi: 4, z_lo: 2; z = z_hi * 2 + z_lo), core: 2. Of those that a mesh axis runs over, the one named last changes fastest.
Arguments:
- source_hidden: bfloat16 [8192, 2048], P('seq', 'head'), may hold values from -64 to 64
- target_hidden: bfloat16 [16384, 2048], P('seq', 'head'), may hold values from -64 to 64
- source_length: int32 [1], replicated, may hold values from 4096 to 8192
- target_length: int32 [1], replicated, may hold values from 8192 to 16384
- encoder_gain: float32 [2048], replicated, may hold values from 0.25 to 1.75
- query_weight: bfloat16 [2048, 2048], P(None, 'head'), may hold values from -1 to 1
- key_weight: bfloat16 [2048, 2048], P(None, 'head'), may hold values from -1 to 1
- value_weight: bfloat16 [2048, 2048], P(None, 'head'), may hold values from -0.5 to 0.5
- output_weight: bfloat16 [2048, 2048], P('head'), may hold values from -0.5 to 0.5
- final_gain: float32 [2048], replicated, may hold values from 0.25 to 1.75
- cross_query: bfloat16 [2048, 2048], P(None, 'head'), may hold values from -1 to 1
- cross_key: bfloat16 [2048, 2048], P(None, 'head'), may hold values from -1 to 1
- cross_value: bfloat16 [2048, 2048], P(None, 'head'), may hold values from -0.5 to 0.5
- cross_gain: float32 [2048], replicated, may hold values from 0.25 to 1.75
Outputs:
- encoder_out: bfloat16 [8192, 2048], P('seq', 'head')
- cross_context: bfloat16 [16384, 2048], P('seq', 'head')
All inputs are finite; a program needn't handle non-finite values.
Results may differ from a plain program's by a relative error of at most 0.03.
Values may be sent and summed in bfloat16 or wider, within the bound.
No kernel may reach another device: no remote copies, remote signals or barrier semaphores. Data moves between devices by JAX's collectives and lax.ppermute only.
A program may use at most 64 MiB of HBM per device.

v0:
```python
import math

import jax
import jax.numpy as jnp
from jax import lax
from jax.sharding import PartitionSpec as P

HD = 128


EPSILON = 1e-05
MASKED = -1e30


def layer_norm(hidden, scale_gain):
    floats = hidden.astype(jnp.float32)
    center = floats - jnp.mean(floats, axis=-1, keepdims=True)
    spread = jnp.mean(center * center, axis=-1, keepdims=True)
    return (center * lax.rsqrt(spread + EPSILON) * scale_gain).astype(jnp.bfloat16)


def project(normed, weight):
    return jnp.dot(normed, weight, preferred_element_type=jnp.float32).astype(jnp.bfloat16)


def make_fold(queries, key_limit):
    head_count = queries.shape[1] // HD
    row_count = queries.shape[0]
    grouped = queries.reshape(row_count, head_count, HD)

    def fold_keys(running, pieces, first_row):
        key_rows, value_rows = pieces
        key_count = key_rows.shape[0]
        block_size = math.gcd(key_count, 1024)

        def block_step(block_index, carried):
            running_max, denominator, context_sum = carried
            offset = block_index * block_size
            key_block = lax.dynamic_slice_in_dim(key_rows, offset, block_size, 0).reshape(
                block_size, head_count, HD
            )
            value_block = lax.dynamic_slice_in_dim(value_rows, offset, block_size, 0).reshape(
                block_size, head_count, HD
            )
            places = offset + lax.iota(jnp.int32, block_size)
            usable = (places < key_limit)[None, None, :]
            scores = jnp.einsum(
                "rhd,khd->hrk", grouped, key_block, preferred_element_type=jnp.float32
            ) * HD ** (-0.5)
            scores = jnp.where(usable, scores, MASKED)
            new_max = jnp.maximum(running_max, jnp.max(scores, axis=-1))
            weights = jnp.where(usable, jnp.exp(scores - new_max[:, :, None]), 0.0)
            rescale = jnp.exp(running_max - new_max)
            denominator = denominator * rescale + jnp.sum(weights, axis=-1)
            update = jnp.einsum(
                "hrk,khd->rhd",
                weights.astype(jnp.bfloat16),
                value_block,
                preferred_element_type=jnp.float32,
            )
            context_sum = context_sum * rescale.T[:, :, None] + update
            return (new_max, denominator, context_sum)

        return lax.fori_loop(0, key_count // block_size, block_step, running)

    initial = (
        jnp.full((head_count, row_count), MASKED, jnp.float32),
        jnp.zeros((head_count, row_count), jnp.float32),
        jnp.zeros((row_count, head_count, HD), jnp.float32),
    )
    return (fold_keys, initial)


def finish(running):
    running_max, denominator, context_sum = running
    row_count = context_sum.shape[0]
    return (context_sum / denominator.T[:, :, None]).reshape(row_count, -1)


def shards(
    source_hidden,
    target_hidden,
    source_length,
    target_length,
    encoder_gain,
    query_weight,
    key_weight,
    value_weight,
    output_weight,
    final_gain,
    cross_query,
    cross_key,
    cross_value,
    cross_gain,
):
    source_full, target_full = (
        lax.all_gather(source_hidden, "head", axis=1, tiled=True),
        lax.all_gather(target_hidden, "head", axis=1, tiled=True),
    )
    key_limit = source_length[0]
    source_norm = layer_norm(source_full, encoder_gain)
    queries = project(source_norm, query_weight)
    keys_local = project(source_norm, key_weight)
    values_local = project(source_norm, value_weight)
    folder, initial = make_fold(queries, key_limit)
    attended = folder(
        initial,
        (
            lax.all_gather(keys_local, "seq", axis=0, tiled=True),
            lax.all_gather(values_local, "seq", axis=0, tiled=True),
        ),
        jnp.int32(0),
    )
    encoder_context = finish(attended).astype(jnp.bfloat16)
    partial_sum = jnp.dot(encoder_context, output_weight, preferred_element_type=jnp.float32)
    share_sum = lax.psum_scatter(
        partial_sum.astype(jnp.bfloat16), "head", scatter_dimension=1, tiled=True
    ).astype(jnp.float32)
    encoder_out = (source_hidden.astype(jnp.float32) + share_sum).astype(jnp.bfloat16)
    encoder_full = lax.all_gather(encoder_out, "head", axis=1, tiled=True)
    encoder_final = layer_norm(encoder_full, final_gain)
    memory_keys = project(encoder_final, cross_key)
    memory_values = project(encoder_final, cross_value)
    target_norm = layer_norm(target_full, cross_gain)
    target_queries = project(target_norm, cross_query)
    cross_folder, cross_initial = make_fold(target_queries, key_limit)
    crossed = cross_folder(
        cross_initial,
        (
            lax.all_gather(memory_keys, "seq", axis=0, tiled=True),
            lax.all_gather(memory_values, "seq", axis=0, tiled=True),
        ),
        jnp.int32(0),
    )
    target_rows = target_hidden.shape[0]
    positions = lax.axis_index("seq") * target_rows + lax.iota(jnp.int32, target_rows)
    live_rows = (positions < target_length[0])[:, None]
    cross_context = jnp.where(live_rows, finish(crossed), 0.0).astype(jnp.bfloat16)
    return (encoder_out, cross_context)


def solution(mesh):
    in_specs = (
        P("seq", "head"),
        P("seq", "head"),
        P(),
        P(),
        P(),
        P(None, "head"),
        P(None, "head"),
        P(None, "head"),
        P("head", None),
        P(),
        P(None, "head"),
        P(None, "head"),
        P(None, "head"),
        P(),
    )
    out_specs = (P("seq", "head"), P("seq", "head"))
    return jax.shard_map(shards, mesh=mesh, in_specs=in_specs, out_specs=out_specs, check_vma=False)
```

profile of v0, /device:TPU:1, one launch (start us, length us, event | category | flops | bytes accessed | tf_op | source)
XLA Modules:
  0.0 650.4 jit_solution(5712484617599095575)
XLA Ops:
  8.0 68.6 %all-gather.8.cloned.1.call-done = bf16[256,2048]{1,0:T(8,128)(2,1)} async-done(((bf16[256,128]{1,0:T(8,128)(2,1)}), bf16[256,2048]{1,0:T(8,128)(2,1)}) %all-gather.8.cloned.1.call-update) | async-done | bytes 1048592 | tf_op jit(solution)/shard_map/all_gather | solution.py:97
  76.6 1.5 convert_reduce_fusion.2
  78.1 1.6 fusion.50
  83.0 63.3 %all-gather.10.cloned.1.call-done = bf16[8192,128]{1,0:T(8,128)(2,1)} async-done(((bf16[256,128]{1,0:T(8,128)(2,1)}), bf16[8192,128]{1,0:T(8,128)(2,1)}) %all-gather.10.cloned.1.call-update) | async-done | bytes 2097168 | tf_op jit(solution)/shard_map/all_gather | solution.py:109
  146.3 69.8 %all-gather.12.cloned.1.call-done = bf16[8192,128]{1,0:T(8,128)(2,1)} async-done(((bf16[256,128]{1,0:T(8,128)(2,1)}), bf16[8192,128]{1,0:T(8,128)(2,1)}) %all-gather.12.cloned.1.call-update) | async-done | bytes 2097168 | tf_op jit(solution)/shard_map/all_gather | solution.py:110
  216.1 29.3 %while.36 = (s32[]{:T(128)}, f32[1,256]{1,0:T(1,128)S(1)}, f32[1,256]{1,0:T(1,128)S(1)}, f32[256,1,128]{0,2,1:T(8,128)S(1)}, s32[]{:T(128)}, /*index=5*/bf16[819...) while((s32[]{:T(128)}, f32[1,256]{1,0:T(1,128)S(1)}, ...), condition=%wide.region_5.6_spmd.clone, body=%wide.region_2.5_spmd.clone.sunk | while | flops 136678656 | bytes 4018367 | solution.py:64
  216.7 1.3 fusion.96
  218.3 1.4 fusion.100
  220.4 1.3 fusion.96
  222.0 1.4 fusion.100
  224.1 1.3 fusion.96
  225.7 1.4 fusion.100
  227.7 1.3 fusion.96
  229.3 1.4 fusion.100
  231.4 1.3 fusion.96
  233.0 1.4 fusion.100
  235.1 1.3 fusion.96
  236.6 1.4 fusion.100
  238.7 1.3 fusion.96
  240.3 1.4 fusion.100
  242.4 1.3 fusion.96
  244.0 1.4 fusion.100
  245.9 1.3 copy.21
  247.2 89.8 %reduce-scatter.4.cloned.1.call-done = bf16[128,256]{1,0:T(8,128)(2,1)} async-done(((bf16[2048,256]{1,0:T(8,128)(2,1)}), bf16[128,256]{1,0:T(8,128)(2,1)}) %reduce-scatter.4.cloned.1.call-update) | async-done | bytes 65552
  339.3 60.9 %all-gather.14.cloned.1.call-done = bf16[256,2048]{1,0:T(8,128)(2,1)} async-done(((bf16[256,128]{1,0:T(8,128)(2,1)}), bf16[256,2048]{1,0:T(8,128)(2,1)}) %all-gather.14.cloned.1.call-update) | async-done | bytes 1048592 | tf_op jit(solution)/shard_map/all_gather | solution.py:120
  400.2 1.5 convert_reduce_fusion.1
  401.8 1.7 fusion.47
  406.7 62.5 %all-gather.18.cloned.1.call-done = bf16[512,2048]{1,0:T(8,128)(2,1)} async-done(((bf16[512,128]{1,0:T(8,128)(2,1)}), bf16[512,2048]{1,0:T(8,128)(2,1)}) %all-gather.18.cloned.1.call-update) | async-done | bytes 2097168 | tf_op jit(solution)/shard_map/all_gather | solution.py:98
  469.2 2.1 convert_reduce_fusion
  473.0 64.2 %all-gather.20.cloned.1.call-done = bf16[8192,128]{1,0:T(8,128)(2,1)} async-done(((bf16[256,128]{1,0:T(8,128)(2,1)}), bf16[8192,128]{1,0:T(8,128)(2,1)}) %all-gather.20.cloned.1.call-update) | async-done | bytes 2097168 | tf_op jit(solution)/shard_map/all_gather | solution.py:131
  537.2 70.0 %all-gather.16.cloned.1.call-done = bf16[8192,128]{1,0:T(8,128)(2,1)} async-done(((bf16[256,128]{1,0:T(8,128)(2,1)}), bf16[8192,128]{1,0:T(8,128)(2,1)}) %all-gather.16.cloned.1.call-update) | async-done | bytes 2097168 | tf_op jit(solution)/shard_map/all_gather | solution.py:130
  607.1 35.5 %while.37 = (s32[]{:T(128)}, f32[1,512]{1,0:T(1,128)S(1)}, f32[1,512]{1,0:T(1,128)S(1)}, f32[512,1,128]{0,2,1:T(8,128)S(1)}, s32[]{:T(128)}, /*index=5*/bf16[819...) while((s32[]{:T(128)}, f32[1,512]{1,0:T(1,128)S(1)}, ...), condition=%wide.region_14.15_spmd.clone, body=%wide.region_11.14_spmd.clone.sunk | while | flops 275452416 | bytes 7508159 | solution.py:64
  607.8 1.4 fusion.103
  609.8 1.7 fusion.107
  612.2 1.4 fusion.103
  614.3 1.7 fusion.107
  616.7 1.4 fusion.103
  618.7 1.7 fusion.107
  621.1 1.4 fusion.103
  623.1 1.7 fusion.107
  625.5 1.4 fusion.103
  627.6 1.7 fusion.107
  630.0 1.4 fusion.103
  632.0 1.7 fusion.107
  634.4 1.4 fusion.103
  636.4 1.7 fusion.107
  638.8 1.4 fusion.103
  640.9 1.7 fusion.107
  (150 shorter events, 29.1 us)
Async XLA Ops:
  7.2 238.2 %copy-start = (bf16[128,2048]{1,0:T(8,128)(2,1)S(1)}, bf16[128,2048]{1,0:T(8,128)(2,1)}, u32[]{:S(2)}) copy-start(bf16[128,2048]{1,0:T(8,128)(2,1)} %param.26) | copy-start | bytes 1572868
  7.2 72.6 %copy-start.8 = (f32[2048]{0:T(1024)S(1)}, f32[2048]{0:T(1024)}, u32[]{:S(2)}) copy-start(f32[2048]{0:T(1024)} %param.22) | copy-start | bytes 24580
  7.2 69.4 %all-gather.8.cloned.1.call-start = ((), (), s32[]{:S(2)}) async-start(), calls=%async_computation.1 | async-start | bytes 1114112 | tf_op jit(solution)/shard_map/all_gather | solution.py:97
  7.9 72.3 %copy-start.4 = (bf16[2048,128]{1,0:T(8,128)(2,1)S(1)}, bf16[2048,128]{1,0:T(8,128)(2,1)}, u32[]{:S(2)}) copy-start(bf16[2048,128]{1,0:T(8,128)(2,1)} %param.24) | copy-start | bytes 1572868
  7.9 138.4 %all-gather.10.cloned.1.call-start = ((), (), s32[]{:S(2)}) async-start(), calls=%async_computation.2 | async-start | bytes 2162688 | tf_op jit(solution)/shard_map/all_gather | solution.py:109
  76.6 3.2 copy-start.1
  79.8 1.6 copy-start.5
  80.2 2.3 copy-start.6
  81.3 134.8 %all-gather.12.cloned.1.call-start = ((), (), s32[]{:S(2)}) async-start(), calls=%async_computation.3 | async-start | bytes 2162688 | tf_op jit(solution)/shard_map/all_gather | solution.py:110
  82.5 254.6 %reduce-scatter.4.cloned.1.call-start = ((), (), s32[]{:S(2)}) async-start(), calls=%async_computation.8 | async-start | bytes 1114112
  245.4 92.6 %copy-start.7 = (bf16[256,128]{1,0:T(8,128)(2,1)S(1)}, bf16[256,128]{1,0:T(8,128)(2,1)}, u32[]{:S(2)}) copy-start(bf16[256,128]{1,0:T(8,128)(2,1)} %param.18) | copy-start | bytes 196612
  247.2 156.3 %copy-start.9 = (bf16[2048,128]{1,0:T(8,128)(2,1)S(1)}, bf16[2048,128]{1,0:T(8,128)(2,1)}, u32[]{:S(2)}) copy-start(bf16[2048,128]{1,0:T(8,128)(2,1)} %param.30) | copy-start | bytes 1572868
  247.2 156.3 %copy-start.12 = (f32[2048]{0:T(1024)S(1)}, f32[2048]{0:T(1024)}, u32[]{:S(2)}) copy-start(f32[2048]{0:T(1024)} %param.27) | copy-start | bytes 24580
  247.2 153.0 %all-gather.14.cloned.1.call-start = ((), (), s32[]{:S(2)}) async-start(), calls=%async_computation.4 | async-start | bytes 1114112 | tf_op jit(solution)/shard_map/all_gather | solution.py:120
  338.7 130.5 %all-gather.18.cloned.1.call-start = ((), (), s32[]{:S(2)}) async-start(), calls=%async_computation.6 | async-start | bytes 2228224 | tf_op jit(solution)/shard_map/all_gather | solution.py:98
  339.3 197.9 %all-gather.20.cloned.1.call-start = ((), (), s32[]{:S(2)}) async-start(), calls=%async_computation.7 | async-start | bytes 2162688 | tf_op jit(solution)/shard_map/all_gather | solution.py:131
  400.2 3.3 copy-start.3
  401.8 3.0 copy-start.10
  404.7 202.4 %all-gather.16.cloned.1.call-start = ((), (), s32[]{:S(2)}) async-start(), calls=%async_computation.5 | async-start | bytes 2162688 | tf_op jit(solution)/shard_map/all_gather | solution.py:130
  469.2 2.2 copy-start.2
  469.2 2.9 copy-start.11
  469.2 2.9 copy-start.13
Sparse Core Ops, SparseCore 0:
  11.0 65.5 all-gather.7
  81.4 64.8 all-gather.9
  149.0 66.9 all-gather.11
  247.3 89.7 reduce-scatter.3
  340.9 59.2 all-gather.13
  403.5 65.6 all-gather.17
  471.6 65.5 all-gather.19
  540.1 66.9 all-gather.15
where the time goes:
time: 652 us; the launch traced here: 650 us
  waiting for transfers between devices  550 us (84%)
  matrix products  52.6 us (8%)
  other arithmetic  28.4 us (4%)
  between operations  15.1 us (2%)
    unnamed x9, waiting for transfers between devices  91.1 us
    all_gather x1, waiting for transfers between devices, shards(): lax.all_gather(memory_keys, 'seq', axis=0, tiled=True)  70 us
    all_gather x1, waiting for transfers between devices, shards(): lax.all_gather(values_local, 'seq', axis=0, tiled=True)  69.8 us
    all_gather x1, waiting for transfers between devices, shards(): lax.all_gather(source_hidden, 'head', axis=1, tiled=True)  68.6 us
    all_gather x1, waiting for transfers between devices, shards(): lax.all_gather(memory_values, 'seq', axis=0, tiled=True)  64.2 us
    all_gather x1, waiting for transfers between devices, shards(): lax.all_gather(keys_local, 'seq', axis=0, tiled=True)  63.3 us
    all_gather x1, waiting for transfers between devices, shards(): lax.all_gather(target_hidden, 'head', axis=1, tiled=True)  62.5 us
    all_gather x1, waiting for transfers between devices, shards(): encoder_full = lax.all_gather(encoder_out, 'head', axis=1, tiled=True)  60.9 us
  transfers between devices with their start and end apart: 8, of which 8 were waited for; matrix products, arithmetic and copies ran while one was open for 2% of the time, Pallas kernels for 0%

commit v1 on v0

v1 whole, which is shorter than its diff:
```python
import functools
import math

import jax
import jax.numpy as jnp
from jax import lax
from jax.experimental import pallas as pl
from jax.experimental.pallas import tpu as pltpu
from jax.sharding import Mesh, PartitionSpec as P

HD = 128
D = 2048
EPSILON = 1e-05
MASKED = -1e30
SCORE_SCALE = HD ** (-0.5) * math.log2(math.e)
F32 = jnp.float32
BF16 = jnp.bfloat16

AXES = (("zl", 2), ("yh", 4), ("yl", 2), ("c", 2), ("zh", 4), ("x", 4))
SEQ = ("zl", "yh", "yl", "c")
HEAD = ("zh", "x")
QUERY_GROUP = ("zl", "yl", "c")
VMEM = pl.BlockSpec(memory_space=pltpu.VMEM)
SMEM = pl.BlockSpec(memory_space=pltpu.SMEM)
VMEM_LIMIT = 48 * 1024 * 1024


def call(kernel, out_shape, *args, specs, scratch=(), flops=0, transcendentals=0):
    outs = jax.tree.leaves(out_shape)
    size = sum(math.prod(a.shape) * a.dtype.itemsize for a in (*args, *outs))
    return pl.pallas_call(
        kernel,
        out_shape=out_shape,
        in_specs=specs,
        out_specs=jax.tree.map(lambda _: VMEM, out_shape),
        scratch_shapes=scratch,
        compiler_params=pltpu.CompilerParams(vmem_limit_bytes=VMEM_LIMIT),
        cost_estimate=pl.CostEstimate(flops=flops, bytes_accessed=size, transcendentals=transcendentals),
    )(*args)


def shape(*dims, dtype=BF16):
    return jax.ShapeDtypeStruct(dims, dtype)


def normed_rows(pieces, gains):
    total = functools.reduce(jnp.add, pieces)
    mean = jnp.sum(total, axis=-1, keepdims=True) * (1.0 / D)
    centers = [p - mean for p in pieces]
    squares = functools.reduce(jnp.add, [c * c for c in centers])
    spread = jnp.sum(squares, axis=-1, keepdims=True) * (1.0 / D)
    inverse = lax.rsqrt(spread + EPSILON)
    return [(c * inverse * g).astype(BF16) for c, g in zip(centers, gains)]


def norm_gathered(x_ref, gain_ref, norm_ref, step=64):
    rows = x_ref.shape[1]

    def body(i, _):
        r = pl.multiple_of(i * step, step)
        pieces = [x_ref[j, pl.ds(r, step), :].astype(F32) for j in range(16)]
        gains = [gain_ref[:, j * 128 : (j + 1) * 128] for j in range(16)]
        for j, n in enumerate(normed_rows(pieces, gains)):
            norm_ref[pl.ds(r, step), j * 128 : (j + 1) * 128] = n
        return 0

    lax.fori_loop(0, rows // step, body, 0)


def qkv_kernel(x_ref, gain_ref, wq_ref, wk_ref, wv_ref, q_ref, kv_ref, norm_ref):
    norm_gathered(x_ref, gain_ref, norm_ref)
    weights = jnp.concatenate([wq_ref[...], wk_ref[...], wv_ref[...]], axis=1)
    out = jnp.dot(norm_ref[...], weights, preferred_element_type=F32)
    q = (out[:, :128] * SCORE_SCALE).astype(BF16)
    k = out[:, 128:256].astype(BF16)
    v = out[:, 256:].astype(BF16)
    for a in range(q_ref.shape[0]):
        q_ref[a] = q
    for b in range(kv_ref.shape[0]):
        kv_ref[b, 0] = k
        kv_ref[b, 1] = v


def target_kernel(x_ref, gain_ref, wq_ref, q_ref, norm_ref):
    norm_gathered(x_ref, gain_ref, norm_ref)
    out = jnp.dot(norm_ref[...], wq_ref[...], preferred_element_type=F32)
    q_ref[...] = (out * SCORE_SCALE).astype(BF16)


def attend_kernel(part, info_ref, q_ref, kv_ref, out_ref, ka_ref, va_ref, qa_ref):
    members, rows, _ = q_ref.shape
    blocks, pieces, _, n, _ = kv_ref.shape
    base, limit, stride = info_ref[0], info_ref[1], info_ref[2]
    lane = lax.broadcasted_iota(jnp.int32, (n, 128), 1)
    row = lax.broadcasted_iota(jnp.int32, (n, 128), 0)
    for b in range(blocks):
        for t in range(pieces):
            at = (b * pieces + t) * n
            place = base + b * stride + t * n + row
            bias = jnp.where((lane == 0) & (place >= limit), MASKED, 0.0).astype(BF16)
            ka_ref[at : at + n, :128] = kv_ref[b, t, 0]
            ka_ref[at : at + n, 128:] = bias
            va_ref[at : at + n, :128] = kv_ref[b, t, 1]
            va_ref[at : at + n, 128:] = jnp.ones((n, 128), BF16)
    qlane = lax.broadcasted_iota(jnp.int32, (rows, 128), 1)
    qa_ref[:, 128:] = jnp.where(qlane == 0, 1.0, 0.0).astype(BF16)
    group = min(part, 128)
    groups = part // group
    eye = lax.broadcasted_iota(jnp.int32, (group, 128), 0) == lax.broadcasted_iota(jnp.int32, (group, 128), 1)
    block = min(rows, 256)

    def body(a, _):
        for r in range(0, rows, block):
            qa_ref[r : r + block, :128] = q_ref[a, r : r + block, :]
            scores = lax.dot_general(
                qa_ref[r : r + block, :], ka_ref[...], (((1,), (1,)), ((), ())), preferred_element_type=F32
            )
            top = jnp.max(scores, axis=1, keepdims=True)
            weights = jnp.exp2(scores - top).astype(BF16)
            summed = jnp.dot(weights, va_ref[...], preferred_element_type=F32)
            denominator = summed[:, 128:]
            context = (summed[:, :128] / denominator).astype(BF16)
            level = top + jnp.log2(denominator)
            for g in range(block // group):
                at = r + g * group
                p, inside = at // part, at % part
                out_ref[a, p, inside : inside + group, :] = context[g * group : (g + 1) * group]
                line = jnp.sum(jnp.where(eye, level[g * group : (g + 1) * group], 0.0), axis=0, keepdims=True)
                stat_ref_store(out_ref, a, p, part, inside // group, groups, line)
        return 0

    lax.fori_loop(0, members, body, 0)


def stat_ref_store(out_ref, a, p, part, g, groups, line):
    high = line.astype(BF16)
    rest = line - high.astype(F32)
    middle = rest.astype(BF16)
    low = (rest - middle.astype(F32)).astype(BF16)
    out_ref[a, p, part + g : part + g + 1, :] = high
    out_ref[a, p, part + groups + g : part + groups + g + 1, :] = middle
    out_ref[a, p, part + 2 * groups + g : part + 2 * groups + g + 1, :] = low


def mixing(levels):
    top = functools.reduce(jnp.maximum, levels)
    raw = [jnp.exp2(v - top) for v in levels]
    total = functools.reduce(jnp.add, raw)
    return [v / total for v in raw]


def combined(read_rows, read_stats, members, part):
    group = min(part, 128)
    groups = part // group
    eye = lax.broadcasted_iota(jnp.int32, (group, 128), 0) == lax.broadcasted_iota(jnp.int32, (group, 128), 1)
    levels = []
    for a in range(members):
        stats = read_stats(a).astype(F32)
        levels.append(stats[:groups] + stats[groups : 2 * groups] + stats[2 * groups : 3 * groups])
    shares = mixing(levels)
    out = []
    for g in range(groups):
        total = None
        for a in range(members):
            column = jnp.sum(jnp.where(eye, shares[a][g : g + 1], 0.0), axis=1, keepdims=True)
            term = read_rows(a)[g * group : (g + 1) * group].astype(F32) * column
            total = term if total is None else total + term
        out.append(total)
    return out


def project_out_kernel(r_ref, w_ref, out_ref, ctx_ref):
    members, heads, full, _ = r_ref.shape
    part = full - 16
    for h in range(heads):
        pieces = combined(
            lambda a: r_ref[a, h, :part, :], lambda a: r_ref[a, h, part:, :], members, part
        )
        ctx_ref[:, h * 128 : (h + 1) * 128] = pieces[0].astype(BF16)
    out = jnp.dot(ctx_ref[...], w_ref[...], preferred_element_type=F32).astype(BF16)
    for z in range(4):
        out_ref[z] = out[z * 16 : (z + 1) * 16]


def residual_kernel(r_ref, s_ref, out_ref):
    for j in range(16):
        cols = slice(j * 128, (j + 1) * 128)
        total = s_ref[j].astype(F32)
        for z in range(4):
            total = total + r_ref[z, :, cols].astype(F32)
        total = total.astype(BF16)
        for z in range(4):
            out_ref[z, :, cols] = total


def memory_kernel(e_ref, gain_ref, wk_ref, wv_ref, kv_ref, norm_ref):
    pieces = [e_ref[:, j * 128 : (j + 1) * 128].astype(F32) for j in range(16)]
    gains = [gain_ref[:, j * 128 : (j + 1) * 128] for j in range(16)]
    for j, n in enumerate(normed_rows(pieces, gains)):
        norm_ref[:, j * 128 : (j + 1) * 128] = n
    for h in range(4):
        weights = jnp.concatenate([wk_ref[h], wv_ref[h]], axis=1)
        out = jnp.dot(norm_ref[...], weights, preferred_element_type=F32).astype(BF16)
        for b in range(4):
            kv_ref[b, h, 0] = out[:, :128]
            kv_ref[b, h, 1] = out[:, 128:]


def finish_kernel(info_ref, r_ref, out_ref):
    members, full, _ = r_ref.shape
    part = full - 16
    pieces = combined(lambda a: r_ref[a, :part, :], lambda a: r_ref[a, part:, :], members, part)
    first, limit = info_ref[0], info_ref[1]
    for g, piece in enumerate(pieces):
        n = piece.shape[0]
        place = first + g * n + lax.broadcasted_iota(jnp.int32, (n, 128), 0)
        out_ref[g * n : (g + 1) * n, :] = jnp.where(place < limit, piece, 0.0).astype(BF16)


def exchange(x, axes):
    return lax.all_to_all(x, axes, 0, 0, tiled=True)


def attend(q, kv, info, part):
    members, rows, _ = q.shape
    keys = kv.shape[0] * kv.shape[1] * kv.shape[3]
    return call(
        functools.partial(attend_kernel, part),
        shape(members, rows // part, part + 16, 128),
        info,
        q,
        kv,
        specs=[SMEM, VMEM, VMEM],
        scratch=[pltpu.VMEM((keys, 256), BF16), pltpu.VMEM((keys, 256), BF16), pltpu.VMEM((rows, 256), BF16)],
        flops=4 * members * rows * keys * 256,
        transcendentals=members * rows * keys,
    )


def shards(
    source_hidden,
    target_hidden,
    source_length,
    target_length,
    encoder_gain,
    query_weight,
    key_weight,
    value_weight,
    output_weight,
    final_gain,
    cross_query,
    cross_key,
    cross_value,
    cross_gain,
):
    rows = source_hidden.shape[0]
    target_rows = target_hidden.shape[0]
    at = {name: lax.axis_index(name) for name, _ in AXES}
    seq_at = ((at["zl"] * 4 + at["yh"]) * 2 + at["yl"]) * 2 + at["c"]
    key_base = ((at["zl"] * 8 + at["yl"]) * 2 + at["c"]) * rows
    key_info = jnp.stack([key_base, source_length[0], jnp.int32(4 * rows)])
    target_info = jnp.stack([seq_at * target_rows, target_length[0]])
    gains = [g.reshape(1, D) for g in (encoder_gain, final_gain, cross_gain)]

    out_weight = lax.all_gather(output_weight, "x", axis=0, tiled=True)
    memory_key_weight = lax.all_gather(cross_key, "x", axis=0)
    memory_value_weight = lax.all_gather(cross_value, "x", axis=0)
    target_full = lax.all_gather(target_hidden, HEAD, axis=0)

    source_full = exchange(jnp.broadcast_to(source_hidden[None], (16, rows, 128)), HEAD)
    queries, keys_values = call(
        qkv_kernel,
        (shape(8, rows, 128), shape(4, 2, rows, 128)),
        source_full,
        gains[0],
        query_weight,
        key_weight,
        value_weight,
        specs=[VMEM] * 5,
        scratch=[pltpu.VMEM((rows, D), BF16)],
        flops=2 * rows * D * 384,
    )
    queries = exchange(queries, QUERY_GROUP)
    keys_values = exchange(keys_values, "yh")
    partial = attend(queries, keys_values.reshape(4, 1, 2, rows, 128), key_info, rows // 4)
    partial = exchange(partial.reshape(32, rows // 4 + 16, 128), QUERY_GROUP + ("x",))
    quarter = rows // 4
    shares = call(
        project_out_kernel,
        shape(4, quarter // 4, D),
        partial.reshape(8, 4, quarter + 16, 128),
        out_weight,
        specs=[VMEM] * 2,
        scratch=[pltpu.VMEM((quarter, 512), BF16)],
        flops=2 * quarter * 512 * D,
    )
    shares = exchange(shares, "zh")
    first = at["x"] * quarter + at["zh"] * (quarter // 4)
    own_source = lax.dynamic_slice_in_dim(source_full, first, quarter // 4, 1)
    encoder_rows = call(
        residual_kernel, shape(4, quarter // 4, D), shares, own_source, specs=[VMEM] * 2
    )
    encoder_rows = exchange(encoder_rows, "zh").reshape(quarter, D)
    memory = call(
        memory_kernel,
        shape(4, 4, 2, quarter, 128),
        encoder_rows,
        gains[1],
        memory_key_weight,
        memory_value_weight,
        specs=[VMEM] * 4,
        scratch=[pltpu.VMEM((quarter, D), BF16)],
        flops=2 * quarter * D * 1024,
    )
    encoder_full = lax.all_gather(encoder_rows, "x", axis=0, tiled=True)
    head_at = at["zh"] * 4 + at["x"]
    encoder_out = lax.dynamic_slice_in_dim(encoder_full, head_at * 128, 128, 1)

    target_queries = call(
        target_kernel,
        shape(target_rows, 128),
        target_full,
        gains[2],
        cross_query,
        specs=[VMEM] * 3,
        scratch=[pltpu.VMEM((target_rows, D), BF16)],
        flops=2 * target_rows * D * 128,
    )
    target_queries = lax.all_gather(target_queries, QUERY_GROUP, axis=0)
    memory = exchange(memory.reshape(16, 2, quarter, 128), ("yh", "x")).reshape(4, 4, 2, quarter, 128)
    crossed = attend(target_queries, memory, key_info, target_rows)
    crossed = exchange(crossed.reshape(8, target_rows + 16, 128), QUERY_GROUP)
    cross_context = call(
        finish_kernel, shape(target_rows, 128), target_info, crossed, specs=[SMEM, VMEM]
    )
    return (encoder_out, cross_context)


def solution(mesh):
    fine = Mesh(mesh.devices.reshape([size for _, size in AXES]), [name for name, _ in AXES])
    columns = P(None, HEAD)
    in_specs = (
        P(SEQ, HEAD),
        P(SEQ, HEAD),
        P(),
        P(),
        P(),
        columns,
        columns,
        columns,
        P(HEAD, None),
        P(),
        columns,
        columns,
        columns,
        P(),
    )
    out_specs = (P(SEQ, HEAD), P(SEQ, HEAD))
    return jax.shard_map(shards, mesh=fine, in_specs=in_specs, out_specs=out_specs, check_vma=False)
```

time: 652 us -> 303 us (0.46)
  waiting for transfers between devices: 550 us -> 154 us
  starting transfers between devices: 0.32 us -> 53.4 us
  matrix products: 52.6 us -> 0 us
  blocking collectives: 0 us -> 36.3 us
  Pallas kernels: 0 us -> 32.2 us
  other arithmetic: 28.4 us -> 0.15 us
  local copies, waits for them, and re-layouts: 2.59 us -> 10.4 us
    all_gather x7 -> x6, waiting for transfers between devices: 459 us -> 124 us  [the longest x1 38.2 us: shards(): memory_value_weight = lax.all_gather(cross_value, 'x', axis=0)]
    unnamed x9 -> x6, waiting for transfers between devices: 91.1 us -> 3.18 us
    all_to_all x0 -> x7, starting transfers between devices: none -> 53.3 us  [exchange(): return lax.all_to_all(x, axes, 0, 0, tiled=True)]
    dot_general x39 -> x0, matrix products: 52.6 us -> none  [the longest x16 24.6 us: block_step(): jnp.einsum('hrk,khd->rhd', weights.astype(jnp.bfloat16), value_block, pre...]
    all_to_all x0 -> x1, blocking collectives: none -> 36.3 us  [exchange(): return lax.all_to_all(x, axes, 0, 0, tiled=True)]
    pallas_call x0 -> x8, Pallas kernels: none -> 32.2 us  [call(): pl.pallas_call(kernel, out_shape=out_shape, in_specs=specs, out_specs=jax...]
    all_to_all x0 -> x7, waiting for transfers between devices: none -> 27.4 us  [exchange(): return lax.all_to_all(x, axes, 0, 0, tiled=True)]
    reduce_sum x22 -> x0, other arithmetic: 15.6 us -> none  [the longest x16 6.42 us: block_step(): denominator = denominator * rescale + jnp.sum(weights, axis=-1)]
  transfers between devices with their start and end apart: 8 -> 13, of which waited for: 8 -> 8; matrix products, arithmetic and copies ran while one was open for 2% -> 1% of each run, Pallas kernels for 0% -> 6%
where the time goes in v1:
time: 303 us
  waiting for transfers between devices  154 us (51%)
  starting transfers between devices  53.4 us (18%)
  blocking collectives  36.3 us (12%)
  Pallas kernels  32.2 us (11%)
  between operations  15.5 us (5%)
  local copies, waits for them, and re-layouts  10.4 us (3%)
    all_to_all x7, starting transfers between devices, exchange(): return lax.all_to_all(x, axes, 0, 0, tiled=True)  53.3 us
    all_gather x1, waiting for transfers between devices, shards(): memory_value_weight = lax.all_gather(cross_value, 'x', axis=0)  38.2 us
    all_to_all x1, blocking collectives, exchange(): return lax.all_to_all(x, axes, 0, 0, tiled=True)  36.3 us
    pallas_call x8, Pallas kernels, call(): pl.pallas_call(kernel, out_shape=out_shape, in_specs=specs, out_specs=jax...  32.2 us
    all_gather x1, waiting for transfers between devices, shards(): encoder_full = lax.all_gather(encoder_rows, 'x', axis=0, tiled=True)  29.6 us
    all_to_all x7, waiting for transfers between devices, exchange(): return lax.all_to_all(x, axes, 0, 0, tiled=True)  27.4 us
    all_gather x1, waiting for transfers between devices, shards(): out_weight = lax.all_gather(output_weight, 'x', axis=0, tiled=True)  22.8 us
    all_gather x1, waiting for transfers between devices, shards(): target_queries = lax.all_gather(target_queries, QUERY_GROUP, axis=0)  21.1 us
  transfers between devices with their start and end apart: 13, of which 8 were waited for; matrix products, arithmetic and copies ran while one was open for 1% of the time, Pallas kernels for 6%

profile of v1, /device:TPU:1, one launch (start us, length us, event | category | flops | bytes accessed | tf_op | source)
XLA Modules:
  0.0 302.5 jit_solution(14479653223788307118)
XLA Ops:
  7.2 0.0 all-gather.15.cloned.1.call-start
  7.2 0.7 all-gather.15.cloned.1.call-update
  7.9 0.0 all-gather.11.cloned.1.call-start
  8.0 0.7 all-gather.11.cloned.1.call-update
  8.7 0.0 all-gather.19.cloned.1.call-start
  8.7 0.7 all-gather.19.cloned.1.call-update
  9.4 1.0 broadcast_in_dim.2
  10.5 36.3 %all_to_all.40.x_ref = bf16[16,256,128]{2,1,0:T(8,128)(2,1)S(1)} all-to-all(bf16[16,256,128]{2,1,0:T(8,128)(2,1)S(1)} %broadcast_in_dim.2), channel_id=1, replica_groups=mesh['zl'=2,'yh'=4,'yl'=2,'c'=2,'zh'=4,'x'=4] {'zh','x'}, dimensions={0} | all-to-all | bytes 2097152 | tf_op jit(solution)/shard_map/all_to_all | solution.py:221
  46.8 2.8 shard_map.149
  49.6 6.6 %all-to-all-start.2 = ((bf16[4,2,256,128]{3,2,1,0:T(8,128)(2,1)}), bf16[4,2,256,128]{3,2,1,0:T(8,128)(2,1)S(1)}, u32[]{:S(2)}, u32[]{:S(2)}) async-start(bf16[4,2,256,128]{3,2,1,0:T(8,128)(2,1)} %get-tuple-element.5), calls=%async_computation.2 | async-start | bytes 1048576 | tf_op jit(solution)/shard_map/all_to_all | solution.py:221
  56.2 0.6 all-gather.21.cloned.1.call-update
  56.8 9.4 %all-to-all-done.2 = bf16[4,2,256,128]{3,2,1,0:T(8,128)(2,1)S(1)} async-done(((bf16[4,2,256,128]{3,2,1,0:T(8,128)(2,1)}), bf16[4,2,256,128]{3,2,1,0:T(8,128)(2,1)S(1)}, u32[]{:S(2)}, u32[]{:S(2)}) %all-to-all-start.2) | async-done | bytes 524320 | tf_op jit(solution)/shard_map/all_to_all | solution.py:221
  66.2 19.5 %all-to-all-start.1 = ((bf16[8,256,128]{2,1,0:T(8,128)(2,1)}), bf16[8,256,128]{2,1,0:T(8,128)(2,1)S(1)}, u32[]{:S(2)}, u32[]{:S(2)}) async-start(bf16[8,256,128]{2,1,0:T(8,128)(2,1)} %get-tuple-element.4), calls=%async_computation.1 | async-start | bytes 1048576 | tf_op jit(solution)/shard_map/all_to_all | solution.py:221
  86.4 0.1 pad_add_fusion.info_ref
  86.5 9.3 %all-to-all-done.1.q_ref = bf16[8,256,128]{2,1,0:T(8,128)(2,1)S(1)} async-done(((bf16[8,256,128]{2,1,0:T(8,128)(2,1)}), bf16[8,256,128]{2,1,0:T(8,128)(2,1)S(1)}, u32[]{:S(2)}, u32[]{:S(2)}) %all-to-all-start.1) | async-done | bytes 524320 | tf_op jit(solution)/shard_map/all_to_all | solution.py:221
  95.8 8.7 %shard_map.150 = bf16[8,4,80,128]{3,2,1,0:T(8,128)(2,1)} custom-call(s32[3]{0:T(128)S(1)} %pad_add_fusion.info_ref, bf16[8,256,128]{2,1,0:T(8,128)(2,1)S(1)} %all-to-all-done.1.q_ref, bf16[4,1,2,256,128]{4,3,2,1,0:T(8,128)(2,1)S(1)} %bitcast.22), custom_call_target="tpu_custom_call" | custom-call | flops 2147483648 | bytes 1703948 | tf_op jit(solution)/shard_map/pallas_call | solution.py:31
  104.6 6.5 %all-to-all-start.3 = ((bf16[32,80,128]{2,1,0:T(8,128)(2,1)}), bf16[32,80,128]{2,1,0:T(8,128)(2,1)S(1)}, u32[]{:S(2)}, u32[]{:S(2)}) async-start(bf16[32,80,128]{2,1,0:T(8,128)(2,1)} %bitcast.3), calls=%async_computation.3 | async-start | bytes 1310720 | tf_op jit(solution)/shard_map/all_to_all | solution.py:221
  111.0 0.0 all-gather.17.cloned.1.call-start
  111.1 0.0 all-gather.15.cloned.1.call-done
  111.1 1.7 copy-done.4
  112.9 3.6 %shard_map.153 = bf16[512,128]{1,0:T(8,128)(2,1)} custom-call(bf16[16,512,128]{2,1,0:T(8,128)(2,1)S(1)} %bitcast.21, f32[1,2048]{1,0:T(1,128)S(1)} %bitcast.25, bf16[2048,128]{1,0:T(8,128)(2,1)S(1)} %copy-done.8), custom_call_target="tpu_custom_call" | custom-call | flops 268435456 | bytes 2760704 | tf_op jit(solution)/shard_map/pallas_call | solution.py:31
  116.4 0.0 all-gather.17.cloned.1.call-update
  116.5 22.8 %all-gather.11.cloned.1.call-done.w_ref = bf16[512,2048]{1,0:T(8,128)(2,1)} async-done(((bf16[128,2048]{1,0:T(8,128)(2,1)}), bf16[512,2048]{1,0:T(8,128)(2,1)}) %all-gather.11.cloned.1.call-update) | async-done | bytes 2097168 | tf_op jit(solution)/shard_map/all_gather | solution.py:265
  139.3 0.0 all-to-all-done.3
  139.3 1.6 copy-done.3
  140.9 1.5 shard_map.151
  142.4 4.0 %all-to-all-start.4 = ((bf16[4,16,2048]{2,1,0:T(8,128)(2,1)}), bf16[4,16,2048]{2,1,0:T(8,128)(2,1)S(1)}, u32[]{:S(2)}, u32[]{:S(2)}) async-start(bf16[4,16,2048]{2,1,0:T(8,128)(2,1)} %shard_map.151), calls=%async_computation.4 | async-start | bytes 524288 | tf_op jit(solution)/shard_map/all_to_all | solution.py:221
  146.4 8.6 %all-to-all-done.4.r_ref = bf16[4,16,2048]{2,1,0:T(8,128)(2,1)S(1)} async-done(((bf16[4,16,2048]{2,1,0:T(8,128)(2,1)}), bf16[4,16,2048]{2,1,0:T(8,128)(2,1)S(1)}, u32[]{:S(2)}, u32[]{:S(2)}) %all-to-all-start.4) | async-done | bytes 262176 | tf_op jit(solution)/shard_map/all_to_all | solution.py:221
  155.0 0.8 shard_map.152
  155.7 4.3 %all-to-all-start.5 = ((bf16[4,16,2048]{2,1,0:T(8,128)(2,1)}), bf16[4,16,2048]{2,1,0:T(8,128)(2,1)S(1)}, u32[]{:S(2)}, u32[]{:S(2)}) async-start(bf16[4,16,2048]{2,1,0:T(8,128)(2,1)} %shard_map.152), calls=%async_computation.5 | async-start | bytes 524288 | tf_op jit(solution)/shard_map/all_to_all | solution.py:221
  160.0 12.1 %all-gather.19.cloned.1.call-done = bf16[8192,128]{1,0:T(8,128)(2,1)} async-done(((bf16[2048,128]{1,0:T(8,128)(2,1)}), bf16[8192,128]{1,0:T(8,128)(2,1)}) %all-gather.19.cloned.1.call-update) | async-done | bytes 2097168 | tf_op jit(solution)/shard_map/all_gather | solution.py:266
  172.2 38.2 %all-gather.21.cloned.1.call-done = bf16[8192,128]{1,0:T(8,128)(2,1)} async-done(((bf16[2048,128]{1,0:T(8,128)(2,1)}), bf16[8192,128]{1,0:T(8,128)(2,1)}) %all-gather.21.cloned.1.call-update) | async-done | bytes 2097168 | tf_op jit(solution)/shard_map/all_gather | solution.py:267
  210.4 0.0 all-to-all-done.5
  210.4 1.7 copy-done.1
  212.1 1.6 copy-done.2
  213.7 1.9 shard_map.154
  215.6 7.7 %all-to-all-start.6 = ((bf16[16,2,64,128]{3,2,1,0:T(8,128)(2,1)}), bf16[16,2,64,128]{3,2,1,0:T(8,128)(2,1)S(1)}, u32[]{:S(2)}, u32[]{:S(2)}) async-start(bf16[16,2,64,128]{3,2,1,0:T(8,128)(2,1)} %bitcast.13), calls=%async_computation.6 | async-start | bytes 1048576 | tf_op jit(solution)/shard_map/all_to_all | solution.py:221
  223.3 21.1 %all-gather.17.cloned.1.call-done = bf16[4096,128]{1,0:T(8,128)(2,1)} async-done(((bf16[512,128]{1,0:T(8,128)(2,1)}), bf16[4096,128]{1,0:T(8,128)(2,1)}) %all-gather.17.cloned.1.call-update) | async-done | bytes 1048592 | tf_op jit(solution)/shard_map/all_gather | solution.py:329
  244.5 0.0 all-to-all-done.6
  244.5 1.2 copy-done.12
  245.7 11.1 %shard_map.155 = bf16[8,1,528,128]{3,2,1,0:T(8,128)(2,1)} custom-call(s32[3]{0:T(128)S(1)} %pad_add_fusion.info_ref, bf16[8,512,128]{2,1,0:T(8,128)(2,1)S(1)} %bitcast.27, bf16[4,4,2,64,128]{4,3,2,1,0:T(8,128)(2,1)S(1)} %bitcast.23), custom_call_target="tpu_custom_call" | custom-call | flops 4294967296 | bytes 2654220 | tf_op jit(solution)/shard_map/pallas_call | solution.py:31
  256.8 4.6 %all-to-all-start.7 = ((bf16[8,528,128]{2,1,0:T(8,128)(2,1)}), bf16[8,528,128]{2,1,0:T(8,128)(2,1)S(1)}, u32[]{:S(2)}, u32[]{:S(2)}) async-start(bf16[8,528,128]{2,1,0:T(8,128)(2,1)} %bitcast.15), calls=%async_computation.7 | async-start | bytes 2162688 | tf_op jit(solution)/shard_map/all_to_all | solution.py:221
  261.4 0.6 all-gather.13.cloned.1.call-update
  262.6 0.1 pad_add_fusion.1.info_ref
  262.7 29.6 %all-gather.13.cloned.1.call-done = bf16[256,2048]{1,0:T(8,128)(2,1)} async-done(((bf16[64,2048]{1,0:T(8,128)(2,1)}), bf16[256,2048]{1,0:T(8,128)(2,1)}) %all-gather.13.cloned.1.call-update) | async-done | bytes 1048592 | tf_op jit(solution)/shard_map/all_gather | solution.py:315
  292.3 1.5 constant_dynamic-slice_fusion
  293.8 0.0 all-to-all-done.7.r_ref
  293.8 1.9 shard_map.156
  (24 shorter events, 0.1 us)
Async XLA Ops:
  7.2 103.9 %all-gather.15.cloned.1.call-start = ((), (), s32[]{:S(2)}) async-start(), calls=%async_computation.10 | async-start | bytes 2228224 | tf_op jit(solution)/shard_map/all_gather | solution.py:268
  7.9 38.9 %copy-start.5 = (bf16[2048,128]{1,0:T(8,128)(2,1)S(1)}, bf16[2048,128]{1,0:T(8,128)(2,1)}, u32[]{:S(2)}) copy-start(bf16[2048,128]{1,0:T(8,128)(2,1)} %wq_ref.2) | copy-start | bytes 1572868
  7.9 38.9 %copy-start.6 = (bf16[2048,128]{1,0:T(8,128)(2,1)S(1)}, bf16[2048,128]{1,0:T(8,128)(2,1)}, u32[]{:S(2)}) copy-start(bf16[2048,128]{1,0:T(8,128)(2,1)} %wk_ref.1) | copy-start | bytes 1572868
  7.9 38.9 %copy-start.7 = (bf16[2048,128]{1,0:T(8,128)(2,1)S(1)}, bf16[2048,128]{1,0:T(8,128)(2,1)}, u32[]{:S(2)}) copy-start(bf16[2048,128]{1,0:T(8,128)(2,1)} %wv_ref.1) | copy-start | bytes 1572868
  7.9 38.9 %copy-start.9 = (f32[2048]{0:T(1024)S(1)}, f32[2048]{0:T(1024)}, u32[]{:S(2)}) copy-start(f32[2048]{0:T(1024)} %param.18) | copy-start | bytes 24580
  7.9 131.3 %all-gather.11.cloned.1.call-start = ((), (), s32[]{:S(2)}) async-start(), calls=%async_computation.8 | async-start | bytes 2621440 | tf_op jit(solution)/shard_map/all_gather | solution.py:265
  8.7 163.5 %all-gather.19.cloned.1.call-start = ((), (), s32[]{:S(2)}) async-start(), calls=%async_computation.12 | async-start | bytes 2621440 | tf_op jit(solution)/shard_map/all_gather | solution.py:266
  49.6 16.6 %all-to-all-start.2 = ((bf16[4,2,256,128]{3,2,1,0:T(8,128)(2,1)}), bf16[4,2,256,128]{3,2,1,0:T(8,128)(2,1)S(1)}, u32[]{:S(2)}, u32[]{:S(2)}) async-start(bf16[4,2,256,128]{3,2,1,0:T(8,128)(2,1)} %get-tuple-element.5), calls=%async_computation.2 | async-start | bytes 1048576 | tf_op jit(solution)/shard_map/all_to_all | solution.py:221
  56.2 154.2 %all-gather.21.cloned.1.call-start = ((), (), s32[]{:S(2)}) async-start(), calls=%async_computation.13 | async-start | bytes 2621440 | tf_op jit(solution)/shard_map/all_gather | solution.py:267
  66.2 29.6 %all-to-all-start.1 = ((bf16[8,256,128]{2,1,0:T(8,128)(2,1)}), bf16[8,256,128]{2,1,0:T(8,128)(2,1)S(1)}, u32[]{:S(2)}, u32[]{:S(2)}) async-start(bf16[8,256,128]{2,1,0:T(8,128)(2,1)} %get-tuple-element.4), calls=%async_computation.1 | async-start | bytes 1048576 | tf_op jit(solution)/shard_map/all_to_all | solution.py:221
  95.8 15.3 %copy-start.8 = (bf16[2048,128]{1,0:T(8,128)(2,1)S(1)}, bf16[2048,128]{1,0:T(8,128)(2,1)}, u32[]{:S(2)}) copy-start(bf16[2048,128]{1,0:T(8,128)(2,1)} %wq_ref.3) | copy-start | bytes 1572868
  95.8 15.3 %copy-start.10 = (f32[2048]{0:T(1024)S(1)}, f32[2048]{0:T(1024)}, u32[]{:S(2)}) copy-start(f32[2048]{0:T(1024)} %param.27) | copy-start | bytes 24580
  104.6 34.7 %all-to-all-start.3 = ((bf16[32,80,128]{2,1,0:T(8,128)(2,1)}), bf16[32,80,128]{2,1,0:T(8,128)(2,1)S(1)}, u32[]{:S(2)}, u32[]{:S(2)}) async-start(bf16[32,80,128]{2,1,0:T(8,128)(2,1)} %bitcast.3), calls=%async_computation.3 | async-start | bytes 1310720 | tf_op jit(solution)/shard_map/all_to_all | solution.py:221
  111.0 133.4 %all-gather.17.cloned.1.call-start = ((), (), s32[]{:S(2)}) async-start(), calls=%async_computation.11 | async-start | bytes 1179648 | tf_op jit(solution)/shard_map/all_gather | solution.py:329
  111.1 1.7 copy-start.4
  139.3 1.6 copy-start.3
  140.9 69.5 %copy-start.11 = (f32[2048]{0:T(1024)S(1)}, f32[2048]{0:T(1024)}, u32[]{:S(2)}) copy-start(f32[2048]{0:T(1024)} %param.23) | copy-start | bytes 24580
  142.4 12.6 %all-to-all-start.4 = ((bf16[4,16,2048]{2,1,0:T(8,128)(2,1)}), bf16[4,16,2048]{2,1,0:T(8,128)(2,1)S(1)}, u32[]{:S(2)}, u32[]{:S(2)}) async-start(bf16[4,16,2048]{2,1,0:T(8,128)(2,1)} %shard_map.151), calls=%async_computation.4 | async-start | bytes 524288 | tf_op jit(solution)/shard_map/all_to_all | solution.py:221
  155.7 54.7 %all-to-all-start.5 = ((bf16[4,16,2048]{2,1,0:T(8,128)(2,1)}), bf16[4,16,2048]{2,1,0:T(8,128)(2,1)S(1)}, u32[]{:S(2)}, u32[]{:S(2)}) async-start(bf16[4,16,2048]{2,1,0:T(8,128)(2,1)} %shard_map.152), calls=%async_computation.5 | async-start | bytes 524288 | tf_op jit(solution)/shard_map/all_to_all | solution.py:221
  210.4 5.2 %copy-start = (bf16[4,16,2048]{2,1,0:T(8,128)(2,1)}, bf16[4,16,2048]{2,1,0:T(8,128)(2,1)S(1)}, u32[]{:S(2)}) copy-start(bf16[4,16,2048]{2,1,0:T(8,128)(2,1)S(1)} %all-to-all-done.5) | copy-start | bytes 786436
  210.4 1.7 copy-start.1
  212.1 1.6 copy-start.2
  215.6 28.9 %all-to-all-start.6 = ((bf16[16,2,64,128]{3,2,1,0:T(8,128)(2,1)}), bf16[16,2,64,128]{3,2,1,0:T(8,128)(2,1)S(1)}, u32[]{:S(2)}, u32[]{:S(2)}) async-start(bf16[16,2,64,128]{3,2,1,0:T(8,128)(2,1)} %bitcast.13), calls=%async_computation.6 | async-start | bytes 1048576 | tf_op jit(solution)/shard_map/all_to_all | solution.py:221
  244.5 1.2 copy-start.12
  256.8 37.0 %all-to-all-start.7 = ((bf16[8,528,128]{2,1,0:T(8,128)(2,1)}), bf16[8,528,128]{2,1,0:T(8,128)(2,1)S(1)}, u32[]{:S(2)}, u32[]{:S(2)}) async-start(bf16[8,528,128]{2,1,0:T(8,128)(2,1)} %bitcast.15), calls=%async_computation.7 | async-start | bytes 2162688 | tf_op jit(solution)/shard_map/all_to_all | solution.py:221
  261.4 30.9 %all-gather.13.cloned.1.call-start = ((), (), s32[]{:S(2)}) async-start(), calls=%async_computation.9 | async-start | bytes 1310720 | tf_op jit(solution)/shard_map/all_gather | solution.py:315
Sparse Core Ops, SparseCore 0:
  11.0 80.5 all-gather.14
  93.7 45.4 all-gather.10
  141.4 30.7 all-gather.18
  174.1 36.2 all-gather.20
  213.0 31.4 all-gather.16
  264.0 28.2 all-gather.12

commit v2 on v1

v2 whole, which is shorter than its diff:
```python
import functools
import math

import jax
import jax.numpy as jnp
from jax import lax
from jax.experimental import pallas as pl
from jax.experimental.pallas import tpu as pltpu
from jax.sharding import Mesh, PartitionSpec as P

HD = 128
D = 2048
EPSILON = 1e-05
MASKED = -1e30
SCORE_SCALE = HD ** (-0.5) * math.log2(math.e)
F32 = jnp.float32
BF16 = jnp.bfloat16

AXES = (("zl", 2), ("yh", 4), ("yl", 2), ("c", 2), ("zh", 4), ("x", 4))
SEQ = ("zl", "yh", "yl", "c")
HEAD = ("zh", "x")
QUERY_GROUP = ("zl", "yl", "c")
VMEM = pl.BlockSpec(memory_space=pltpu.VMEM)
SMEM = pl.BlockSpec(memory_space=pltpu.SMEM)
ANY = pl.BlockSpec(memory_space=pl.ANY)
HBM = pl.BlockSpec(memory_space=pltpu.HBM)
DMA = pltpu.SemaphoreType.DMA


def call(kernel, out_shape, *args, specs, out=None, scratch=(), limit=48, flops=0, transcendentals=0):
    outs = jax.tree.leaves(out_shape)
    size = sum(math.prod(a.shape) * a.dtype.itemsize for a in (*args, *outs))
    return pl.pallas_call(
        kernel,
        out_shape=out_shape,
        in_specs=specs,
        out_specs=jax.tree.map(lambda _: VMEM, out_shape) if out is None else out,
        scratch_shapes=scratch,
        compiler_params=pltpu.CompilerParams(vmem_limit_bytes=int(limit * 1024 * 1024)),
        cost_estimate=pl.CostEstimate(flops=flops, bytes_accessed=size, transcendentals=transcendentals),
    )(*args)


def shape(*dims, dtype=BF16):
    return jax.ShapeDtypeStruct(dims, dtype)


def started(pairs, sems):
    copies = [pltpu.make_async_copy(a, b, sems.at[i]) for i, (a, b) in enumerate(pairs)]
    for copy in copies:
        copy.start()
    return copies


def wait_for(copies):
    for copy in copies:
        copy.wait()


def repeat_kernel(x_ref, out_ref, sems):
    wait_for(started([(x_ref, out_ref.at[i]) for i in range(out_ref.shape[0])], sems))


def repeated(x, times):
    return call(
        repeat_kernel, shape(times, *x.shape), x, specs=[VMEM], out=HBM, scratch=[DMA((times,))], limit=63.9
    )


def normed_rows(pieces, gains):
    total = functools.reduce(jnp.add, pieces)
    mean = jnp.sum(total, axis=-1, keepdims=True) * (1.0 / D)
    centers = [p - mean for p in pieces]
    squares = functools.reduce(jnp.add, [c * c for c in centers])
    spread = jnp.sum(squares, axis=-1, keepdims=True) * (1.0 / D)
    inverse = lax.rsqrt(spread + EPSILON)
    return [(c * inverse * g).astype(BF16) for c, g in zip(centers, gains)]


def norm_gathered(x_ref, gain_ref, norm_ref, step=64):
    rows = x_ref.shape[1]

    def body(i, _):
        r = pl.multiple_of(i * step, step)
        pieces = [x_ref[j, pl.ds(r, step), :].astype(F32) for j in range(16)]
        gains = [gain_ref[:, j * 128 : (j + 1) * 128] for j in range(16)]
        for j, n in enumerate(normed_rows(pieces, gains)):
            norm_ref[pl.ds(r, step), j * 128 : (j + 1) * 128] = n
        return 0

    lax.fori_loop(0, rows // step, body, 0)


def qkv_kernel(x_ref, gain_ref, wq_ref, wk_ref, wv_ref, q_ref, kv_ref, norm_ref, w_ref, q_one_ref, in_sems, out_sems):
    weights = started(
        [(w, w_ref.at[:, i * 128 : (i + 1) * 128]) for i, w in enumerate((wq_ref, wk_ref, wv_ref))], in_sems
    )
    norm_gathered(x_ref, gain_ref, norm_ref)
    wait_for(weights)
    out = jnp.dot(norm_ref[...], w_ref[...], preferred_element_type=F32)
    q_one_ref[...] = (out[:, :128] * SCORE_SCALE).astype(BF16)
    copies = started([(q_one_ref, q_ref.at[a]) for a in range(q_ref.shape[0])], out_sems)
    kv_ref[0] = out[:, 128:256].astype(BF16)
    kv_ref[1] = out[:, 256:].astype(BF16)
    wait_for(copies)


def target_kernel(x_ref, gain_ref, wq_ref, q_ref, norm_ref, x_vmem, w_ref, x_sems, w_sem):
    rows = x_ref.shape[1]
    parts = x_vmem.shape[0]
    step = rows // parts
    weights = started([(wq_ref, w_ref)], w_sem)
    pieces = started(
        [(x_ref.at[:, i * step : (i + 1) * step, :], x_vmem.at[i]) for i in range(parts)], x_sems
    )
    for i, piece in enumerate(pieces):
        piece.wait()
        norm_gathered(x_vmem.at[i], gain_ref, norm_ref.at[i * step : (i + 1) * step, :])
    wait_for(weights)
    out = jnp.dot(norm_ref[...], w_ref[...], preferred_element_type=F32)
    q_ref[...] = (out * SCORE_SCALE).astype(BF16)


def attend_kernel(part, blocks, fetched, info_ref, q_ref, *refs):
    kv_refs, (out_ref, ka_ref, va_ref, *q_scratch) = refs[: len(refs) - 3 - fetched * 2], refs[len(refs) - 3 - fetched * 2 :]
    members, rows, _ = q_ref.shape
    q_vmem, q_copy = q_ref, []
    if fetched:
        q_vmem, q_sem = q_scratch
        q_copy = started([(q_ref, q_vmem)], q_sem)
    limit = info_ref[0]
    n = kv_refs[0].shape[-2]
    lane = lax.broadcasted_iota(jnp.int32, (n, 128), 1)
    row = lax.broadcasted_iota(jnp.int32, (n, 128), 0)
    for b, (ref, at) in enumerate(blocks):
        place = info_ref[1 + b] + row
        bias = jnp.where((lane == 0) & (place >= limit), MASKED, 0.0).astype(BF16)
        here = slice(b * n, (b + 1) * n)
        ka_ref[here, :128] = kv_refs[ref][(*at, 0)]
        ka_ref[here, 128:] = bias
        va_ref[here, :128] = kv_refs[ref][(*at, 1)]
        va_ref[here, 128:] = jnp.ones((n, 128), BF16)
    ones = jnp.where(lax.broadcasted_iota(jnp.int32, (256, 128), 1) == 0, 1.0, 0.0).astype(BF16)
    group = min(part, 128)
    groups = part // group
    eye = lax.broadcasted_iota(jnp.int32, (group, 128), 0) == lax.broadcasted_iota(jnp.int32, (group, 128), 1)
    block = 256
    each = rows // block
    unroll = 8

    wait_for(q_copy)

    def body(i, _):
        for u in range(unroll):
            step = i * unroll + u
            a, r = (step, 0) if each == 1 else (step // each, (u % each) * block)
            q = jnp.concatenate([q_vmem[a, pl.ds(r, block), :], ones], axis=1)
            scores = lax.dot_general(q, ka_ref[...], (((1,), (1,)), ((), ())), preferred_element_type=F32)
            top = jnp.max(scores, axis=1, keepdims=True)
            weights = jnp.exp2(scores - top).astype(BF16)
            summed = jnp.dot(weights, va_ref[...], preferred_element_type=F32)
            denominator = summed[:, 128:]
            context = (summed[:, :128] / denominator).astype(BF16)
            level = top + jnp.log2(denominator)
            for g in range(block // group):
                at = r + g * group
                p, inside = at // part, at % part
                out_ref[a, p, inside : inside + group, :] = context[g * group : (g + 1) * group]
                line = jnp.sum(jnp.where(eye, level[g * group : (g + 1) * group], 0.0), axis=0, keepdims=True)
                stat_ref_store(out_ref, a, p, part, inside // group, groups, line)
        return 0

    lax.fori_loop(0, members * each // unroll, body, 0)


def stat_ref_store(out_ref, a, p, part, g, groups, line):
    high = line.astype(BF16)
    rest = line - high.astype(F32)
    middle = rest.astype(BF16)
    low = (rest - middle.astype(F32)).astype(BF16)
    out_ref[a, p, part + g : part + g + 1, :] = high
    out_ref[a, p, part + groups + g : part + groups + g + 1, :] = middle
    out_ref[a, p, part + 2 * groups + g : part + 2 * groups + g + 1, :] = low


def mixing(levels):
    top = functools.reduce(jnp.maximum, levels)
    raw = [jnp.exp2(v - top) for v in levels]
    total = functools.reduce(jnp.add, raw)
    return [v / total for v in raw]


def combined(read_rows, read_stats, members, part):
    group = min(part, 128)
    groups = part // group
    eye = lax.broadcasted_iota(jnp.int32, (group, 128), 0) == lax.broadcasted_iota(jnp.int32, (group, 128), 1)
    levels = []
    for a in range(members):
        stats = read_stats(a).astype(F32)
        levels.append(stats[:groups] + stats[groups : 2 * groups] + stats[2 * groups : 3 * groups])
    shares = mixing(levels)
    out = []
    for g in range(groups):
        total = None
        for a in range(members):
            column = jnp.sum(jnp.where(eye, shares[a][g : g + 1], 0.0), axis=1, keepdims=True)
            term = read_rows(a)[g * group : (g + 1) * group].astype(F32) * column
            total = term if total is None else total + term
        out.append(total)
    return out


def project_out_kernel(info_ref, r_ref, own_ref, mine_ref, theirs_ref, out_ref, ctx_ref, w_ref, sems):
    core = info_ref[0]
    half = D // 2
    copies = started(
        [(own_ref, w_ref.at[:128])]
        + [
            (ref.at[k], w_ref.at[(k + 1) * 128 : (k + 2) * 128, pl.ds(pl.multiple_of(first * half, half), half)])
            for ref, first in ((mine_ref, core), (theirs_ref, 1 - core))
            for k in range(3)
        ],
        sems,
    )
    members, _, full, _ = r_ref.shape
    part = full - 16
    for k in range(4):
        h = info_ref[1 + k]
        pieces = combined(
            lambda a: r_ref[a, h, :part, :], lambda a: r_ref[a, h, part:, :], members, part
        )
        ctx_ref[:, k * 128 : (k + 1) * 128] = pieces[0].astype(BF16)
    wait_for(copies)
    out = jnp.dot(ctx_ref[...], w_ref[...], preferred_element_type=F32).astype(BF16)
    for z in range(4):
        out_ref[z] = out[z * 16 : (z + 1) * 16]


def residual_kernel(r_ref, s_ref, out_ref):
    for j in range(16):
        cols = slice(j * 128, (j + 1) * 128)
        total = s_ref[j].astype(F32)
        for z in range(4):
            total = total + r_ref[z, :, cols].astype(F32)
        total = total.astype(BF16)
        for z in range(4):
            out_ref[z, :, cols] = total


def memory_kernel(info_ref, e_ref, gain_ref, mine_ref, theirs_ref, kv_ref, norm_ref, e_vmem, w_ref, sems, e_sem):
    core = info_ref[0]
    half = D // 2
    rows = started([(e_ref, e_vmem)], e_sem)
    copies = started(
        [
            (ref.at[h, t], w_ref.at[h, pl.ds(pl.multiple_of(first * half, half), half), t * 128 : (t + 1) * 128])
            for h in range(4)
            for ref, first in ((mine_ref, core), (theirs_ref, 1 - core))
            for t in range(2)
        ],
        sems,
    )
    wait_for(rows)
    pieces = [e_vmem[:, j * 128 : (j + 1) * 128].astype(F32) for j in range(16)]
    gains = [gain_ref[:, j * 128 : (j + 1) * 128] for j in range(16)]
    for j, n in enumerate(normed_rows(pieces, gains)):
        norm_ref[:, j * 128 : (j + 1) * 128] = n
    for h in range(4):
        wait_for(copies[h * 4 : (h + 1) * 4])
        out = jnp.dot(norm_ref[...], w_ref[h], preferred_element_type=F32).astype(BF16)
        for b in range(4):
            kv_ref[b, h, 0] = out[:, :128]
            kv_ref[b, h, 1] = out[:, 128:]


def finish_kernel(info_ref, r_ref, out_ref):
    members, full, _ = r_ref.shape
    part = full - 16
    pieces = combined(lambda a: r_ref[a, :part, :], lambda a: r_ref[a, part:, :], members, part)
    first, limit = info_ref[0], info_ref[1]
    for g, piece in enumerate(pieces):
        n = piece.shape[0]
        place = first + g * n + lax.broadcasted_iota(jnp.int32, (n, 128), 0)
        out_ref[g * n : (g + 1) * n, :] = jnp.where(place < limit, piece, 0.0).astype(BF16)


def exchange(x, axes):
    return lax.all_to_all(x, axes, 0, 0, tiled=True)


def attend(q, kvs, blocks, info, part, fetched):
    members, rows, _ = q.shape
    keys = len(blocks) * kvs[0].shape[-2]
    return call(
        functools.partial(attend_kernel, part, blocks, fetched),
        shape(members, rows // part, part + 16, 128),
        info,
        q,
        *kvs,
        specs=[SMEM, ANY if fetched else VMEM] + [VMEM] * len(kvs),
        scratch=[pltpu.VMEM((keys, 256), BF16), pltpu.VMEM((keys, 256), BF16)]
        + ([pltpu.VMEM(q.shape, BF16), DMA((1,))] if fetched else []),
        limit=62 if fetched else 48,
        flops=4 * members * rows * keys * 256,
        transcendentals=members * rows * keys,
    )


def swapped(x, axis, size, by):
    return lax.ppermute(x, axis, [(i, i ^ by) for i in range(size)])


def together(*arrays):
    return lax.optimization_barrier(arrays)


def shards(
    source_hidden,
    target_hidden,
    source_length,
    target_length,
    encoder_gain,
    query_weight,
    key_weight,
    value_weight,
    output_weight,
    final_gain,
    cross_query,
    cross_key,
    cross_value,
    cross_gain,
):
    rows = source_hidden.shape[0]
    target_rows = target_hidden.shape[0]
    at = {name: lax.axis_index(name) for name, _ in AXES}
    seq_at = ((at["zl"] * 4 + at["yh"]) * 2 + at["yl"]) * 2 + at["c"]
    quarter = rows // 4
    core_info = jnp.stack([at["c"], at["x"], at["x"] ^ 1, at["x"] ^ 3, at["x"] ^ 2])

    def first_of(yh):
        return (((at["zl"] * 4 + yh) * 2 + at["yl"]) * 2 + at["c"]) * rows

    key_info = jnp.stack([source_length[0]] + [first_of(at["yh"] ^ k) for k in range(4)])
    memory_info = jnp.stack(
        [source_length[0]] + [first_of(k // 4) + (k % 4) * quarter for k in range(16)]
    )
    target_info = jnp.stack([seq_at * target_rows, target_length[0]])
    gains = [g.reshape(1, D) for g in (encoder_gain, final_gain, cross_gain)]

    half = at["c"] * (D // 2)
    out_half = lax.dynamic_slice_in_dim(output_weight, half, D // 2, 1)
    out_halves = [swapped(out_half, "x", 4, k) for k in (1, 3)]
    target_full = lax.all_gather(target_hidden, HEAD, axis=0)
    source_full = exchange(repeated(source_hidden, 16), HEAD)
    source_full, *out_halves = together(source_full, *out_halves)
    out_halves.append(swapped(out_halves[0], "x", 4, 3))
    half_weights = jnp.stack([lax.dynamic_slice_in_dim(w, half, D // 2, 0) for w in (cross_key, cross_value)])
    source_full, half_weights = together(source_full, half_weights)
    mine = lax.all_gather(half_weights, "x", axis=0)

    queries, keys_values = call(
        qkv_kernel,
        (shape(8, rows, 128), shape(2, rows, 128)),
        source_full,
        gains[0],
        query_weight,
        key_weight,
        value_weight,
        specs=[VMEM, VMEM, ANY, ANY, ANY],
        out=(HBM, VMEM),
        scratch=[
            pltpu.VMEM((rows, D), BF16),
            pltpu.VMEM((D, 384), BF16),
            pltpu.VMEM((rows, 128), BF16),
            DMA((3,)),
            DMA((8,)),
        ],
        flops=2 * rows * D * 384,
    )
    key_sets = [keys_values] + [swapped(keys_values, "yh", 4, k) for k in (1, 2, 3)]
    queries = exchange(queries, QUERY_GROUP)
    queries, out_halves[2] = together(queries, out_halves[2])
    out_mine = jnp.stack(out_halves)
    out_theirs = swapped(out_mine, "c", 2, 1)
    partial = attend(queries, key_sets, [(k, ()) for k in range(4)], key_info, quarter, False)
    partial = exchange(partial.reshape(32, rows // 4 + 16, 128), QUERY_GROUP + ("x",))
    target_queries = call(
        target_kernel,
        shape(target_rows, 128),
        target_full,
        gains[2],
        cross_query,
        specs=[ANY, VMEM, ANY],
        scratch=[
            pltpu.VMEM((target_rows, D), BF16),
            pltpu.VMEM((4, 16, target_rows // 4, 128), BF16),
            pltpu.VMEM((D, 128), BF16),
            DMA((4,)),
            DMA((1,)),
        ],
        flops=2 * target_rows * D * 128,
    )
    partial, target_queries = together(partial, target_queries)
    shares = call(
        project_out_kernel,
        shape(4, quarter // 4, D),
        core_info,
        partial.reshape(8, 4, quarter + 16, 128),
        output_weight,
        out_mine,
        out_theirs,
        specs=[SMEM, VMEM] + [ANY] * 3,
        scratch=[pltpu.VMEM((quarter, 512), BF16), pltpu.VMEM((512, D), BF16), DMA((7,))],
        limit=62.5,
        flops=2 * quarter * 512 * D,
    )
    shares = exchange(shares, "zh")
    shares, mine = together(shares, mine)
    theirs = swapped(mine, "c", 2, 1)
    first = at["x"] * quarter + at["zh"] * (quarter // 4)
    own_source = lax.dynamic_slice_in_dim(source_full, first, quarter // 4, 1)
    encoder_rows = call(
        residual_kernel, shape(4, quarter // 4, D), shares, own_source, specs=[VMEM] * 2
    )
    encoder_rows = exchange(encoder_rows, "zh").reshape(quarter, D)
    memory = call(
        memory_kernel,
        shape(4, 4, 2, quarter, 128),
        core_info,
        encoder_rows,
        gains[1],
        mine,
        theirs,
        specs=[SMEM, ANY, VMEM, ANY, ANY],
        scratch=[
            pltpu.VMEM((quarter, D), BF16),
            pltpu.VMEM((quarter, D), BF16),
            pltpu.VMEM((4, D, 256), BF16),
            DMA((16,)),
            DMA((1,)),
        ],
        limit=63,
        flops=2 * quarter * D * 1024,
    )
    encoder_full = lax.all_gather(encoder_rows, "x", axis=0, tiled=True)

    target_queries = lax.all_gather(target_queries, QUERY_GROUP, axis=0)
    memory = exchange(memory.reshape(16, 2, quarter, 128), ("yh", "x")).reshape(4, 4, 2, quarter, 128)
    crossed = attend(
        target_queries, [memory], [(0, (k // 4, k % 4)) for k in range(16)], memory_info, target_rows, True
    )
    crossed, encoder_full = together(crossed, encoder_full)
    crossed = exchange(crossed.reshape(8, target_rows + 16, 128), QUERY_GROUP)
    head_at = at["zh"] * 4 + at["x"]
    encoder_out = lax.dynamic_slice_in_dim(encoder_full, head_at * 128, 128, 1)
    cross_context = call(
        finish_kernel, shape(target_rows, 128), target_info, crossed, specs=[SMEM, VMEM]
    )
    return (encoder_out, cross_context)


def solution(mesh):
    fine = Mesh(mesh.devices.reshape([size for _, size in AXES]), [name for name, _ in AXES])
    columns = P(None, HEAD)
    in_specs = (
        P(SEQ, HEAD),
        P(SEQ, HEAD),
        P(),
        P(),
        P(),
        columns,
        columns,
        columns,
        P(HEAD, None),
        P(),
        columns,
        columns,
        columns,
        P(),
    )
    out_specs = (P(SEQ, HEAD), P(SEQ, HEAD))
    return jax.shard_map(shards, mesh=fine, in_specs=in_specs, out_specs=out_specs, check_vma=False)
```

time: 303 us -> 218 us (0.72)
  waiting for transfers between devices: 154 us -> 53.3 us
  starting transfers between devices: 53.4 us -> 75.8 us
  blocking collectives: 36.3 us -> 26.5 us
    all_gather x3 -> x1, waiting for transfers between devices: 73.2 us -> 0.01 us  [shards(): mine = lax.all_gather(half_weights, 'x', axis=0)]
    ppermute x0 -> x8, starting transfers between devices: none -> 27.4 us  [swapped(): return lax.ppermute(x, axis, [(i, i ^ by) for i in range(size)])]
    all_gather x1, waiting for transfers between devices: 29.6 us -> 5.85 us  [shards(): encoder_full = lax.all_gather(encoder_rows, 'x', axis=0, tiled=True)]
    ppermute x0 -> x8, waiting for transfers between devices: none -> 22.7 us  [swapped(): return lax.ppermute(x, axis, [(i, i ^ by) for i in range(size)])]
    all_gather x1, waiting for transfers between devices: 21.1 us -> 0.01 us  [shards(): target_queries = lax.all_gather(target_queries, QUERY_GROUP, axis=0)]
    all_to_all x1 -> x2, blocking collectives: 36.3 us -> 26.5 us  [exchange(): return lax.all_to_all(x, axes, 0, 0, tiled=True)]
    all_to_all x7 -> x5, starting transfers between devices: 53.3 us -> 48.3 us  [exchange(): return lax.all_to_all(x, axes, 0, 0, tiled=True)]
    unnamed x26 -> x20, local copies, waits for them, and re-layouts: 7.86 us -> 3.29 us
  transfers between devices with their start and end apart: 13 -> 17, of which waited for: 8 -> 9; matrix products, arithmetic and copies ran while one was open for 1% -> 3% of each run, Pallas kernels for 6% -> 15%
where the time goes in v2:
time: 218 us; the launch traced here: 215 us
  starting transfers between devices  75.8 us (35%)
  waiting for transfers between devices  53.3 us (24%)
  Pallas kernels  33.7 us (15%)
  blocking collectives  26.5 us (12%)
  between operations  15.4 us (7%)
  local copies, waits for them, and re-layouts  8.29 us (4%)
    all_to_all x5, starting transfers between devices, exchange(): return lax.all_to_all(x, axes, 0, 0, tiled=True)  48.3 us
    pallas_call x9, Pallas kernels, call(): pl.pallas_call(kernel, out_shape=out_shape, in_specs=specs, out_specs=jax...  33.7 us
    ppermute x8, starting transfers between devices, swapped(): return lax.ppermute(x, axis, [(i, i ^ by) for i in range(size)])  27.4 us
    all_to_all x2, blocking collectives, exchange(): return lax.all_to_all(x, axes, 0, 0, tiled=True)  26.5 us
    all_to_all x5, waiting for transfers between devices, exchange(): return lax.all_to_all(x, axes, 0, 0, tiled=True)  24 us
    ppermute x8, waiting for transfers between devices, swapped(): return lax.ppermute(x, axis, [(i, i ^ by) for i in range(size)])  22.7 us
    all_gather x1, waiting for transfers between devices, shards(): encoder_full = lax.all_gather(encoder_rows, 'x', axis=0, tiled=True)  5.85 us
  transfers between devices with their start and end apart: 17, of which 9 were waited for; matrix products, arithmetic and copies ran while one was open for 3% of the time, Pallas kernels for 15%

profile of v2, /device:TPU:1, one launch (start us, length us, event | category | flops | bytes accessed | tf_op | source)
XLA Modules:
  0.0 215.1 jit_solution(13094325420532809980)
XLA Ops:
  7.2 0.7 all-gather.10.cloned.1.call-update
  7.9 2.0 shard_map.149
  9.9 13.4 %all-to-all-start = ((bf16[16,256,128]{2,1,0:T(8,128)(2,1)}), bf16[16,256,128]{2,1,0:T(8,128)(2,1)S(1)}, u32[]{:S(2)}, u32[]{:S(2)}) async-start(bf16[16,256,128]{2,1,0:T(8,128)(2,1)} %shard_map.149), calls=%async_computation | async-start | bytes 2097152 | tf_op jit(solution)/shard_map/all_to_all | solution.py:288
  23.4 0.0 all-gather.14.cloned.1.call-start
  23.4 1.1 constant_dynamic-slice_fusion.2
  24.5 3.3 %collective-permute-start = (bf16[128,1024]{1,0:T(8,128)(2,1)S(1)}, bf16[128,1024]{1,0:T(8,128)(2,1)}, u32[]{:S(2)}, u32[]{:S(2)}) collective-permute-start(bf16[128,1024]{1,0:T(8,128)(2,1)S(1)} %constant_dynamic-slice_fusion.2), channel_id=1, source_target_pairs={{0,1},{1,0},{2,3},{3,2},{4,5},{5,4},{6,7},{7,6},{8,9},{9,8},{10,11... | collective-permute-start | bytes 786440 | tf_op jit(solution)/shard_map/ppermute | solution.py:310
  27.8 3.7 %collective-permute-start.1 = (bf16[128,1024]{1,0:T(8,128)(2,1)S(1)}, bf16[128,1024]{1,0:T(8,128)(2,1)}, u32[]{:S(2)}, u32[]{:S(2)}) collective-permute-start(bf16[128,1024]{1,0:T(8,128)(2,1)S(1)} %constant_dynamic-slice_fusion.2), channel_id=1, source_target_pairs={{0,3},{1,2},{2,1},{3,0},{4,7},{5,6},{6,5},{7,4},{8,11},{9,10},{10,... | collective-permute-start | bytes 786440 | tf_op jit(solution)/shard_map/ppermute | solution.py:310
  31.5 1.1 dynamic-slice_bitcast_fusion
  32.6 0.8 pad_maximum_fusion.1
  33.4 7.7 %collective-permute-done = bf16[128,1024]{1,0:T(8,128)(2,1)} collective-permute-done((bf16[128,1024]{1,0:T(8,128)(2,1)S(1)}, bf16[128,1024]{1,0:T(8,128)(2,1)}, u32[]{:S(2)}, u32[]{:S(2)}) %collective-permute-start) | collective-permute-done | bytes 262176 | tf_op jit(solution)/shard_map/ppermute | solution.py:310
  41.1 5.5 %collective-permute-done.1 = bf16[128,1024]{1,0:T(8,128)(2,1)} collective-permute-done((bf16[128,1024]{1,0:T(8,128)(2,1)S(1)}, bf16[128,1024]{1,0:T(8,128)(2,1)}, u32[]{:S(2)}, u32[]{:S(2)}) %collective-permute-start.1) | collective-permute-done | bytes 262176 | tf_op jit(solution)/shard_map/ppermute | solution.py:310
  46.7 2.9 %shard_map.150 = (bf16[8,256,128]{2,1,0:T(8,128)(2,1)S(1)}, bf16[2,256,128]{2,1,0:T(8,128)(2,1)S(1)}) custom-call(bf16[16,256,128]{2,1,0:T(8,128)(2,1)S(1)} %all-to-all-done.x_ref, f32[1,2048]{1,0:T(1,128)S(1)} %bitcast.46, bf16[2048,128]{1,0:T(8,128)(2,1)S(1)} %copy-done.1, bf16[2048,128]{1,0:T(8,128)(2,1)S(1)} %copy-done.2, bf16[2048,128]{1,0:T(8,128)(2,1)S(1)} %copy-done.3), custom_call_target="tpu_custom_call" | custom-call | flops 402653184 | bytes 3284992 | tf_op jit(solution)/shard_map/pallas_call | solution.py:33
  49.6 0.8 copy-done.4
  50.4 15.4 %all-to-all-start.1 = ((bf16[8,256,128]{2,1,0:T(8,128)(2,1)}), bf16[8,256,128]{2,1,0:T(8,128)(2,1)S(1)}, u32[]{:S(2)}, u32[]{:S(2)}) async-start(bf16[8,256,128]{2,1,0:T(8,128)(2,1)} %copy-done.4), calls=%async_computation.1 | async-start | bytes 1048576 | tf_op jit(solution)/shard_map/all_to_all | solution.py:288
  65.8 1.9 collective-permute-start.2
  67.7 4.2 %collective-permute-start.3 = (bf16[2,256,128]{2,1,0:T(8,128)(2,1)S(1)}, bf16[2,256,128]{2,1,0:T(8,128)(2,1)S(1)}, u32[]{:S(2)}, u32[]{:S(2)}) collective-permute-start(bf16[2,256,128]{2,1,0:T(8,128)(2,1)S(1)} %get-tuple-element.22.refs_0_), channel_id=1, source_target_pairs={{0,64},{64,0},{128,192},{192,128},{1,65},{65,1},{129,193},{193,129... | collective-permute-start | bytes 393224 | tf_op jit(solution)/shard_map/ppermute | solution.py:310
  71.9 4.7 %collective-permute-start.4 = (bf16[2,256,128]{2,1,0:T(8,128)(2,1)S(1)}, bf16[2,256,128]{2,1,0:T(8,128)(2,1)S(1)}, u32[]{:S(2)}, u32[]{:S(2)}) collective-permute-start(bf16[2,256,128]{2,1,0:T(8,128)(2,1)S(1)} %get-tuple-element.22.refs_0_), channel_id=1, source_target_pairs={{0,128},{64,192},{128,0},{192,64},{1,129},{65,193},{129,1},{193,65... | collective-permute-start | bytes 393224 | tf_op jit(solution)/shard_map/ppermute | solution.py:310
  76.6 2.5 %collective-permute-start.5 = (bf16[2,256,128]{2,1,0:T(8,128)(2,1)S(1)}, bf16[2,256,128]{2,1,0:T(8,128)(2,1)S(1)}, u32[]{:S(2)}, u32[]{:S(2)}) collective-permute-start(bf16[2,256,128]{2,1,0:T(8,128)(2,1)S(1)} %get-tuple-element.22.refs_0_), channel_id=1, source_target_pairs={{0,192},{64,128},{128,64},{192,0},{1,193},{65,129},{129,65},{193,1... | collective-permute-start | bytes 393224 | tf_op jit(solution)/shard_map/ppermute | solution.py:310
  79.8 0.1 stack.132.info_ref
  79.9 0.7 collective-permute-done.2
  80.6 2.0 collective-permute-done.4.refs_2_
  82.5 6.8 %collective-permute-done.5.refs_3_ = bf16[2,256,128]{2,1,0:T(8,128)(2,1)S(1)} collective-permute-done((bf16[2,256,128]{2,1,0:T(8,128)(2,1)S(1)}, bf16[2,256,128]{2,1,0:T(8,128)(2,1)S(1)}, u32[]{:S(2)}, u32[]{:S(2)}) %collective-permute-start.5) | collective-permute-done | bytes 131104 | tf_op jit(solution)/shard_map/ppermute | solution.py:310
  89.4 4.4 %shard_map.151 = bf16[8,4,80,128]{3,2,1,0:T(8,128)(2,1)} custom-call(s32[5]{0:T(128)S(1)} %stack.132.info_ref, bf16[8,256,128]{2,1,0:T(8,128)(2,1)S(1)} %all-to-all-done.1.q_ref, bf16[2,256,128]{2,1,0:T(8,128)(2,1)S(1)} %get-tuple-element.22.refs_0_, bf16[2,256,128]{2,1,0:T(8,128)(2,1)S(1)} %collective-permute-done.3.refs_1_, ...), custom_call_target="tpu_custom_call" | custom-call | flops 2147483648 | bytes 1703956 | tf_op jit(solution)/shard_map/pallas_call | solution.py:33
  93.7 8.9 %all-to-all-start.2 = ((bf16[32,80,128]{2,1,0:T(8,128)(2,1)}), bf16[32,80,128]{2,1,0:T(8,128)(2,1)}, u32[]{:S(2)}, u32[]{:S(2)}) async-start(bf16[32,80,128]{2,1,0:T(8,128)(2,1)} %bitcast.23), calls=%async_computation.2 | async-start | bytes 1310720 | tf_op jit(solution)/shard_map/all_to_all | solution.py:288
  102.7 0.0 all-gather.12.cloned.1.call-start
  102.7 1.1 pad_maximum_fusion.mine_ref
  103.8 2.2 %collective-permute-start.6 = (bf16[3,128,1024]{2,1,0:T(8,128)(2,1)S(1)}, bf16[3,128,1024]{2,1,0:T(8,128)(2,1)}, u32[]{:S(2)}, u32[]{:S(2)}) collective-permute-start(bf16[3,128,1024]{2,1,0:T(8,128)(2,1)S(1)} %pad_maximum_fusion.mine_ref), channel_id=1, source_target_pairs={{0,16},{16,0},{1,17},{17,1},{2,18},{18,2},{3,19},{19,3},{4,20},{20... | collective-permute-start | bytes 2359304 | tf_op jit(solution)/shard_map/ppermute | solution.py:310
  106.1 0.6 stack.141.info_ref
  106.7 1.7 copy-done
  108.4 3.7 %shard_map.152 = bf16[512,128]{1,0:T(8,128)(2,1)} custom-call(bf16[16,512,128]{2,1,0:T(8,128)(2,1)S(1)} %bitcast.45, f32[1,2048]{1,0:T(1,128)S(1)} %bitcast.47, bf16[2048,128]{1,0:T(8,128)(2,1)S(1)} %copy-done.5), custom_call_target="tpu_custom_call" | custom-call | flops 268435456 | bytes 2760704 | tf_op jit(solution)/shard_map/pallas_call | solution.py:33
  112.1 2.7 %all-to-all-done.2 = bf16[32,80,128]{2,1,0:T(8,128)(2,1)} async-done(((bf16[32,80,128]{2,1,0:T(8,128)(2,1)}), bf16[32,80,128]{2,1,0:T(8,128)(2,1)}, u32[]{:S(2)}, u32[]{:S(2)}) %all-to-all-start.2) | async-done | bytes 655392 | tf_op jit(solution)/shard_map/all_to_all | solution.py:288
  114.8 3.9 %shard_map.153 = bf16[4,16,2048]{2,1,0:T(8,128)(2,1)} custom-call(s32[5]{0:T(128)} %stack.141.info_ref, bf16[8,4,80,128]{3,2,1,0:T(8,128)(2,1)} %bitcast.32.r_ref, bf16[128,2048]{1,0:T(8,128)(2,1)} %own_ref.1, bf16[3,128,1024]{2,1,0:T(8,128)(2,1)} %copy-done.8, bf16[3,128,1024]{2,1,0:T(8,128)(2,1)} %collective-permute-done.6.theirs_ref), custom_call_target="tpu_custom_call" | custom-call | flops 134217728 | bytes 3014676 | tf_op jit(solution)/shard_map/pallas_call | solution.py:33
  118.7 12.6 %all_to_all.35.r_ref = bf16[4,16,2048]{2,1,0:T(8,128)(2,1)S(1)} all-to-all(bf16[4,16,2048]{2,1,0:T(8,128)(2,1)} %shard_map.153), channel_id=1, replica_groups=mesh['zl'=2,'yh'=4,'yl'=2,'c'=2,'zh'=4,'x'=4] {'zh'}, dimensions={0} | all-to-all | bytes 524288 | tf_op jit(solution)/shard_map/all_to_all | solution.py:288
  131.3 5.0 %collective-permute-start.7 = (bf16[4,2,1024,128]{3,2,1,0:T(8,128)(2,1)}, bf16[4,2,1024,128]{3,2,1,0:T(8,128)(2,1)}, u32[]{:S(2)}, u32[]{:S(2)}) collective-permute-start(bf16[4,2,1024,128]{3,2,1,0:T(8,128)(2,1)} %bitcast.50), channel_id=1, source_target_pairs={{0,16},{16,0},{1,17},{17,1},{2,18},{18,2},{3,19},{19,3},{4,20},{20... | collective-permute-start | bytes 6291464 | tf_op jit(solution)/shard_map/ppermute | solution.py:310
  136.3 0.0 all-gather.8.cloned.1.call-start
  136.4 13.9 %all_to_all.36 = bf16[4,16,2048]{2,1,0:T(8,128)(2,1)} all-to-all(bf16[4,16,2048]{2,1,0:T(8,128)(2,1)S(1)} %shard_map.154), channel_id=1, replica_groups=mesh['zl'=2,'yh'=4,'yl'=2,'c'=2,'zh'=4,'x'=4] {'zh'}, dimensions={0} | all-to-all | bytes 524288 | tf_op jit(solution)/shard_map/all_to_all | solution.py:288
  150.3 5.8 %shard_map.155 = bf16[4,4,2,64,128]{4,3,2,1,0:T(8,128)(2,1)} custom-call(s32[5]{0:T(128)} %stack.141.info_ref, bf16[64,2048]{1,0:T(8,128)(2,1)} %bitcast.49, f32[1,2048]{1,0:T(1,128)} %bitcast.56, bf16[4,2,1024,128]{3,2,1,0:T(8,128)(2,1)} %bitcast.51, bf16[4,2,1024,128]{3,2,1,0:T(8,128)(2,1)} %collective-permute-done.7.theirs_ref), custom_call_target="tpu_custom_call" | custom-call | flops 268435456 | bytes 4988948 | tf_op jit(solution)/shard_map/pallas_call | solution.py:33
  156.1 5.1 %all-to-all-start.5 = ((bf16[16,2,64,128]{3,2,1,0:T(8,128)(2,1)}), bf16[16,2,64,128]{3,2,1,0:T(8,128)(2,1)S(1)}, u32[]{:S(2)}, u32[]{:S(2)}) async-start(bf16[16,2,64,128]{3,2,1,0:T(8,128)(2,1)} %bitcast.52), calls=%async_computation.5 | async-start | bytes 1048576 | tf_op jit(solution)/shard_map/all_to_all | solution.py:288
  161.3 0.6 stack.127.info_ref
  161.9 11.3 %all-to-all-done.5 = bf16[16,2,64,128]{3,2,1,0:T(8,128)(2,1)S(1)} async-done(((bf16[16,2,64,128]{3,2,1,0:T(8,128)(2,1)}), bf16[16,2,64,128]{3,2,1,0:T(8,128)(2,1)S(1)}, u32[]{:S(2)}, u32[]{:S(2)}) %all-to-all-start.5) | async-done | bytes 524320 | tf_op jit(solution)/shard_map/all_to_all | solution.py:288
  173.2 0.8 copy-done.9
  174.0 9.1 %shard_map.156 = bf16[8,1,528,128]{3,2,1,0:T(8,128)(2,1)} custom-call(s32[17]{0:T(128)} %stack.127.info_ref, bf16[8,512,128]{2,1,0:T(8,128)(2,1)} %bitcast.57, bf16[4,4,2,64,128]{4,3,2,1,0:T(8,128)(2,1)} %bitcast.54), custom_call_target="tpu_custom_call" | custom-call | flops 4294967296 | bytes 2654276 | tf_op jit(solution)/shard_map/pallas_call | solution.py:33
  183.1 5.9 %all-gather.8.cloned.1.call-done = bf16[256,2048]{1,0:T(8,128)(2,1)} async-done(((bf16[64,2048]{1,0:T(8,128)(2,1)}), bf16[256,2048]{1,0:T(8,128)(2,1)}) %all-gather.8.cloned.1.call-update) | async-done | bytes 1048592 | tf_op jit(solution)/shard_map/all_gather | solution.py:445
  188.9 5.4 %all-to-all-start.6 = ((bf16[8,528,128]{2,1,0:T(8,128)(2,1)}), bf16[8,528,128]{2,1,0:T(8,128)(2,1)S(1)}, u32[]{:S(2)}, u32[]{:S(2)}) async-start(bf16[8,528,128]{2,1,0:T(8,128)(2,1)} %bitcast.53), calls=%async_computation.6 | async-start | bytes 2162688 | tf_op jit(solution)/shard_map/all_to_all | solution.py:288
  195.0 0.1 pad_add_fusion.info_ref
  195.1 1.5 constant_dynamic-slice_fusion
  196.6 10.1 %all-to-all-done.6.r_ref = bf16[8,528,128]{2,1,0:T(8,128)(2,1)S(1)} async-done(((bf16[8,528,128]{2,1,0:T(8,128)(2,1)}), bf16[8,528,128]{2,1,0:T(8,128)(2,1)S(1)}, u32[]{:S(2)}, u32[]{:S(2)}) %all-to-all-start.6) | async-done | bytes 1081376 | tf_op jit(solution)/shard_map/all_to_all | solution.py:288
  206.7 1.9 shard_map.157
  (31 shorter events, 0.2 us)
Async XLA Ops:
  7.2 99.5 %all-gather.10.cloned.1.call-start = ((), (), s32[]{:S(2)}) async-start(), calls=%async_computation.8 | async-start | bytes 2228224 | tf_op jit(solution)/shard_map/all_gather | solution.py:353
  9.9 36.8 %all-to-all-start = ((bf16[16,256,128]{2,1,0:T(8,128)(2,1)}), bf16[16,256,128]{2,1,0:T(8,128)(2,1)S(1)}, u32[]{:S(2)}, u32[]{:S(2)}) async-start(bf16[16,256,128]{2,1,0:T(8,128)(2,1)} %shard_map.149), calls=%async_computation | async-start | bytes 2097152 | tf_op jit(solution)/shard_map/all_to_all | solution.py:288
  23.3 23.3 %copy-start.1 = (bf16[2048,128]{1,0:T(8,128)(2,1)S(1)}, bf16[2048,128]{1,0:T(8,128)(2,1)}, u32[]{:S(2)}) copy-start(bf16[2048,128]{1,0:T(8,128)(2,1)} %wq_ref.2) | copy-start | bytes 1572868
  23.3 23.3 %copy-start.2 = (bf16[2048,128]{1,0:T(8,128)(2,1)S(1)}, bf16[2048,128]{1,0:T(8,128)(2,1)}, u32[]{:S(2)}) copy-start(bf16[2048,128]{1,0:T(8,128)(2,1)} %wk_ref.1) | copy-start | bytes 1572868
  23.3 23.3 %copy-start.3 = (bf16[2048,128]{1,0:T(8,128)(2,1)S(1)}, bf16[2048,128]{1,0:T(8,128)(2,1)}, u32[]{:S(2)}) copy-start(bf16[2048,128]{1,0:T(8,128)(2,1)} %wv_ref.1) | copy-start | bytes 1572868
  23.4 23.3 %copy-start.6 = (f32[2048]{0:T(1024)S(1)}, f32[2048]{0:T(1024)}, u32[]{:S(2)}) copy-start(f32[2048]{0:T(1024)} %param.18) | copy-start | bytes 24580
  23.4 107.9 %all-gather.14.cloned.1.call-start = ((), (), s32[]{:S(2)}) async-start(), calls=%async_computation.10 | async-start | bytes 2621440 | tf_op jit(solution)/shard_map/all_gather | solution.py:359
  24.5 16.7 %collective-permute-start = (bf16[128,1024]{1,0:T(8,128)(2,1)S(1)}, bf16[128,1024]{1,0:T(8,128)(2,1)}, u32[]{:S(2)}, u32[]{:S(2)}) collective-permute-start(bf16[128,1024]{1,0:T(8,128)(2,1)S(1)} %constant_dynamic-slice_fusion.2), channel_id=1, source_target_pairs={{0,1},{1,0},{2,3},{3,2},{4,5},{5,4},{6,7},{7,6},{8,9},{9,8},{10,11... | collective-permute-start | bytes 786440 | tf_op jit(solution)/shard_map/ppermute | solution.py:310
  27.8 18.9 %collective-permute-start.1 = (bf16[128,1024]{1,0:T(8,128)(2,1)S(1)}, bf16[128,1024]{1,0:T(8,128)(2,1)}, u32[]{:S(2)}, u32[]{:S(2)}) collective-permute-start(bf16[128,1024]{1,0:T(8,128)(2,1)S(1)} %constant_dynamic-slice_fusion.2), channel_id=1, source_target_pairs={{0,3},{1,2},{2,1},{3,0},{4,7},{5,6},{6,5},{7,4},{8,11},{9,10},{10,... | collective-permute-start | bytes 786440 | tf_op jit(solution)/shard_map/ppermute | solution.py:310
  49.6 0.8 copy-start.4
  50.4 30.2 %all-to-all-start.1 = ((bf16[8,256,128]{2,1,0:T(8,128)(2,1)}), bf16[8,256,128]{2,1,0:T(8,128)(2,1)S(1)}, u32[]{:S(2)}, u32[]{:S(2)}) async-start(bf16[8,256,128]{2,1,0:T(8,128)(2,1)} %copy-done.4), calls=%async_computation.1 | async-start | bytes 1048576 | tf_op jit(solution)/shard_map/all_to_all | solution.py:288
  65.8 14.8 %collective-permute-start.2 = (bf16[128,1024]{1,0:T(8,128)(2,1)}, bf16[128,1024]{1,0:T(8,128)(2,1)S(1)}, u32[]{:S(2)}, u32[]{:S(2)}) collective-permute-start(bf16[128,1024]{1,0:T(8,128)(2,1)} %collective-permute-done), channel_id=1, source_target_pairs={{0,3},{1,2},{2,1},{3,0},{4,7},{5,6},{6,5},{7,4},{8,11},{9,10},{10,... | collective-permute-start | bytes 786440 | tf_op jit(solution)/shard_map/ppermute | solution.py:310
  67.7 12.9 %collective-permute-start.3 = (bf16[2,256,128]{2,1,0:T(8,128)(2,1)S(1)}, bf16[2,256,128]{2,1,0:T(8,128)(2,1)S(1)}, u32[]{:S(2)}, u32[]{:S(2)}) collective-permute-start(bf16[2,256,128]{2,1,0:T(8,128)(2,1)S(1)} %get-tuple-element.22.refs_0_), channel_id=1, source_target_pairs={{0,64},{64,0},{128,192},{192,128},{1,65},{65,1},{129,193},{193,129... | collective-permute-start | bytes 393224 | tf_op jit(solution)/shard_map/ppermute | solution.py:310
  71.9 10.6 %collective-permute-start.4 = (bf16[2,256,128]{2,1,0:T(8,128)(2,1)S(1)}, bf16[2,256,128]{2,1,0:T(8,128)(2,1)S(1)}, u32[]{:S(2)}, u32[]{:S(2)}) collective-permute-start(bf16[2,256,128]{2,1,0:T(8,128)(2,1)S(1)} %get-tuple-element.22.refs_0_), channel_id=1, source_target_pairs={{0,128},{64,192},{128,0},{192,64},{1,129},{65,193},{129,1},{193,65... | collective-permute-start | bytes 393224 | tf_op jit(solution)/shard_map/ppermute | solution.py:310
  76.6 12.7 %collective-permute-start.5 = (bf16[2,256,128]{2,1,0:T(8,128)(2,1)S(1)}, bf16[2,256,128]{2,1,0:T(8,128)(2,1)S(1)}, u32[]{:S(2)}, u32[]{:S(2)}) collective-permute-start(bf16[2,256,128]{2,1,0:T(8,128)(2,1)S(1)} %get-tuple-element.22.refs_0_), channel_id=1, source_target_pairs={{0,192},{64,128},{128,64},{192,0},{1,193},{65,129},{129,65},{193,1... | collective-permute-start | bytes 393224 | tf_op jit(solution)/shard_map/ppermute | solution.py:310
  93.7 12.9 %copy-start.5 = (bf16[2048,128]{1,0:T(8,128)(2,1)S(1)}, bf16[2048,128]{1,0:T(8,128)(2,1)}, u32[]{:S(2)}) copy-start(bf16[2048,128]{1,0:T(8,128)(2,1)} %wq_ref.3) | copy-start | bytes 1572868
  93.7 12.9 %copy-start.7 = (f32[2048]{0:T(1024)S(1)}, f32[2048]{0:T(1024)}, u32[]{:S(2)}) copy-start(f32[2048]{0:T(1024)} %param.27) | copy-start | bytes 24580
  93.7 21.0 %all-to-all-start.2 = ((bf16[32,80,128]{2,1,0:T(8,128)(2,1)}), bf16[32,80,128]{2,1,0:T(8,128)(2,1)}, u32[]{:S(2)}, u32[]{:S(2)}) async-start(bf16[32,80,128]{2,1,0:T(8,128)(2,1)} %bitcast.23), calls=%async_computation.2 | async-start | bytes 1310720 | tf_op jit(solution)/shard_map/all_to_all | solution.py:288
  102.7 59.2 %all-gather.12.cloned.1.call-start = ((), (), s32[]{:S(2)}) async-start(), calls=%async_computation.9 | async-start | bytes 1179648 | tf_op jit(solution)/shard_map/all_gather | solution.py:447
  103.8 8.3 %copy-start.8 = (bf16[3,128,1024]{2,1,0:T(8,128)(2,1)}, bf16[3,128,1024]{2,1,0:T(8,128)(2,1)S(1)}, u32[]{:S(2)}) copy-start(bf16[3,128,1024]{2,1,0:T(8,128)(2,1)S(1)} %pad_maximum_fusion.mine_ref) | copy-start | bytes 2359300
  103.8 10.9 %collective-permute-start.6 = (bf16[3,128,1024]{2,1,0:T(8,128)(2,1)S(1)}, bf16[3,128,1024]{2,1,0:T(8,128)(2,1)}, u32[]{:S(2)}, u32[]{:S(2)}) collective-permute-start(bf16[3,128,1024]{2,1,0:T(8,128)(2,1)S(1)} %pad_maximum_fusion.mine_ref), channel_id=1, source_target_pairs={{0,16},{16,0},{1,17},{17,1},{2,18},{18,2},{3,19},{19,3},{4,20},{20... | collective-permute-start | bytes 2359304 | tf_op jit(solution)/shard_map/ppermute | solution.py:310
  106.7 1.7 copy-start
  131.3 19.0 %collective-permute-start.7 = (bf16[4,2,1024,128]{3,2,1,0:T(8,128)(2,1)}, bf16[4,2,1024,128]{3,2,1,0:T(8,128)(2,1)}, u32[]{:S(2)}, u32[]{:S(2)}) collective-permute-start(bf16[4,2,1024,128]{3,2,1,0:T(8,128)(2,1)} %bitcast.50), channel_id=1, source_target_pairs={{0,16},{16,0},{1,17},{17,1},{2,18},{18,2},{3,19},{19,3},{4,20},{20... | collective-permute-start | bytes 6291464 | tf_op jit(solution)/shard_map/ppermute | solution.py:310
  136.3 52.6 %all-gather.8.cloned.1.call-start = ((), (), s32[]{:S(2)}) async-start(), calls=%async_computation.7 | async-start | bytes 1310720 | tf_op jit(solution)/shard_map/all_gather | solution.py:445
  156.1 17.0 %all-to-all-start.5 = ((bf16[16,2,64,128]{3,2,1,0:T(8,128)(2,1)}), bf16[16,2,64,128]{3,2,1,0:T(8,128)(2,1)S(1)}, u32[]{:S(2)}, u32[]{:S(2)}) async-start(bf16[16,2,64,128]{3,2,1,0:T(8,128)(2,1)} %bitcast.52), calls=%async_computation.5 | async-start | bytes 1048576 | tf_op jit(solution)/shard_map/all_to_all | solution.py:288
  173.2 0.8 copy-start.9
  188.9 17.7 %all-to-all-start.6 = ((bf16[8,528,128]{2,1,0:T(8,128)(2,1)}), bf16[8,528,128]{2,1,0:T(8,128)(2,1)S(1)}, u32[]{:S(2)}, u32[]{:S(2)}) async-start(bf16[8,528,128]{2,1,0:T(8,128)(2,1)} %bitcast.53), calls=%async_computation.6 | async-start | bytes 2162688 | tf_op jit(solution)/shard_map/all_to_all | solution.py:288
Sparse Core Ops, SparseCore 0:
  11.0 82.4 all-gather.9
  95.6 35.4 all-gather.13
  136.4 22.0 all-gather.11
  160.5 28.4 all-gather.7

commit v3 on v2

--- a/solution.py
+++ b/solution.py
@@ -61,9 +61,9 @@
     wait_for(started([(x_ref, out_ref.at[i]) for i in range(out_ref.shape[0])], sems))
 
 
-def repeated(x, times):
+def repeated(x, times, limit):
     return call(
-        repeat_kernel, shape(times, *x.shape), x, specs=[VMEM], out=HBM, scratch=[DMA((times,))], limit=63.9
+        repeat_kernel, shape(times, *x.shape), x, specs=[VMEM], out=HBM, scratch=[DMA((times,))], limit=limit
     )
 
 
@@ -77,12 +77,16 @@
     return [(c * inverse * g).astype(BF16) for c, g in zip(centers, gains)]
 
 
-def norm_gathered(x_ref, gain_ref, norm_ref, step=64):
+def x_first(j):
+    return (j % 4) * 4 + j // 4
+
+
+def norm_gathered(x_ref, gain_ref, norm_ref, order=lambda j: j, step=64):
     rows = x_ref.shape[1]
 
     def body(i, _):
         r = pl.multiple_of(i * step, step)
-        pieces = [x_ref[j, pl.ds(r, step), :].astype(F32) for j in range(16)]
+        pieces = [x_ref[order(j), pl.ds(r, step), :].astype(F32) for j in range(16)]
         gains = [gain_ref[:, j * 128 : (j + 1) * 128] for j in range(16)]
         for j, n in enumerate(normed_rows(pieces, gains)):
             norm_ref[pl.ds(r, step), j * 128 : (j + 1) * 128] = n
@@ -95,7 +99,7 @@
     weights = started(
         [(w, w_ref.at[:, i * 128 : (i + 1) * 128]) for i, w in enumerate((wq_ref, wk_ref, wv_ref))], in_sems
     )
-    norm_gathered(x_ref, gain_ref, norm_ref)
+    norm_gathered(x_ref, gain_ref, norm_ref, x_first)
     wait_for(weights)
     out = jnp.dot(norm_ref[...], w_ref[...], preferred_element_type=F32)
     q_one_ref[...] = (out[:, :128] * SCORE_SCALE).astype(BF16)
@@ -239,7 +243,7 @@
 def residual_kernel(r_ref, s_ref, out_ref):
     for j in range(16):
         cols = slice(j * 128, (j + 1) * 128)
-        total = s_ref[j].astype(F32)
+        total = s_ref[x_first(j)].astype(F32)
         for z in range(4):
             total = total + r_ref[z, :, cols].astype(F32)
         total = total.astype(BF16)
@@ -247,13 +251,13 @@
             out_ref[z, :, cols] = total
 
 
-def memory_kernel(info_ref, e_ref, gain_ref, mine_ref, theirs_ref, kv_ref, norm_ref, e_vmem, w_ref, sems, e_sem):
+def memory_kernel(info_ref, e_ref, gain_ref, mine_ref, theirs_ref, kv_ref, own_ref, norm_ref, e_vmem, w_ref, sems, e_sem):
     core = info_ref[0]
     half = D // 2
     rows = started([(e_ref, e_vmem)], e_sem)
     copies = started(
         [
-            (ref.at[h, t], w_ref.at[h, pl.ds(pl.multiple_of(first * half, half), half), t * 128 : (t + 1) * 128])
+            (ref.at[h, t], w_ref.at[h, t, pl.ds(pl.multiple_of(first * half, half), half), :])
             for h in range(4)
             for ref, first in ((mine_ref, core), (theirs_ref, 1 - core))
             for t in range(2)
@@ -261,13 +265,17 @@
         sems,
     )
     wait_for(rows)
+    for h in range(4):
+        at = pl.multiple_of((info_ref[5] * 4 + h) * 128, 128)
+        own_ref[h] = e_vmem[:, pl.ds(at, 128)]
     pieces = [e_vmem[:, j * 128 : (j + 1) * 128].astype(F32) for j in range(16)]
     gains = [gain_ref[:, j * 128 : (j + 1) * 128] for j in range(16)]
     for j, n in enumerate(normed_rows(pieces, gains)):
         norm_ref[:, j * 128 : (j + 1) * 128] = n
     for h in range(4):
         wait_for(copies[h * 4 : (h + 1) * 4])
-        out = jnp.dot(norm_ref[...], w_ref[h], preferred_element_type=F32).astype(BF16)
+        weights = jnp.concatenate([w_ref[h, 0], w_ref[h, 1]], axis=1)
+        out = jnp.dot(norm_ref[...], weights, preferred_element_type=F32).astype(BF16)
         for b in range(4):
             kv_ref[b, h, 0] = out[:, :128]
             kv_ref[b, h, 1] = out[:, 128:]
@@ -335,7 +343,7 @@
     at = {name: lax.axis_index(name) for name, _ in AXES}
     seq_at = ((at["zl"] * 4 + at["yh"]) * 2 + at["yl"]) * 2 + at["c"]
     quarter = rows // 4
-    core_info = jnp.stack([at["c"], at["x"], at["x"] ^ 1, at["x"] ^ 3, at["x"] ^ 2])
+    core_info = jnp.stack([at["c"], at["x"], at["x"] ^ 1, at["x"] ^ 3, at["x"] ^ 2, at["zh"]])
 
     def first_of(yh):
         return (((at["zl"] * 4 + yh) * 2 + at["yl"]) * 2 + at["c"]) * rows
@@ -348,16 +356,10 @@
     gains = [g.reshape(1, D) for g in (encoder_gain, final_gain, cross_gain)]
 
     half = at["c"] * (D // 2)
-    out_half = lax.dynamic_slice_in_dim(output_weight, half, D // 2, 1)
-    out_halves = [swapped(out_half, "x", 4, k) for k in (1, 3)]
-    target_full = lax.all_gather(target_hidden, HEAD, axis=0)
-    source_full = exchange(repeated(source_hidden, 16), HEAD)
-    source_full, *out_halves = together(source_full, *out_halves)
-    out_halves.append(swapped(out_halves[0], "x", 4, 3))
     half_weights = jnp.stack([lax.dynamic_slice_in_dim(w, half, D // 2, 0) for w in (cross_key, cross_value)])
-    source_full, half_weights = together(source_full, half_weights)
     mine = lax.all_gather(half_weights, "x", axis=0)
-
+    source_some = exchange(repeated(source_hidden, 4, 63.9), "zh")
+    source_full = exchange(repeated(source_some, 4, 60), "x").reshape(16, rows, 128)
     queries, keys_values = call(
         qkv_kernel,
         (shape(8, rows, 128), shape(2, rows, 128)),
@@ -377,13 +379,41 @@
         ],
         flops=2 * rows * D * 384,
     )
+    queries, target_hidden = together(queries, target_hidden)
+    target_hidden, mine = together(target_hidden, mine)
+    target_full = lax.all_gather(target_hidden, HEAD, axis=0)
     key_sets = [keys_values] + [swapped(keys_values, "yh", 4, k) for k in (1, 2, 3)]
     queries = exchange(queries, QUERY_GROUP)
-    queries, out_halves[2] = together(queries, out_halves[2])
+    out_half = lax.dynamic_slice_in_dim(output_weight, half, D // 2, 1)
+    queries, out_half = together(queries, out_half)
+    out_halves = [swapped(out_half, "x", 4, k) for k in (1, 3, 2)]
+    partial = attend(queries, key_sets, [(k, ()) for k in range(4)], key_info, quarter, False)
+    partial, mine, *out_halves = together(partial, mine, *out_halves)
     out_mine = jnp.stack(out_halves)
     out_theirs = swapped(out_mine, "c", 2, 1)
-    partial = attend(queries, key_sets, [(k, ()) for k in range(4)], key_info, quarter, False)
     partial = exchange(partial.reshape(32, rows // 4 + 16, 128), QUERY_GROUP + ("x",))
+    shares = call(
+        project_out_kernel,
+        shape(4, quarter // 4, D),
+        core_info,
+        partial.reshape(8, 4, quarter + 16, 128),
+        output_weight,
+        out_mine,
+        out_theirs,
+        specs=[SMEM, VMEM] + [ANY] * 3,
+        scratch=[pltpu.VMEM((quarter, 512), BF16), pltpu.VMEM((512, D), BF16), DMA((7,))],
+        limit=62.5,
+        flops=2 * quarter * 512 * D,
+    )
+    shares = exchange(shares, "zh")
+    theirs = swapped(mine, "c", 2, 1)
+    shares, theirs = together(shares, theirs)
+    first = at["x"] * quarter + at["zh"] * (quarter // 4)
+    own_source = lax.dynamic_slice_in_dim(source_full, first, quarter // 4, 1)
+    encoder_rows = call(
+        residual_kernel, shape(4, quarter // 4, D), shares, own_source, specs=[VMEM] * 2
+    )
+    encoder_rows = exchange(encoder_rows, "zh").reshape(quarter, D)
     target_queries = call(
         target_kernel,
         shape(target_rows, 128),
@@ -400,32 +430,10 @@
         ],
         flops=2 * target_rows * D * 128,
     )
-    partial, target_queries = together(partial, target_queries)
-    shares = call(
-        project_out_kernel,
-        shape(4, quarter // 4, D),
-        core_info,
-        partial.reshape(8, 4, quarter + 16, 128),
-        output_weight,
-        out_mine,
-        out_theirs,
-        specs=[SMEM, VMEM] + [ANY] * 3,
-        scratch=[pltpu.VMEM((quarter, 512), BF16), pltpu.VMEM((512, D), BF16), DMA((7,))],
-        limit=62.5,
-        flops=2 * quarter * 512 * D,
-    )
-    shares = exchange(shares, "zh")
-    shares, mine = together(shares, mine)
-    theirs = swapped(mine, "c", 2, 1)
-    first = at["x"] * quarter + at["zh"] * (quarter // 4)
-    own_source = lax.dynamic_slice_in_dim(source_full, first, quarter // 4, 1)
-    encoder_rows = call(
-        residual_kernel, shape(4, quarter // 4, D), shares, own_source, specs=[VMEM] * 2
-    )
-    encoder_rows = exchange(encoder_rows, "zh").reshape(quarter, D)
-    memory = call(
+    encoder_rows, target_queries = together(encoder_rows, target_queries)
+    memory, own_columns = call(
         memory_kernel,
-        shape(4, 4, 2, quarter, 128),
+        (shape(4, 4, 2, quarter, 128), shape(4, quarter, 128)),
         core_info,
         encoder_rows,
         gains[1],
@@ -435,24 +443,23 @@
         scratch=[
             pltpu.VMEM((quarter, D), BF16),
             pltpu.VMEM((quarter, D), BF16),
-            pltpu.VMEM((4, D, 256), BF16),
+            pltpu.VMEM((4, 2, D, 128), BF16),
             DMA((16,)),
             DMA((1,)),
         ],
         limit=63,
         flops=2 * quarter * D * 1024,
     )
-    encoder_full = lax.all_gather(encoder_rows, "x", axis=0, tiled=True)
 
     target_queries = lax.all_gather(target_queries, QUERY_GROUP, axis=0)
     memory = exchange(memory.reshape(16, 2, quarter, 128), ("yh", "x")).reshape(4, 4, 2, quarter, 128)
+    memory, own_columns = together(memory, own_columns)
+    encoder_out = exchange(own_columns, "x").reshape(rows, 128)
     crossed = attend(
         target_queries, [memory], [(0, (k // 4, k % 4)) for k in range(16)], memory_info, target_rows, True
     )
-    crossed, encoder_full = together(crossed, encoder_full)
+    crossed, encoder_out = together(crossed, encoder_out)
     crossed = exchange(crossed.reshape(8, target_rows + 16, 128), QUERY_GROUP)
-    head_at = at["zh"] * 4 + at["x"]
-    encoder_out = lax.dynamic_slice_in_dim(encoder_full, head_at * 128, 128, 1)
     cross_context = call(
         finish_kernel, shape(target_rows, 128), target_info, crossed, specs=[SMEM, VMEM]
     )

time: 218 us -> 237 us (1.087)
  blocking collectives: 26.5 us -> 48.9 us
  starting transfers between devices: 75.8 us -> 63.6 us
  waiting for transfers between devices: 53.3 us -> 59.6 us
  Pallas kernels: 33.7 us -> 36.1 us
    all_to_all x5 -> x7, waiting for transfers between devices: 24 us -> 53.3 us  [exchange(): return lax.all_to_all(x, axes, 0, 0, tiled=True)]
    all_to_all x2, blocking collectives: 26.5 us -> 48.9 us  [exchange(): return lax.all_to_all(x, axes, 0, 0, tiled=True)]
    ppermute x8, waiting for transfers between devices: 22.7 us -> 6.23 us  [swapped(): return lax.ppermute(x, axis, [(i, i ^ by) for i in range(size)])]
    all_to_all x5 -> x7, starting transfers between devices: 48.3 us -> 38.9 us  [exchange(): return lax.all_to_all(x, axes, 0, 0, tiled=True)]
    all_gather x1 -> x0, waiting for transfers between devices: 5.85 us -> none  [shards(): encoder_full = lax.all_gather(encoder_rows, 'x', axis=0, tiled=True)]
    ppermute x8, starting transfers between devices: 27.4 us -> 24.6 us  [swapped(): return lax.ppermute(x, axis, [(i, i ^ by) for i in range(size)])]
    pallas_call x9 -> x10, Pallas kernels: 33.7 us -> 36.1 us  [call(): pl.pallas_call(kernel, out_shape=out_shape, in_specs=specs, out_specs=jax...]
  transfers between devices with their start and end apart: 17 -> 18, of which waited for: 9 -> 8; matrix products, arithmetic and copies ran while one was open for 3% -> 2% of each run, Pallas kernels for 15% -> 15%
where the time goes in v3:
time: 237 us; the launch traced here: 233 us
  starting transfers between devices  63.6 us (27%)
  waiting for transfers between devices  59.6 us (25%)
  blocking collectives  48.9 us (21%)
  Pallas kernels  36.1 us (15%)
  between operations  15.4 us (6%)
  local copies, waits for them, and re-layouts  7.22 us (3%)
    all_to_all x7, waiting for transfers between devices, exchange(): return lax.all_to_all(x, axes, 0, 0, tiled=True)  53.3 us
    all_to_all x2, blocking collectives, exchange(): return lax.all_to_all(x, axes, 0, 0, tiled=True)  48.9 us
    all_to_all x7, starting transfers between devices, exchange(): return lax.all_to_all(x, axes, 0, 0, tiled=True)  38.9 us
    pallas_call x10, Pallas kernels, call(): pl.pallas_call(kernel, out_shape=out_shape, in_specs=specs, out_specs=jax...  36.1 us
    ppermute x8, starting transfers between devices, swapped(): return lax.ppermute(x, axis, [(i, i ^ by) for i in range(size)])  24.6 us
    ppermute x8, waiting for transfers between devices, swapped(): return lax.ppermute(x, axis, [(i, i ^ by) for i in range(size)])  6.23 us
  transfers between devices with their start and end apart: 18, of which 8 were waited for; matrix products, arithmetic and copies ran while one was open for 2% of the time, Pallas kernels for 15%

profile of v3, /device:TPU:1, one launch (start us, length us, event | category | flops | bytes accessed | tf_op | source)
XLA Modules:
  0.0 232.9 jit_solution(4574089099217705444)
XLA Ops:
  7.2 1.1 dynamic-slice_bitcast_fusion
  8.3 0.8 pad_maximum_fusion.1
  9.2 0.0 all-gather.9.cloned.1.call-start
  9.2 1.6 shard_map.149
  10.8 19.8 %all_to_all.45.x_ref = bf16[4,256,128]{2,1,0:T(8,128)(2,1)} all-to-all(bf16[4,256,128]{2,1,0:T(8,128)(2,1)} %shard_map.149), channel_id=1, replica_groups=mesh['zl'=2,'yh'=4,'yl'=2,'c'=2,'zh'=4,'x'=4] {'zh'}, dimensions={0} | all-to-all | bytes 524288 | tf_op jit(solution)/shard_map/all_to_all | solution.py:296
  30.7 2.0 shard_map.150
  32.7 29.0 %all_to_all.46 = bf16[4,4,256,128]{3,2,1,0:T(8,128)(2,1)S(1)} all-to-all(bf16[4,4,256,128]{3,2,1,0:T(8,128)(2,1)} %shard_map.150), channel_id=1, replica_groups=mesh['zl'=2,'yh'=4,'yl'=2,'c'=2,'zh'=4,'x'=4] {'x'}, dimensions={0} | all-to-all | bytes 2097152 | tf_op jit(solution)/shard_map/all_to_all | solution.py:296
  61.7 3.0 %shard_map.151 = (bf16[8,256,128]{2,1,0:T(8,128)(2,1)}, bf16[2,256,128]{2,1,0:T(8,128)(2,1)S(1)}) custom-call(bf16[16,256,128]{2,1,0:T(8,128)(2,1)S(1)} %bitcast.48, f32[1,2048]{1,0:T(1,128)S(1)} %bitcast.51, bf16[2048,128]{1,0:T(8,128)(2,1)S(1)} %copy-done.1, bf16[2048,128]{1,0:T(8,128)(2,1)S(1)} %copy-done.2, bf16[2048,128]{1,0:T(8,128)(2,1)S(1)} %copy-done.3), custom_call_target="tpu_custom_call" | custom-call | flops 402653184 | bytes 3284992 | tf_op jit(solution)/shard_map/pallas_call | solution.py:33
  64.8 5.8 %all-to-all-start.2 = ((bf16[8,256,128]{2,1,0:T(8,128)(2,1)}), bf16[8,256,128]{2,1,0:T(8,128)(2,1)S(1)}, u32[]{:S(2)}, u32[]{:S(2)}) async-start(bf16[8,256,128]{2,1,0:T(8,128)(2,1)} %get-tuple-element.26), calls=%async_computation.2 | async-start | bytes 1048576 | tf_op jit(solution)/shard_map/all_to_all | solution.py:296
  70.5 4.9 %collective-permute-start.2 = (bf16[2,256,128]{2,1,0:T(8,128)(2,1)S(1)}, bf16[2,256,128]{2,1,0:T(8,128)(2,1)S(1)}, u32[]{:S(2)}, u32[]{:S(2)}) collective-permute-start(bf16[2,256,128]{2,1,0:T(8,128)(2,1)S(1)} %get-tuple-element.28.refs_0_), channel_id=1, source_target_pairs={{0,192},{64,128},{128,64},{192,0},{1,193},{65,129},{129,65},{193,1... | collective-permute-start | bytes 393224 | tf_op jit(solution)/shard_map/ppermute | solution.py:318
  75.4 4.3 %collective-permute-start.1 = (bf16[2,256,128]{2,1,0:T(8,128)(2,1)S(1)}, bf16[2,256,128]{2,1,0:T(8,128)(2,1)S(1)}, u32[]{:S(2)}, u32[]{:S(2)}) collective-permute-start(bf16[2,256,128]{2,1,0:T(8,128)(2,1)S(1)} %get-tuple-element.28.refs_0_), channel_id=1, source_target_pairs={{0,128},{64,192},{128,0},{192,64},{1,129},{65,193},{129,1},{193,65... | collective-permute-start | bytes 393224 | tf_op jit(solution)/shard_map/ppermute | solution.py:318
  79.7 2.2 collective-permute-start
  81.9 1.0 constant_dynamic-slice_fusion.1
  82.9 2.7 %collective-permute-start.5 = (bf16[128,1024]{1,0:T(8,128)(2,1)S(1)}, bf16[128,1024]{1,0:T(8,128)(2,1)S(1)}, u32[]{:S(2)}, u32[]{:S(2)}) collective-permute-start(bf16[128,1024]{1,0:T(8,128)(2,1)S(1)} %constant_dynamic-slice_fusion.1), channel_id=1, source_target_pairs={{0,2},{1,3},{2,0},{3,1},{4,6},{5,7},{6,4},{7,5},{8,10},{9,11},{10,... | collective-permute-start | bytes 786440 | tf_op jit(solution)/shard_map/ppermute | solution.py:318
  85.6 4.1 %collective-permute-start.4 = (bf16[128,1024]{1,0:T(8,128)(2,1)S(1)}, bf16[128,1024]{1,0:T(8,128)(2,1)}, u32[]{:S(2)}, u32[]{:S(2)}) collective-permute-start(bf16[128,1024]{1,0:T(8,128)(2,1)S(1)} %constant_dynamic-slice_fusion.1), channel_id=1, source_target_pairs={{0,3},{1,2},{2,1},{3,0},{4,7},{5,6},{6,5},{7,4},{8,11},{9,10},{10,... | collective-permute-start | bytes 786440 | tf_op jit(solution)/shard_map/ppermute | solution.py:318
  89.7 1.9 collective-permute-start.3
  92.3 0.1 stack.142.info_ref
  92.4 2.5 %collective-permute-done.refs_1_ = bf16[2,256,128]{2,1,0:T(8,128)(2,1)S(1)} collective-permute-done((bf16[2,256,128]{2,1,0:T(8,128)(2,1)S(1)}, bf16[2,256,128]{2,1,0:T(8,128)(2,1)S(1)}, u32[]{:S(2)}, u32[]{:S(2)}) %collective-permute-start) | collective-permute-done | bytes 131104 | tf_op jit(solution)/shard_map/ppermute | solution.py:318
  94.9 4.4 %shard_map.152 = bf16[8,4,80,128]{3,2,1,0:T(8,128)(2,1)} custom-call(s32[5]{0:T(128)S(1)} %stack.142.info_ref, bf16[8,256,128]{2,1,0:T(8,128)(2,1)S(1)} %all-to-all-done.2.q_ref, bf16[2,256,128]{2,1,0:T(8,128)(2,1)S(1)} %get-tuple-element.28.refs_0_, bf16[2,256,128]{2,1,0:T(8,128)(2,1)S(1)} %collective-permute-done.refs_1_, ...), custom_call_target="tpu_custom_call" | custom-call | flops 2147483648 | bytes 1703956 | tf_op jit(solution)/shard_map/pallas_call | solution.py:33
  99.3 2.2 collective-permute-done.4
  101.5 2.4 %collective-permute-start.7 = (bf16[4,2,1024,128]{3,2,1,0:T(8,128)(2,1)}, bf16[4,2,1024,128]{3,2,1,0:T(8,128)(2,1)}, u32[]{:S(2)}, u32[]{:S(2)}) collective-permute-start(bf16[4,2,1024,128]{3,2,1,0:T(8,128)(2,1)} %bitcast.30.mine_ref), channel_id=1, source_target_pairs={{0,16},{16,0},{1,17},{17,1},{2,18},{18,2},{3,19},{19,3},{4,20},{20... | collective-permute-start | bytes 6291464 | tf_op jit(solution)/shard_map/ppermute | solution.py:318
  103.9 5.2 %all-to-all-start.3 = ((bf16[32,80,128]{2,1,0:T(8,128)(2,1)}), bf16[32,80,128]{2,1,0:T(8,128)(2,1)S(1)}, u32[]{:S(2)}, u32[]{:S(2)}) async-start(bf16[32,80,128]{2,1,0:T(8,128)(2,1)} %bitcast.31), calls=%async_computation.3 | async-start | bytes 1310720 | tf_op jit(solution)/shard_map/all_to_all | solution.py:296
  109.1 1.1 pad_maximum_fusion.mine_ref
  110.2 2.1 collective-permute-start.6
  112.4 0.6 stack.137.info_ref
  113.0 1.5 collective-permute-done.6.theirs_ref
  114.5 11.0 %all-to-all-done.3 = bf16[32,80,128]{2,1,0:T(8,128)(2,1)S(1)} async-done(((bf16[32,80,128]{2,1,0:T(8,128)(2,1)}), bf16[32,80,128]{2,1,0:T(8,128)(2,1)S(1)}, u32[]{:S(2)}, u32[]{:S(2)}) %all-to-all-start.3) | async-done | bytes 655392 | tf_op jit(solution)/shard_map/all_to_all | solution.py:296
  125.6 0.9 copy-done.8
  126.5 4.0 %shard_map.153 = bf16[4,16,2048]{2,1,0:T(8,128)(2,1)} custom-call(s32[6]{0:T(128)} %stack.137.info_ref, bf16[8,4,80,128]{3,2,1,0:T(8,128)(2,1)} %bitcast.53, bf16[128,2048]{1,0:T(8,128)(2,1)} %own_ref.1, bf16[3,128,1024]{2,1,0:T(8,128)(2,1)} %copy-done.7, bf16[3,128,1024]{2,1,0:T(8,128)(2,1)} %collective-permute-done.6.theirs_ref), custom_call_target="tpu_custom_call" | custom-call | flops 134217728 | bytes 3014680 | tf_op jit(solution)/shard_map/pallas_call | solution.py:33
  130.4 5.3 %all-to-all-start.4 = ((bf16[4,16,2048]{2,1,0:T(8,128)(2,1)}), bf16[4,16,2048]{2,1,0:T(8,128)(2,1)S(1)}, u32[]{:S(2)}, u32[]{:S(2)}) async-start(bf16[4,16,2048]{2,1,0:T(8,128)(2,1)} %shard_map.153), calls=%async_computation.4 | async-start | bytes 524288 | tf_op jit(solution)/shard_map/all_to_all | solution.py:296
  135.8 8.2 %all-to-all-done.4.r_ref = bf16[4,16,2048]{2,1,0:T(8,128)(2,1)S(1)} async-done(((bf16[4,16,2048]{2,1,0:T(8,128)(2,1)}), bf16[4,16,2048]{2,1,0:T(8,128)(2,1)S(1)}, u32[]{:S(2)}, u32[]{:S(2)}) %all-to-all-start.4) | async-done | bytes 262176 | tf_op jit(solution)/shard_map/all_to_all | solution.py:296
  144.0 0.8 shard_map.154
  144.8 3.7 %all-to-all-start.5 = ((bf16[4,16,2048]{2,1,0:T(8,128)(2,1)}), bf16[4,16,2048]{2,1,0:T(8,128)(2,1)S(1)}, u32[]{:S(2)}, u32[]{:S(2)}) async-start(bf16[4,16,2048]{2,1,0:T(8,128)(2,1)} %shard_map.154), calls=%async_computation.5 | async-start | bytes 524288 | tf_op jit(solution)/shard_map/all_to_all | solution.py:296
  148.5 1.6 copy-done
  150.1 3.7 %shard_map.155 = bf16[512,128]{1,0:T(8,128)(2,1)} custom-call(bf16[16,512,128]{2,1,0:T(8,128)(2,1)S(1)} %bitcast.50, f32[1,2048]{1,0:T(1,128)S(1)} %bitcast.52, bf16[2048,128]{1,0:T(8,128)(2,1)S(1)} %copy-done.4), custom_call_target="tpu_custom_call" | custom-call | flops 268435456 | bytes 2760704 | tf_op jit(solution)/shard_map/pallas_call | solution.py:33
  153.8 2.8 %all-to-all-done.5 = bf16[4,16,2048]{2,1,0:T(8,128)(2,1)S(1)} async-done(((bf16[4,16,2048]{2,1,0:T(8,128)(2,1)}), bf16[4,16,2048]{2,1,0:T(8,128)(2,1)S(1)}, u32[]{:S(2)}, u32[]{:S(2)}) %all-to-all-start.5) | async-done | bytes 262176 | tf_op jit(solution)/shard_map/all_to_all | solution.py:296
  156.6 0.7 copy-done.9
  157.3 5.8 %shard_map.156 = (bf16[4,4,2,64,128]{4,3,2,1,0:T(8,128)(2,1)}, bf16[4,64,128]{2,1,0:T(8,128)(2,1)}) custom-call(s32[6]{0:T(128)} %stack.137.info_ref, bf16[64,2048]{1,0:T(8,128)(2,1)} %bitcast.55, f32[1,2048]{1,0:T(1,128)} %bitcast.60, bf16[4,2,1024,128]{3,2,1,0:T(8,128)(2,1)} %bitcast.30.mine_ref, bf16[4,2,1024,128]{3,2,1,0:T(8,128)(2,1)} %collective-permute-done.7.theirs_ref), custom_call_target="tpu_custom_call" | custom-call | flops 268435456 | bytes 5054488 | tf_op jit(solution)/shard_map/pallas_call | solution.py:33
  163.1 9.4 %all-to-all-start.6 = ((bf16[16,2,64,128]{3,2,1,0:T(8,128)(2,1)}), bf16[16,2,64,128]{3,2,1,0:T(8,128)(2,1)S(1)}, u32[]{:S(2)}, u32[]{:S(2)}) async-start(bf16[16,2,64,128]{3,2,1,0:T(8,128)(2,1)} %bitcast.57), calls=%async_computation.6 | async-start | bytes 1048576 | tf_op jit(solution)/shard_map/all_to_all | solution.py:296
  172.5 0.6 stack.130.info_ref
  173.1 19.8 %all-to-all-done.6 = bf16[16,2,64,128]{3,2,1,0:T(8,128)(2,1)S(1)} async-done(((bf16[16,2,64,128]{3,2,1,0:T(8,128)(2,1)}), bf16[16,2,64,128]{3,2,1,0:T(8,128)(2,1)S(1)}, u32[]{:S(2)}, u32[]{:S(2)}) %all-to-all-start.6) | async-done | bytes 524320 | tf_op jit(solution)/shard_map/all_to_all | solution.py:296
  192.9 3.5 %all-to-all-start.7 = ((bf16[4,64,128]{2,1,0:T(8,128)(2,1)}), bf16[4,64,128]{2,1,0:T(8,128)(2,1)S(1)}, u32[]{:S(2)}, u32[]{:S(2)}) async-start(bf16[4,64,128]{2,1,0:T(8,128)(2,1)} %get-tuple-element.45), calls=%async_computation.7 | async-start | bytes 131072 | tf_op jit(solution)/shard_map/all_to_all | solution.py:296
  196.4 9.1 %shard_map.157 = bf16[8,1,528,128]{3,2,1,0:T(8,128)(2,1)} custom-call(s32[17]{0:T(128)} %stack.130.info_ref, bf16[8,512,128]{2,1,0:T(8,128)(2,1)} %bitcast.61, bf16[4,4,2,64,128]{4,3,2,1,0:T(8,128)(2,1)} %bitcast.56), custom_call_target="tpu_custom_call" | custom-call | flops 4294967296 | bytes 2654276 | tf_op jit(solution)/shard_map/pallas_call | solution.py:33
  205.5 6.0 %all-to-all-start.8 = ((bf16[8,528,128]{2,1,0:T(8,128)(2,1)}), bf16[8,528,128]{2,1,0:T(8,128)(2,1)S(1)}, u32[]{:S(2)}, u32[]{:S(2)}) async-start(bf16[8,528,128]{2,1,0:T(8,128)(2,1)} %bitcast.54), calls=%async_computation.8 | async-start | bytes 2162688 | tf_op jit(solution)/shard_map/all_to_all | solution.py:296
  212.2 0.1 pad_add_fusion.info_ref
  212.3 11.5 %all-to-all-done.8.r_ref = bf16[8,528,128]{2,1,0:T(8,128)(2,1)S(1)} async-done(((bf16[8,528,128]{2,1,0:T(8,128)(2,1)}), bf16[8,528,128]{2,1,0:T(8,128)(2,1)S(1)}, u32[]{:S(2)}, u32[]{:S(2)}) %all-to-all-start.8) | async-done | bytes 1081376 | tf_op jit(solution)/shard_map/all_to_all | solution.py:296
  223.8 1.9 shard_map.158
  225.7 0.6 copy.19
  (35 shorter events, 0.2 us)
Async XLA Ops:
  7.2 57.6 %all-gather.7.cloned.1.call-start = ((), (), s32[]{:S(2)}) async-start(), calls=%async_computation.9 | async-start | bytes 2621440 | tf_op jit(solution)/shard_map/all_gather | solution.py:360
  9.2 52.6 %copy-start.5 = (f32[2048]{0:T(1024)S(1)}, f32[2048]{0:T(1024)}, u32[]{:S(2)}) copy-start(f32[2048]{0:T(1024)} %param.18) | copy-start | bytes 24580
  9.2 139.3 %all-gather.9.cloned.1.call-start = ((), (), s32[]{:S(2)}) async-start(), calls=%async_computation.10 | async-start | bytes 2228224 | tf_op jit(solution)/shard_map/all_gather | solution.py:384
  10.8 50.9 %copy-start.1 = (bf16[2048,128]{1,0:T(8,128)(2,1)S(1)}, bf16[2048,128]{1,0:T(8,128)(2,1)}, u32[]{:S(2)}) copy-start(bf16[2048,128]{1,0:T(8,128)(2,1)} %wq_ref.2) | copy-start | bytes 1572868
  10.8 50.9 %copy-start.2 = (bf16[2048,128]{1,0:T(8,128)(2,1)S(1)}, bf16[2048,128]{1,0:T(8,128)(2,1)}, u32[]{:S(2)}) copy-start(bf16[2048,128]{1,0:T(8,128)(2,1)} %wk_ref.1) | copy-start | bytes 1572868
  10.8 50.9 %copy-start.3 = (bf16[2048,128]{1,0:T(8,128)(2,1)S(1)}, bf16[2048,128]{1,0:T(8,128)(2,1)}, u32[]{:S(2)}) copy-start(bf16[2048,128]{1,0:T(8,128)(2,1)} %wv_ref.1) | copy-start | bytes 1572868
  64.8 18.1 %all-to-all-start.2 = ((bf16[8,256,128]{2,1,0:T(8,128)(2,1)}), bf16[8,256,128]{2,1,0:T(8,128)(2,1)S(1)}, u32[]{:S(2)}, u32[]{:S(2)}) async-start(bf16[8,256,128]{2,1,0:T(8,128)(2,1)} %get-tuple-element.26), calls=%async_computation.2 | async-start | bytes 1048576 | tf_op jit(solution)/shard_map/all_to_all | solution.py:296
  70.5 19.2 %collective-permute-start.2 = (bf16[2,256,128]{2,1,0:T(8,128)(2,1)S(1)}, bf16[2,256,128]{2,1,0:T(8,128)(2,1)S(1)}, u32[]{:S(2)}, u32[]{:S(2)}) collective-permute-start(bf16[2,256,128]{2,1,0:T(8,128)(2,1)S(1)} %get-tuple-element.28.refs_0_), channel_id=1, source_target_pairs={{0,192},{64,128},{128,64},{192,0},{1,193},{65,129},{129,65},{193,1... | collective-permute-start | bytes 393224 | tf_op jit(solution)/shard_map/ppermute | solution.py:318
  75.4 17.0 %collective-permute-start.1 = (bf16[2,256,128]{2,1,0:T(8,128)(2,1)S(1)}, bf16[2,256,128]{2,1,0:T(8,128)(2,1)S(1)}, u32[]{:S(2)}, u32[]{:S(2)}) collective-permute-start(bf16[2,256,128]{2,1,0:T(8,128)(2,1)S(1)} %get-tuple-element.28.refs_0_), channel_id=1, source_target_pairs={{0,128},{64,192},{128,0},{192,64},{1,129},{65,193},{129,1},{193,65... | collective-permute-start | bytes 393224 | tf_op jit(solution)/shard_map/ppermute | solution.py:318
  79.7 15.2 %collective-permute-start = (bf16[2,256,128]{2,1,0:T(8,128)(2,1)S(1)}, bf16[2,256,128]{2,1,0:T(8,128)(2,1)S(1)}, u32[]{:S(2)}, u32[]{:S(2)}) collective-permute-start(bf16[2,256,128]{2,1,0:T(8,128)(2,1)S(1)} %get-tuple-element.28.refs_0_), channel_id=1, source_target_pairs={{0,64},{64,0},{128,192},{192,128},{1,65},{65,1},{129,193},{193,129... | collective-permute-start | bytes 393224 | tf_op jit(solution)/shard_map/ppermute | solution.py:318
  82.9 16.4 %collective-permute-start.5 = (bf16[128,1024]{1,0:T(8,128)(2,1)S(1)}, bf16[128,1024]{1,0:T(8,128)(2,1)S(1)}, u32[]{:S(2)}, u32[]{:S(2)}) collective-permute-start(bf16[128,1024]{1,0:T(8,128)(2,1)S(1)} %constant_dynamic-slice_fusion.1), channel_id=1, source_target_pairs={{0,2},{1,3},{2,0},{3,1},{4,6},{5,7},{6,4},{7,5},{8,10},{9,11},{10,... | collective-permute-start | bytes 786440 | tf_op jit(solution)/shard_map/ppermute | solution.py:318
  85.6 15.9 %collective-permute-start.4 = (bf16[128,1024]{1,0:T(8,128)(2,1)S(1)}, bf16[128,1024]{1,0:T(8,128)(2,1)}, u32[]{:S(2)}, u32[]{:S(2)}) collective-permute-start(bf16[128,1024]{1,0:T(8,128)(2,1)S(1)} %constant_dynamic-slice_fusion.1), channel_id=1, source_target_pairs={{0,3},{1,2},{2,1},{3,0},{4,7},{5,6},{6,5},{7,4},{8,11},{9,10},{10,... | collective-permute-start | bytes 786440 | tf_op jit(solution)/shard_map/ppermute | solution.py:318
  89.7 11.8 %collective-permute-start.3 = (bf16[128,1024]{1,0:T(8,128)(2,1)S(1)}, bf16[128,1024]{1,0:T(8,128)(2,1)}, u32[]{:S(2)}, u32[]{:S(2)}) collective-permute-start(bf16[128,1024]{1,0:T(8,128)(2,1)S(1)} %constant_dynamic-slice_fusion.1), channel_id=1, source_target_pairs={{0,1},{1,0},{2,3},{3,2},{4,5},{5,4},{6,7},{7,6},{8,9},{9,8},{10,11... | collective-permute-start | bytes 786440 | tf_op jit(solution)/shard_map/ppermute | solution.py:318
  101.5 42.5 %collective-permute-start.7 = (bf16[4,2,1024,128]{3,2,1,0:T(8,128)(2,1)}, bf16[4,2,1024,128]{3,2,1,0:T(8,128)(2,1)}, u32[]{:S(2)}, u32[]{:S(2)}) collective-permute-start(bf16[4,2,1024,128]{3,2,1,0:T(8,128)(2,1)} %bitcast.30.mine_ref), channel_id=1, source_target_pairs={{0,16},{16,0},{1,17},{17,1},{2,18},{18,2},{3,19},{19,3},{4,20},{20... | collective-permute-start | bytes 6291464 | tf_op jit(solution)/shard_map/ppermute | solution.py:318
  103.9 21.7 %all-to-all-start.3 = ((bf16[32,80,128]{2,1,0:T(8,128)(2,1)}), bf16[32,80,128]{2,1,0:T(8,128)(2,1)S(1)}, u32[]{:S(2)}, u32[]{:S(2)}) async-start(bf16[32,80,128]{2,1,0:T(8,128)(2,1)} %bitcast.31), calls=%async_computation.3 | async-start | bytes 1310720 | tf_op jit(solution)/shard_map/all_to_all | solution.py:296
  110.2 15.4 %copy-start.7 = (bf16[3,128,1024]{2,1,0:T(8,128)(2,1)}, bf16[3,128,1024]{2,1,0:T(8,128)(2,1)S(1)}, u32[]{:S(2)}) copy-start(bf16[3,128,1024]{2,1,0:T(8,128)(2,1)S(1)} %pad_maximum_fusion.mine_ref) | copy-start | bytes 2359300
  110.2 4.3 %collective-permute-start.6 = (bf16[3,128,1024]{2,1,0:T(8,128)(2,1)S(1)}, bf16[3,128,1024]{2,1,0:T(8,128)(2,1)}, u32[]{:S(2)}, u32[]{:S(2)}) collective-permute-start(bf16[3,128,1024]{2,1,0:T(8,128)(2,1)S(1)} %pad_maximum_fusion.mine_ref), channel_id=1, source_target_pairs={{0,16},{16,0},{1,17},{17,1},{2,18},{18,2},{3,19},{19,3},{4,20},{20... | collective-permute-start | bytes 2359304 | tf_op jit(solution)/shard_map/ppermute | solution.py:318
  125.6 0.9 copy-start.8
  126.5 22.0 %copy-start.6 = (f32[2048]{0:T(1024)S(1)}, f32[2048]{0:T(1024)}, u32[]{:S(2)}) copy-start(f32[2048]{0:T(1024)} %param.27) | copy-start | bytes 24580
  130.4 18.1 %copy-start.4 = (bf16[2048,128]{1,0:T(8,128)(2,1)S(1)}, bf16[2048,128]{1,0:T(8,128)(2,1)}, u32[]{:S(2)}) copy-start(bf16[2048,128]{1,0:T(8,128)(2,1)} %wq_ref.3) | copy-start | bytes 1572868
  130.4 13.6 %all-to-all-start.4 = ((bf16[4,16,2048]{2,1,0:T(8,128)(2,1)}), bf16[4,16,2048]{2,1,0:T(8,128)(2,1)S(1)}, u32[]{:S(2)}, u32[]{:S(2)}) async-start(bf16[4,16,2048]{2,1,0:T(8,128)(2,1)} %shard_map.153), calls=%async_computation.4 | async-start | bytes 524288 | tf_op jit(solution)/shard_map/all_to_all | solution.py:296
  144.8 11.8 %all-to-all-start.5 = ((bf16[4,16,2048]{2,1,0:T(8,128)(2,1)}), bf16[4,16,2048]{2,1,0:T(8,128)(2,1)S(1)}, u32[]{:S(2)}, u32[]{:S(2)}) async-start(bf16[4,16,2048]{2,1,0:T(8,128)(2,1)} %shard_map.154), calls=%async_computation.5 | async-start | bytes 524288 | tf_op jit(solution)/shard_map/all_to_all | solution.py:296
  148.5 47.9 %all-gather.11.cloned.1.call-start = ((), (), s32[]{:S(2)}) async-start(), calls=%async_computation.11 | async-start | bytes 1179648 | tf_op jit(solution)/shard_map/all_gather | solution.py:454
  148.5 1.6 copy-start
  156.6 0.7 copy-start.9
  163.1 29.9 %all-to-all-start.6 = ((bf16[16,2,64,128]{3,2,1,0:T(8,128)(2,1)}), bf16[16,2,64,128]{3,2,1,0:T(8,128)(2,1)S(1)}, u32[]{:S(2)}, u32[]{:S(2)}) async-start(bf16[16,2,64,128]{3,2,1,0:T(8,128)(2,1)} %bitcast.57), calls=%async_computation.6 | async-start | bytes 1048576 | tf_op jit(solution)/shard_map/all_to_all | solution.py:296
  192.9 3.5 %copy-start.10 = (bf16[16,2,64,128]{3,2,1,0:T(8,128)(2,1)}, bf16[16,2,64,128]{3,2,1,0:T(8,128)(2,1)S(1)}, u32[]{:S(2)}) copy-start(bf16[16,2,64,128]{3,2,1,0:T(8,128)(2,1)S(1)} %all-to-all-done.6) | copy-start | bytes 1572868
  192.9 12.6 %all-to-all-start.7 = ((bf16[4,64,128]{2,1,0:T(8,128)(2,1)}), bf16[4,64,128]{2,1,0:T(8,128)(2,1)S(1)}, u32[]{:S(2)}, u32[]{:S(2)}) async-start(bf16[4,64,128]{2,1,0:T(8,128)(2,1)} %get-tuple-element.45), calls=%async_computation.7 | async-start | bytes 131072 | tf_op jit(solution)/shard_map/all_to_all | solution.py:296
  205.5 18.3 %all-to-all-start.8 = ((bf16[8,528,128]{2,1,0:T(8,128)(2,1)}), bf16[8,528,128]{2,1,0:T(8,128)(2,1)S(1)}, u32[]{:S(2)}, u32[]{:S(2)}) async-start(bf16[8,528,128]{2,1,0:T(8,128)(2,1)} %bitcast.54), calls=%async_computation.8 | async-start | bytes 2162688 | tf_op jit(solution)/shard_map/all_to_all | solution.py:296
Sparse Core Ops, SparseCore 0:
  10.1 52.2 all-gather.6
  65.4 73.5 all-gather.8
  156.7 33.4 all-gather.10

commit v4 on v2

--- a/solution.py
+++ b/solution.py
@@ -91,17 +91,17 @@
     lax.fori_loop(0, rows // step, body, 0)
 
 
-def qkv_kernel(x_ref, gain_ref, wq_ref, wk_ref, wv_ref, q_ref, kv_ref, norm_ref, w_ref, q_one_ref, in_sems, out_sems):
+def qkv_kernel(x_ref, gain_ref, wq_ref, wk_ref, wv_ref, q_ref, kv_ref, norm_ref, w_ref, kv_one_ref, in_sems, out_sems):
     weights = started(
         [(w, w_ref.at[:, i * 128 : (i + 1) * 128]) for i, w in enumerate((wq_ref, wk_ref, wv_ref))], in_sems
     )
     norm_gathered(x_ref, gain_ref, norm_ref)
     wait_for(weights)
     out = jnp.dot(norm_ref[...], w_ref[...], preferred_element_type=F32)
-    q_one_ref[...] = (out[:, :128] * SCORE_SCALE).astype(BF16)
-    copies = started([(q_one_ref, q_ref.at[a]) for a in range(q_ref.shape[0])], out_sems)
-    kv_ref[0] = out[:, 128:256].astype(BF16)
-    kv_ref[1] = out[:, 256:].astype(BF16)
+    kv_one_ref[0] = out[:, 128:256].astype(BF16)
+    kv_one_ref[1] = out[:, 256:].astype(BF16)
+    copies = started([(kv_one_ref, kv_ref.at[b]) for b in range(kv_ref.shape[0])], out_sems)
+    q_ref[...] = (out[:, :128] * SCORE_SCALE).astype(BF16)
     wait_for(copies)
 
 
@@ -121,9 +121,12 @@
     q_ref[...] = (out * SCORE_SCALE).astype(BF16)
 
 
-def attend_kernel(part, blocks, fetched, info_ref, q_ref, *refs):
+def attend_kernel(part, blocks, fetched, split, info_ref, *refs):
+    q_refs, refs = refs[:split], refs[split:]
+    q_ref = q_refs[0]
     kv_refs, (out_ref, ka_ref, va_ref, *q_scratch) = refs[: len(refs) - 3 - fetched * 2], refs[len(refs) - 3 - fetched * 2 :]
-    members, rows, _ = q_ref.shape
+    rows = q_ref.shape[-2]
+    members = split if split > 1 else q_ref.shape[0]
     q_vmem, q_copy = q_ref, []
     if fetched:
         q_vmem, q_sem = q_scratch
@@ -146,7 +149,7 @@
     eye = lax.broadcasted_iota(jnp.int32, (group, 128), 0) == lax.broadcasted_iota(jnp.int32, (group, 128), 1)
     block = 256
     each = rows // block
-    unroll = 8
+    unroll = min(8, members * each)
 
     wait_for(q_copy)
 
@@ -154,7 +157,12 @@
         for u in range(unroll):
             step = i * unroll + u
             a, r = (step, 0) if each == 1 else (step // each, (u % each) * block)
-            q = jnp.concatenate([q_vmem[a, pl.ds(r, block), :], ones], axis=1)
+            if split > 1:
+                q = q_refs[u // each][r : r + block, :]
+                a = info_ref[1 + len(blocks) + u // each]
+            else:
+                q = q_vmem[a, pl.ds(r, block), :]
+            q = jnp.concatenate([q, ones], axis=1)
             scores = lax.dot_general(q, ka_ref[...], (((1,), (1,)), ((), ())), preferred_element_type=F32)
             top = jnp.max(scores, axis=1, keepdims=True)
             weights = jnp.exp2(scores - top).astype(BF16)
@@ -288,18 +296,20 @@
     return lax.all_to_all(x, axes, 0, 0, tiled=True)
 
 
-def attend(q, kvs, blocks, info, part, fetched):
-    members, rows, _ = q.shape
+def attend(qs, kvs, blocks, info, part, fetched):
+    split = len(qs)
+    rows = qs[0].shape[-2]
+    members = split if split > 1 else qs[0].shape[0]
     keys = len(blocks) * kvs[0].shape[-2]
     return call(
-        functools.partial(attend_kernel, part, blocks, fetched),
+        functools.partial(attend_kernel, part, blocks, fetched, split),
         shape(members, rows // part, part + 16, 128),
         info,
-        q,
+        *qs,
         *kvs,
-        specs=[SMEM, ANY if fetched else VMEM] + [VMEM] * len(kvs),
+        specs=[SMEM] + [ANY if fetched else VMEM] * split + [VMEM] * len(kvs),
         scratch=[pltpu.VMEM((keys, 256), BF16), pltpu.VMEM((keys, 256), BF16)]
-        + ([pltpu.VMEM(q.shape, BF16), DMA((1,))] if fetched else []),
+        + ([pltpu.VMEM(qs[0].shape, BF16), DMA((1,))] if fetched else []),
         limit=62 if fetched else 48,
         flops=4 * members * rows * keys * 256,
         transcendentals=members * rows * keys,
@@ -340,7 +350,11 @@
     def first_of(yh):
         return (((at["zl"] * 4 + yh) * 2 + at["yl"]) * 2 + at["c"]) * rows
 
-    key_info = jnp.stack([source_length[0]] + [first_of(at["yh"] ^ k) for k in range(4)])
+    key_info = jnp.stack(
+        [source_length[0]]
+        + [(((k // 4 * 4 + at["yh"]) * 2 + k // 2 % 2) * 2 + k % 2) * rows for k in range(8)]
+        + [at["yh"] ^ k for k in range(4)]
+    )
     memory_info = jnp.stack(
         [source_length[0]] + [first_of(k // 4) + (k % 4) * quarter for k in range(16)]
     )
@@ -360,30 +374,30 @@
 
     queries, keys_values = call(
         qkv_kernel,
-        (shape(8, rows, 128), shape(2, rows, 128)),
+        (shape(rows, 128), shape(8, 2, rows, 128)),
         source_full,
         gains[0],
         query_weight,
         key_weight,
         value_weight,
         specs=[VMEM, VMEM, ANY, ANY, ANY],
-        out=(HBM, VMEM),
+        out=(VMEM, HBM),
         scratch=[
             pltpu.VMEM((rows, D), BF16),
             pltpu.VMEM((D, 384), BF16),
-            pltpu.VMEM((rows, 128), BF16),
+            pltpu.VMEM((2, rows, 128), BF16),
             DMA((3,)),
             DMA((8,)),
         ],
         flops=2 * rows * D * 384,
     )
-    key_sets = [keys_values] + [swapped(keys_values, "yh", 4, k) for k in (1, 2, 3)]
-    queries = exchange(queries, QUERY_GROUP)
-    queries, out_halves[2] = together(queries, out_halves[2])
+    queries = [queries] + [swapped(queries, "yh", 4, k) for k in (1, 2, 3)]
+    keys_values = exchange(keys_values, QUERY_GROUP).reshape(8, 1, 2, rows, 128)
+    keys_values, out_halves[2] = together(keys_values, out_halves[2])
     out_mine = jnp.stack(out_halves)
     out_theirs = swapped(out_mine, "c", 2, 1)
-    partial = attend(queries, key_sets, [(k, ()) for k in range(4)], key_info, quarter, False)
-    partial = exchange(partial.reshape(32, rows // 4 + 16, 128), QUERY_GROUP + ("x",))
+    partial = attend(queries, [keys_values], [(0, (k, 0)) for k in range(8)], key_info, quarter, False)
+    partial = exchange(partial.reshape(16, rows // 4 + 16, 128), ("yh", "x"))
     target_queries = call(
         target_kernel,
         shape(target_rows, 128),
@@ -405,7 +419,7 @@
         project_out_kernel,
         shape(4, quarter // 4, D),
         core_info,
-        partial.reshape(8, 4, quarter + 16, 128),
+        partial.reshape(4, 4, quarter + 16, 128),
         output_weight,
         out_mine,
         out_theirs,
@@ -447,7 +461,7 @@
     target_queries = lax.all_gather(target_queries, QUERY_GROUP, axis=0)
     memory = exchange(memory.reshape(16, 2, quarter, 128), ("yh", "x")).reshape(4, 4, 2, quarter, 128)
     crossed = attend(
-        target_queries, [memory], [(0, (k // 4, k % 4)) for k in range(16)], memory_info, target_rows, True
+        [target_queries], [memory], [(0, (k // 4, k % 4)) for k in range(16)], memory_info, target_rows, True
     )
     crossed, encoder_full = together(crossed, encoder_full)
     crossed = exchange(crossed.reshape(8, target_rows + 16, 128), QUERY_GROUP)

time: 218 us -> 224 us (1.028)
    all_to_all x5, waiting for transfers between devices: 24 us -> 37.4 us  [exchange(): return lax.all_to_all(x, axes, 0, 0, tiled=True)]
    ppermute x8, waiting for transfers between devices: 22.7 us -> 13.4 us  [swapped(): return lax.ppermute(x, axis, [(i, i ^ by) for i in range(size)])]
    all_gather x1, waiting for transfers between devices: 5.85 us -> 1.86 us  [shards(): encoder_full = lax.all_gather(encoder_rows, 'x', axis=0, tiled=True)]
  transfers between devices with their start and end apart: 17 -> 17, of which waited for: 9 -> 8; matrix products, arithmetic and copies ran while one was open for 3% -> 4% of each run, Pallas kernels for 15% -> 15%
where the time goes in v4:
time: 224 us; the launch traced here: 221 us
  starting transfers between devices  76.3 us (34%)
  waiting for transfers between devices  54.6 us (24%)
  Pallas kernels  34.5 us (15%)
  blocking collectives  26.5 us (12%)
  between operations  15.4 us (7%)
  local copies, waits for them, and re-layouts  10.2 us (5%)
  other arithmetic  3.01 us (1%)
    all_to_all x5, starting transfers between devices, exchange(): return lax.all_to_all(x, axes, 0, 0, tiled=True)  47.4 us
    all_to_all x5, waiting for transfers between devices, exchange(): return lax.all_to_all(x, axes, 0, 0, tiled=True)  37.4 us
    pallas_call x9, Pallas kernels, call(): pl.pallas_call(kernel, out_shape=out_shape, in_specs=specs, out_specs=jax...  34.5 us
    ppermute x8, starting transfers between devices, swapped(): return lax.ppermute(x, axis, [(i, i ^ by) for i in range(size)])  28.8 us
    all_to_all x2, blocking collectives, exchange(): return lax.all_to_all(x, axes, 0, 0, tiled=True)  26.5 us
    ppermute x8, waiting for transfers between devices, swapped(): return lax.ppermute(x, axis, [(i, i ^ by) for i in range(size)])  13.4 us
    unnamed x20, local copies, waits for them, and re-layouts  5.19 us
  transfers between devices with their start and end apart: 17, of which 8 were waited for; matrix products, arithmetic and copies ran while one was open for 4% of the time, Pallas kernels for 15%

profile of v4, /device:TPU:1, one launch (start us, length us, event | category | flops | bytes accessed | tf_op | source)
XLA Modules:
  0.0 220.5 jit_solution(4309832799181434856)
XLA Ops:
  7.2 0.7 all-gather.10.cloned.1.call-update
  7.9 2.0 shard_map.149
  9.9 13.6 %all-to-all-start = ((bf16[16,256,128]{2,1,0:T(8,128)(2,1)}), bf16[16,256,128]{2,1,0:T(8,128)(2,1)S(1)}, u32[]{:S(2)}, u32[]{:S(2)}) async-start(bf16[16,256,128]{2,1,0:T(8,128)(2,1)} %shard_map.149), calls=%async_computation | async-start | bytes 2097152 | tf_op jit(solution)/shard_map/all_to_all | solution.py:296
  23.5 1.0 constant_dynamic-slice_fusion.2
  24.5 3.3 %collective-permute-start = (bf16[128,1024]{1,0:T(8,128)(2,1)S(1)}, bf16[128,1024]{1,0:T(8,128)(2,1)}, u32[]{:S(2)}, u32[]{:S(2)}) collective-permute-start(bf16[128,1024]{1,0:T(8,128)(2,1)S(1)} %constant_dynamic-slice_fusion.2), channel_id=1, source_target_pairs={{0,1},{1,0},{2,3},{3,2},{4,5},{5,4},{6,7},{7,6},{8,9},{9,8},{10,11... | collective-permute-start | bytes 786440 | tf_op jit(solution)/shard_map/ppermute | solution.py:320
  27.7 3.7 %collective-permute-start.1 = (bf16[128,1024]{1,0:T(8,128)(2,1)S(1)}, bf16[128,1024]{1,0:T(8,128)(2,1)}, u32[]{:S(2)}, u32[]{:S(2)}) collective-permute-start(bf16[128,1024]{1,0:T(8,128)(2,1)S(1)} %constant_dynamic-slice_fusion.2), channel_id=1, source_target_pairs={{0,3},{1,2},{2,1},{3,0},{4,7},{5,6},{6,5},{7,4},{8,11},{9,10},{10,... | collective-permute-start | bytes 786440 | tf_op jit(solution)/shard_map/ppermute | solution.py:320
  31.5 1.1 dynamic-slice_bitcast_fusion
  32.5 0.9 pad_maximum_fusion.1
  33.4 7.8 %collective-permute-done = bf16[128,1024]{1,0:T(8,128)(2,1)} collective-permute-done((bf16[128,1024]{1,0:T(8,128)(2,1)S(1)}, bf16[128,1024]{1,0:T(8,128)(2,1)}, u32[]{:S(2)}, u32[]{:S(2)}) %collective-permute-start) | collective-permute-done | bytes 262176 | tf_op jit(solution)/shard_map/ppermute | solution.py:320
  41.2 5.6 %collective-permute-done.1 = bf16[128,1024]{1,0:T(8,128)(2,1)} collective-permute-done((bf16[128,1024]{1,0:T(8,128)(2,1)S(1)}, bf16[128,1024]{1,0:T(8,128)(2,1)}, u32[]{:S(2)}, u32[]{:S(2)}) %collective-permute-start.1) | collective-permute-done | bytes 262176 | tf_op jit(solution)/shard_map/ppermute | solution.py:320
  46.9 3.6 %shard_map.150 = (bf16[256,128]{1,0:T(8,128)(2,1)S(1)}, bf16[8,2,256,128]{3,2,1,0:T(8,128)(2,1)S(1)}) custom-call(bf16[16,256,128]{2,1,0:T(8,128)(2,1)S(1)} %all-to-all-done.x_ref, f32[1,2048]{1,0:T(1,128)S(1)} %bitcast.56, bf16[2048,128]{1,0:T(8,128)(2,1)S(1)} %copy-done.2, bf16[2048,128]{1,0:T(8,128)(2,1)S(1)} %copy-done.3, bf16[2048,128]{1,0:T(8,128)(2,1)S(1)} %copy-done.4), custom_call_target="tpu_custom_call" | custom-call | flops 402653184 | bytes 3743744 | tf_op jit(solution)/shard_map/pallas_call | solution.py:33
  50.4 1.0 copy-done.1
  51.4 15.4 %all-to-all-start.1 = ((bf16[8,2,256,128]{3,2,1,0:T(8,128)(2,1)}), bf16[8,2,256,128]{3,2,1,0:T(8,128)(2,1)S(1)}, u32[]{:S(2)}, u32[]{:S(2)}) async-start(bf16[8,2,256,128]{3,2,1,0:T(8,128)(2,1)} %copy-done.1), calls=%async_computation.1 | async-start | bytes 2097152 | tf_op jit(solution)/shard_map/all_to_all | solution.py:296
  66.8 0.7 all-gather.14.cloned.1.call-update
  67.5 1.9 collective-permute-start.5
  70.1 0.1 stack.164.info_ref
  70.2 4.2 %collective-permute-start.2 = (bf16[256,128]{1,0:T(8,128)(2,1)S(1)}, bf16[256,128]{1,0:T(8,128)(2,1)S(1)}, u32[]{:S(2)}, u32[]{:S(2)}) collective-permute-start(bf16[256,128]{1,0:T(8,128)(2,1)S(1)} %get-tuple-element.19.refs_0_), channel_id=1, source_target_pairs={{0,64},{64,0},{128,192},{192,128},{1,65},{65,1},{129,193},{193,129... | collective-permute-start | bytes 196616 | tf_op jit(solution)/shard_map/ppermute | solution.py:320
  74.4 4.8 %collective-permute-start.3 = (bf16[256,128]{1,0:T(8,128)(2,1)S(1)}, bf16[256,128]{1,0:T(8,128)(2,1)S(1)}, u32[]{:S(2)}, u32[]{:S(2)}) collective-permute-start(bf16[256,128]{1,0:T(8,128)(2,1)S(1)} %get-tuple-element.19.refs_0_), channel_id=1, source_target_pairs={{0,128},{64,192},{128,0},{192,64},{1,129},{65,193},{129,1},{193,65... | collective-permute-start | bytes 196616 | tf_op jit(solution)/shard_map/ppermute | solution.py:320
  79.2 2.4 %collective-permute-start.4 = (bf16[256,128]{1,0:T(8,128)(2,1)S(1)}, bf16[256,128]{1,0:T(8,128)(2,1)S(1)}, u32[]{:S(2)}, u32[]{:S(2)}) collective-permute-start(bf16[256,128]{1,0:T(8,128)(2,1)S(1)} %get-tuple-element.19.refs_0_), channel_id=1, source_target_pairs={{0,192},{64,128},{128,64},{192,0},{1,193},{65,129},{129,65},{193,1... | collective-permute-start | bytes 196616 | tf_op jit(solution)/shard_map/ppermute | solution.py:320
  81.6 7.6 %all-to-all-done.1 = bf16[8,2,256,128]{3,2,1,0:T(8,128)(2,1)S(1)} async-done(((bf16[8,2,256,128]{3,2,1,0:T(8,128)(2,1)}), bf16[8,2,256,128]{3,2,1,0:T(8,128)(2,1)S(1)}, u32[]{:S(2)}, u32[]{:S(2)}) %all-to-all-start.1) | async-done | bytes 1048608 | tf_op jit(solution)/shard_map/all_to_all | solution.py:296
  89.3 2.1 pad_maximum_fusion.mine_ref
  91.3 3.9 %collective-permute-start.6 = (bf16[3,128,1024]{2,1,0:T(8,128)(2,1)}, bf16[3,128,1024]{2,1,0:T(8,128)(2,1)}, u32[]{:S(2)}, u32[]{:S(2)}) collective-permute-start(bf16[3,128,1024]{2,1,0:T(8,128)(2,1)} %pad_maximum_fusion.mine_ref), channel_id=1, source_target_pairs={{0,16},{16,0},{1,17},{17,1},{2,18},{18,2},{3,19},{19,3},{4,20},{20... | collective-permute-start | bytes 2359304 | tf_op jit(solution)/shard_map/ppermute | solution.py:320
  95.2 4.6 %shard_map.151 = bf16[4,4,80,128]{3,2,1,0:T(8,128)(2,1)} custom-call(s32[13]{0:T(128)S(1)} %stack.164.info_ref, bf16[256,128]{1,0:T(8,128)(2,1)S(1)} %get-tuple-element.19.refs_0_, bf16[256,128]{1,0:T(8,128)(2,1)S(1)} %collective-permute-done.2.refs_1_, bf16[256,128]{1,0:T(8,128)(2,1)S(1)} %collective-permute-done.3.refs_2_, ...), custom_call_target="tpu_custom_call" | custom-call | flops 2147483648 | bytes 1638452 | tf_op jit(solution)/shard_map/pallas_call | solution.py:33
  99.9 5.3 %all-to-all-start.2 = ((bf16[16,80,128]{2,1,0:T(8,128)(2,1)}), bf16[16,80,128]{2,1,0:T(8,128)(2,1)S(1)}, u32[]{:S(2)}, u32[]{:S(2)}) async-start(bf16[16,80,128]{2,1,0:T(8,128)(2,1)} %bitcast.32), calls=%async_computation.2 | async-start | bytes 655360 | tf_op jit(solution)/shard_map/all_to_all | solution.py:296
  105.2 0.0 all-gather.12.cloned.1.call-start
  105.3 0.7 stack.173.info_ref
  106.0 1.6 copy-done
  107.6 1.0 copy-done.5
  108.6 3.7 %shard_map.152 = bf16[512,128]{1,0:T(8,128)(2,1)} custom-call(bf16[16,512,128]{2,1,0:T(8,128)(2,1)S(1)} %bitcast.54, f32[1,2048]{1,0:T(1,128)S(1)} %bitcast.57, bf16[2048,128]{1,0:T(8,128)(2,1)S(1)} %copy-done.5), custom_call_target="tpu_custom_call" | custom-call | flops 268435456 | bytes 2760704 | tf_op jit(solution)/shard_map/pallas_call | solution.py:33
  112.3 4.5 %all-to-all-done.2 = bf16[16,80,128]{2,1,0:T(8,128)(2,1)S(1)} async-done(((bf16[16,80,128]{2,1,0:T(8,128)(2,1)}), bf16[16,80,128]{2,1,0:T(8,128)(2,1)S(1)}, u32[]{:S(2)}, u32[]{:S(2)}) %all-to-all-start.2) | async-done | bytes 327712 | tf_op jit(solution)/shard_map/all_to_all | solution.py:296
  116.8 0.7 copy-done.8
  117.5 3.8 %shard_map.153 = bf16[4,16,2048]{2,1,0:T(8,128)(2,1)} custom-call(s32[5]{0:T(128)} %stack.173.info_ref, bf16[4,4,80,128]{3,2,1,0:T(8,128)(2,1)} %bitcast.63, bf16[128,2048]{1,0:T(8,128)(2,1)} %own_ref.1, bf16[3,128,1024]{2,1,0:T(8,128)(2,1)} %pad_maximum_fusion.mine_ref, bf16[3,128,1024]{2,1,0:T(8,128)(2,1)} %collective-permute-done.6.theirs_ref), custom_call_target="tpu_custom_call" | custom-call | flops 134217728 | bytes 2686996 | tf_op jit(solution)/shard_map/pallas_call | solution.py:33
  121.3 12.4 %all_to_all.35.r_ref = bf16[4,16,2048]{2,1,0:T(8,128)(2,1)S(1)} all-to-all(bf16[4,16,2048]{2,1,0:T(8,128)(2,1)} %shard_map.153), channel_id=1, replica_groups=mesh['zl'=2,'yh'=4,'yl'=2,'c'=2,'zh'=4,'x'=4] {'zh'}, dimensions={0} | all-to-all | bytes 524288 | tf_op jit(solution)/shard_map/all_to_all | solution.py:296
  133.7 0.5 all-gather.14.cloned.1.call-done
  134.2 4.7 %collective-permute-start.7 = (bf16[4,2,1024,128]{3,2,1,0:T(8,128)(2,1)}, bf16[4,2,1024,128]{3,2,1,0:T(8,128)(2,1)}, u32[]{:S(2)}, u32[]{:S(2)}) collective-permute-start(bf16[4,2,1024,128]{3,2,1,0:T(8,128)(2,1)} %bitcast.60), channel_id=1, source_target_pairs={{0,16},{16,0},{1,17},{17,1},{2,18},{18,2},{3,19},{19,3},{4,20},{20... | collective-permute-start | bytes 6291464 | tf_op jit(solution)/shard_map/ppermute | solution.py:320
  139.0 14.2 %all_to_all.36 = bf16[4,16,2048]{2,1,0:T(8,128)(2,1)} all-to-all(bf16[4,16,2048]{2,1,0:T(8,128)(2,1)S(1)} %shard_map.154), channel_id=1, replica_groups=mesh['zl'=2,'yh'=4,'yl'=2,'c'=2,'zh'=4,'x'=4] {'zh'}, dimensions={0} | all-to-all | bytes 524288 | tf_op jit(solution)/shard_map/all_to_all | solution.py:296
  153.2 5.8 %shard_map.155 = bf16[4,4,2,64,128]{4,3,2,1,0:T(8,128)(2,1)} custom-call(s32[5]{0:T(128)} %stack.173.info_ref, bf16[64,2048]{1,0:T(8,128)(2,1)} %bitcast.59, f32[1,2048]{1,0:T(1,128)} %bitcast.67, bf16[4,2,1024,128]{3,2,1,0:T(8,128)(2,1)} %bitcast.61, bf16[4,2,1024,128]{3,2,1,0:T(8,128)(2,1)} %collective-permute-done.7.theirs_ref), custom_call_target="tpu_custom_call" | custom-call | flops 268435456 | bytes 4988948 | tf_op jit(solution)/shard_map/pallas_call | solution.py:33
  159.1 7.7 %all-to-all-start.5 = ((bf16[16,2,64,128]{3,2,1,0:T(8,128)(2,1)}), bf16[16,2,64,128]{3,2,1,0:T(8,128)(2,1)S(1)}, u32[]{:S(2)}, u32[]{:S(2)}) async-start(bf16[16,2,64,128]{3,2,1,0:T(8,128)(2,1)} %bitcast.62), calls=%async_computation.5 | async-start | bytes 1048576 | tf_op jit(solution)/shard_map/all_to_all | solution.py:296
  166.8 0.7 stack.151.info_ref
  167.5 15.2 %all-to-all-done.5 = bf16[16,2,64,128]{3,2,1,0:T(8,128)(2,1)S(1)} async-done(((bf16[16,2,64,128]{3,2,1,0:T(8,128)(2,1)}), bf16[16,2,64,128]{3,2,1,0:T(8,128)(2,1)S(1)}, u32[]{:S(2)}, u32[]{:S(2)}) %all-to-all-start.5) | async-done | bytes 524320 | tf_op jit(solution)/shard_map/all_to_all | solution.py:296
  182.7 0.8 copy-done.9
  183.5 9.1 %shard_map.156 = bf16[8,1,528,128]{3,2,1,0:T(8,128)(2,1)} custom-call(s32[17]{0:T(128)} %stack.151.info_ref, bf16[8,512,128]{2,1,0:T(8,128)(2,1)} %bitcast.68, bf16[4,4,2,64,128]{4,3,2,1,0:T(8,128)(2,1)} %bitcast.65), custom_call_target="tpu_custom_call" | custom-call | flops 4294967296 | bytes 2654276 | tf_op jit(solution)/shard_map/pallas_call | solution.py:33
  192.6 1.9 all-gather.8.cloned.1.call-done
  194.4 5.4 %all-to-all-start.6 = ((bf16[8,528,128]{2,1,0:T(8,128)(2,1)}), bf16[8,528,128]{2,1,0:T(8,128)(2,1)S(1)}, u32[]{:S(2)}, u32[]{:S(2)}) async-start(bf16[8,528,128]{2,1,0:T(8,128)(2,1)} %bitcast.64), calls=%async_computation.6 | async-start | bytes 2162688 | tf_op jit(solution)/shard_map/all_to_all | solution.py:296
  200.5 0.1 pad_add_fusion.info_ref
  200.6 1.5 constant_dynamic-slice_fusion
  202.0 10.1 %all-to-all-done.6.r_ref = bf16[8,528,128]{2,1,0:T(8,128)(2,1)S(1)} async-done(((bf16[8,528,128]{2,1,0:T(8,128)(2,1)}), bf16[8,528,128]{2,1,0:T(8,128)(2,1)S(1)}, u32[]{:S(2)}, u32[]{:S(2)}) %all-to-all-start.6) | async-done | bytes 1081376 | tf_op jit(solution)/shard_map/all_to_all | solution.py:296
  212.1 1.9 shard_map.157
  (31 shorter events, 0.2 us)
Async XLA Ops:
  7.2 98.8 %all-gather.10.cloned.1.call-start = ((), (), s32[]{:S(2)}) async-start(), calls=%async_computation.8 | async-start | bytes 2228224 | tf_op jit(solution)/shard_map/all_gather | solution.py:367
  9.9 37.0 %copy-start.2 = (bf16[2048,128]{1,0:T(8,128)(2,1)S(1)}, bf16[2048,128]{1,0:T(8,128)(2,1)}, u32[]{:S(2)}) copy-start(bf16[2048,128]{1,0:T(8,128)(2,1)} %wq_ref.2) | copy-start | bytes 1572868
  9.9 37.0 %copy-start.3 = (bf16[2048,128]{1,0:T(8,128)(2,1)S(1)}, bf16[2048,128]{1,0:T(8,128)(2,1)}, u32[]{:S(2)}) copy-start(bf16[2048,128]{1,0:T(8,128)(2,1)} %wk_ref.1) | copy-start | bytes 1572868
  9.9 37.0 %copy-start.4 = (bf16[2048,128]{1,0:T(8,128)(2,1)S(1)}, bf16[2048,128]{1,0:T(8,128)(2,1)}, u32[]{:S(2)}) copy-start(bf16[2048,128]{1,0:T(8,128)(2,1)} %wv_ref.1) | copy-start | bytes 1572868
  9.9 37.0 %copy-start.6 = (f32[2048]{0:T(1024)S(1)}, f32[2048]{0:T(1024)}, u32[]{:S(2)}) copy-start(f32[2048]{0:T(1024)} %param.18) | copy-start | bytes 24580
  9.9 36.9 %all-to-all-start = ((bf16[16,256,128]{2,1,0:T(8,128)(2,1)}), bf16[16,256,128]{2,1,0:T(8,128)(2,1)S(1)}, u32[]{:S(2)}, u32[]{:S(2)}) async-start(bf16[16,256,128]{2,1,0:T(8,128)(2,1)} %shard_map.149), calls=%async_computation | async-start | bytes 2097152 | tf_op jit(solution)/shard_map/all_to_all | solution.py:296
  24.5 16.7 %collective-permute-start = (bf16[128,1024]{1,0:T(8,128)(2,1)S(1)}, bf16[128,1024]{1,0:T(8,128)(2,1)}, u32[]{:S(2)}, u32[]{:S(2)}) collective-permute-start(bf16[128,1024]{1,0:T(8,128)(2,1)S(1)} %constant_dynamic-slice_fusion.2), channel_id=1, source_target_pairs={{0,1},{1,0},{2,3},{3,2},{4,5},{5,4},{6,7},{7,6},{8,9},{9,8},{10,11... | collective-permute-start | bytes 786440 | tf_op jit(solution)/shard_map/ppermute | solution.py:320
  27.7 19.1 %collective-permute-start.1 = (bf16[128,1024]{1,0:T(8,128)(2,1)S(1)}, bf16[128,1024]{1,0:T(8,128)(2,1)}, u32[]{:S(2)}, u32[]{:S(2)}) collective-permute-start(bf16[128,1024]{1,0:T(8,128)(2,1)S(1)} %constant_dynamic-slice_fusion.2), channel_id=1, source_target_pairs={{0,3},{1,2},{2,1},{3,0},{4,7},{5,6},{6,5},{7,4},{8,11},{9,10},{10,... | collective-permute-start | bytes 786440 | tf_op jit(solution)/shard_map/ppermute | solution.py:320
  50.4 1.0 copy-start.1
  51.4 37.8 %all-to-all-start.1 = ((bf16[8,2,256,128]{3,2,1,0:T(8,128)(2,1)}), bf16[8,2,256,128]{3,2,1,0:T(8,128)(2,1)S(1)}, u32[]{:S(2)}, u32[]{:S(2)}) async-start(bf16[8,2,256,128]{3,2,1,0:T(8,128)(2,1)} %copy-done.1), calls=%async_computation.1 | async-start | bytes 2097152 | tf_op jit(solution)/shard_map/all_to_all | solution.py:296
  66.8 67.4 %all-gather.14.cloned.1.call-start = ((), (), s32[]{:S(2)}) async-start(), calls=%async_computation.10 | async-start | bytes 2621440 | tf_op jit(solution)/shard_map/all_gather | solution.py:373
  67.5 14.1 %collective-permute-start.5 = (bf16[128,1024]{1,0:T(8,128)(2,1)}, bf16[128,1024]{1,0:T(8,128)(2,1)S(1)}, u32[]{:S(2)}, u32[]{:S(2)}) collective-permute-start(bf16[128,1024]{1,0:T(8,128)(2,1)} %collective-permute-done), channel_id=1, source_target_pairs={{0,3},{1,2},{2,1},{3,0},{4,7},{5,6},{6,5},{7,4},{8,11},{9,10},{10,... | collective-permute-start | bytes 786440 | tf_op jit(solution)/shard_map/ppermute | solution.py:320
  70.2 25.0 %collective-permute-start.2 = (bf16[256,128]{1,0:T(8,128)(2,1)S(1)}, bf16[256,128]{1,0:T(8,128)(2,1)S(1)}, u32[]{:S(2)}, u32[]{:S(2)}) collective-permute-start(bf16[256,128]{1,0:T(8,128)(2,1)S(1)} %get-tuple-element.19.refs_0_), channel_id=1, source_target_pairs={{0,64},{64,0},{128,192},{192,128},{1,65},{65,1},{129,193},{193,129... | collective-permute-start | bytes 196616 | tf_op jit(solution)/shard_map/ppermute | solution.py:320
  74.4 20.8 %collective-permute-start.3 = (bf16[256,128]{1,0:T(8,128)(2,1)S(1)}, bf16[256,128]{1,0:T(8,128)(2,1)S(1)}, u32[]{:S(2)}, u32[]{:S(2)}) collective-permute-start(bf16[256,128]{1,0:T(8,128)(2,1)S(1)} %get-tuple-element.19.refs_0_), channel_id=1, source_target_pairs={{0,128},{64,192},{128,0},{192,64},{1,129},{65,193},{129,1},{193,65... | collective-permute-start | bytes 196616 | tf_op jit(solution)/shard_map/ppermute | solution.py:320
  79.2 16.1 %collective-permute-start.4 = (bf16[256,128]{1,0:T(8,128)(2,1)S(1)}, bf16[256,128]{1,0:T(8,128)(2,1)S(1)}, u32[]{:S(2)}, u32[]{:S(2)}) collective-permute-start(bf16[256,128]{1,0:T(8,128)(2,1)S(1)} %get-tuple-element.19.refs_0_), channel_id=1, source_target_pairs={{0,192},{64,128},{128,64},{192,0},{1,193},{65,129},{129,65},{193,1... | collective-permute-start | bytes 196616 | tf_op jit(solution)/shard_map/ppermute | solution.py:320
  91.3 14.6 %copy-start.7 = (f32[2048]{0:T(1024)S(1)}, f32[2048]{0:T(1024)}, u32[]{:S(2)}) copy-start(f32[2048]{0:T(1024)} %param.27) | copy-start | bytes 24580
  91.3 25.4 %collective-permute-start.6 = (bf16[3,128,1024]{2,1,0:T(8,128)(2,1)}, bf16[3,128,1024]{2,1,0:T(8,128)(2,1)}, u32[]{:S(2)}, u32[]{:S(2)}) collective-permute-start(bf16[3,128,1024]{2,1,0:T(8,128)(2,1)} %pad_maximum_fusion.mine_ref), channel_id=1, source_target_pairs={{0,16},{16,0},{1,17},{17,1},{2,18},{18,2},{3,19},{19,3},{4,20},{20... | collective-permute-start | bytes 2359304 | tf_op jit(solution)/shard_map/ppermute | solution.py:320
  99.9 16.9 %all-to-all-start.2 = ((bf16[16,80,128]{2,1,0:T(8,128)(2,1)}), bf16[16,80,128]{2,1,0:T(8,128)(2,1)S(1)}, u32[]{:S(2)}, u32[]{:S(2)}) async-start(bf16[16,80,128]{2,1,0:T(8,128)(2,1)} %bitcast.32), calls=%async_computation.2 | async-start | bytes 655360 | tf_op jit(solution)/shard_map/all_to_all | solution.py:296
  105.2 62.2 %all-gather.12.cloned.1.call-start = ((), (), s32[]{:S(2)}) async-start(), calls=%async_computation.9 | async-start | bytes 1179648 | tf_op jit(solution)/shard_map/all_gather | solution.py:461
  106.0 1.6 copy-start
  107.6 1.0 copy-start.5
  116.8 0.7 copy-start.8
  134.2 19.1 %collective-permute-start.7 = (bf16[4,2,1024,128]{3,2,1,0:T(8,128)(2,1)}, bf16[4,2,1024,128]{3,2,1,0:T(8,128)(2,1)}, u32[]{:S(2)}, u32[]{:S(2)}) collective-permute-start(bf16[4,2,1024,128]{3,2,1,0:T(8,128)(2,1)} %bitcast.60), channel_id=1, source_target_pairs={{0,16},{16,0},{1,17},{17,1},{2,18},{18,2},{3,19},{19,3},{4,20},{20... | collective-permute-start | bytes 6291464 | tf_op jit(solution)/shard_map/ppermute | solution.py:320
  138.9 55.5 %all-gather.8.cloned.1.call-start = ((), (), s32[]{:S(2)}) async-start(), calls=%async_computation.7 | async-start | bytes 1310720 | tf_op jit(solution)/shard_map/all_gather | solution.py:459
  159.1 23.6 %all-to-all-start.5 = ((bf16[16,2,64,128]{3,2,1,0:T(8,128)(2,1)}), bf16[16,2,64,128]{3,2,1,0:T(8,128)(2,1)S(1)}, u32[]{:S(2)}, u32[]{:S(2)}) async-start(bf16[16,2,64,128]{3,2,1,0:T(8,128)(2,1)} %bitcast.62), calls=%async_computation.5 | async-start | bytes 1048576 | tf_op jit(solution)/shard_map/all_to_all | solution.py:296
  182.7 0.8 copy-start.9
  194.4 17.7 %all-to-all-start.6 = ((bf16[8,528,128]{2,1,0:T(8,128)(2,1)}), bf16[8,528,128]{2,1,0:T(8,128)(2,1)S(1)}, u32[]{:S(2)}, u32[]{:S(2)}) async-start(bf16[8,528,128]{2,1,0:T(8,128)(2,1)} %bitcast.64), calls=%async_computation.6 | async-start | bytes 2162688 | tf_op jit(solution)/shard_map/all_to_all | solution.py:296
Sparse Core Ops, SparseCore 0:
  11.0 87.5 all-gather.9
  100.7 33.4 all-gather.13
  139.0 25.6 all-gather.11
  166.7 27.6 all-gather.7

commit v5 on v2

--- a/solution.py
+++ b/solution.py
@@ -122,12 +122,13 @@
 
 
 def attend_kernel(part, blocks, fetched, info_ref, q_ref, *refs):
-    kv_refs, (out_ref, ka_ref, va_ref, *q_scratch) = refs[: len(refs) - 3 - fetched * 2], refs[len(refs) - 3 - fetched * 2 :]
+    kv_refs, (out_ref, ka_ref, va_ref, *q_scratch) = refs[: len(refs) - 3 - fetched * 4], refs[len(refs) - 3 - fetched * 4 :]
     members, rows, _ = q_ref.shape
     q_vmem, q_copy = q_ref, []
     if fetched:
-        q_vmem, q_sem = q_scratch
-        q_copy = started([(q_ref, q_vmem)], q_sem)
+        q_vmem, out_vmem, q_sem, out_sem = q_scratch
+        q_copy = started([(q_ref.at[a], q_vmem.at[a]) for a in range(members)], q_sem)
+        out_ref, out_hbm = out_vmem, out_ref
     limit = info_ref[0]
     n = kv_refs[0].shape[-2]
     lane = lax.broadcasted_iota(jnp.int32, (n, 128), 1)
@@ -148,8 +149,6 @@
     each = rows // block
     unroll = 8
 
-    wait_for(q_copy)
-
     def body(i, _):
         for u in range(unroll):
             step = i * unroll + u
@@ -170,7 +169,18 @@
                 stat_ref_store(out_ref, a, p, part, inside // group, groups, line)
         return 0
 
-    lax.fori_loop(0, members * each // unroll, body, 0)
+    if not fetched:
+        lax.fori_loop(0, members * each // unroll, body, 0)
+        return
+    out_copies = []
+    for i in range(members * each // unroll):
+        done = range(i * unroll // each, (i + 1) * unroll // each)
+        wait_for([q_copy[a] for a in done])
+        body(i, 0)
+        out_copies += [pltpu.make_async_copy(out_ref.at[a], out_hbm.at[a], out_sem.at[a]) for a in done]
+        for copy in out_copies[-len(done) :]:
+            copy.start()
+    wait_for(out_copies)
 
 
 def stat_ref_store(out_ref, a, p, part, g, groups, line):
@@ -299,7 +309,17 @@
         *kvs,
         specs=[SMEM, ANY if fetched else VMEM] + [VMEM] * len(kvs),
         scratch=[pltpu.VMEM((keys, 256), BF16), pltpu.VMEM((keys, 256), BF16)]
-        + ([pltpu.VMEM(q.shape, BF16), DMA((1,))] if fetched else []),
+        + (
+            [
+                pltpu.VMEM(q.shape, BF16),
+                pltpu.VMEM((members, rows // part, part + 16, 128), BF16),
+                DMA((members,)),
+                DMA((members,)),
+            ]
+            if fetched
+            else []
+        ),
+        out=HBM if fetched else None,
         limit=62 if fetched else 48,
         flops=4 * members * rows * keys * 256,
         transcendentals=members * rows * keys,
@@ -348,12 +368,8 @@
     gains = [g.reshape(1, D) for g in (encoder_gain, final_gain, cross_gain)]
 
     half = at["c"] * (D // 2)
-    out_half = lax.dynamic_slice_in_dim(output_weight, half, D // 2, 1)
-    out_halves = [swapped(out_half, "x", 4, k) for k in (1, 3)]
     target_full = lax.all_gather(target_hidden, HEAD, axis=0)
     source_full = exchange(repeated(source_hidden, 16), HEAD)
-    source_full, *out_halves = together(source_full, *out_halves)
-    out_halves.append(swapped(out_halves[0], "x", 4, 3))
     half_weights = jnp.stack([lax.dynamic_slice_in_dim(w, half, D // 2, 0) for w in (cross_key, cross_value)])
     source_full, half_weights = together(source_full, half_weights)
     mine = lax.all_gather(half_weights, "x", axis=0)
@@ -379,10 +395,13 @@
     )
     key_sets = [keys_values] + [swapped(keys_values, "yh", 4, k) for k in (1, 2, 3)]
     queries = exchange(queries, QUERY_GROUP)
-    queries, out_halves[2] = together(queries, out_halves[2])
+    out_half = lax.dynamic_slice_in_dim(output_weight, half, D // 2, 1)
+    queries, out_half = together(queries, out_half)
+    out_halves = [swapped(out_half, "x", 4, k) for k in (1, 3, 2)]
+    partial = attend(queries, key_sets, [(k, ()) for k in range(4)], key_info, quarter, False)
+    partial, *out_halves = together(partial, *out_halves)
     out_mine = jnp.stack(out_halves)
     out_theirs = swapped(out_mine, "c", 2, 1)
-    partial = attend(queries, key_sets, [(k, ()) for k in range(4)], key_info, quarter, False)
     partial = exchange(partial.reshape(32, rows // 4 + 16, 128), QUERY_GROUP + ("x",))
     target_queries = call(
         target_kernel,

time: 218 us -> 224 us (1.028)
  waiting for transfers between devices: 53.3 us -> 60.9 us
    all_to_all x5, waiting for transfers between devices: 24 us -> 49.4 us  [exchange(): return lax.all_to_all(x, axes, 0, 0, tiled=True)]
    ppermute x8, waiting for transfers between devices: 22.7 us -> 7.9 us  [swapped(): return lax.ppermute(x, axis, [(i, i ^ by) for i in range(size)])]
    all_gather x1, waiting for transfers between devices: 5.85 us -> 2.02 us  [shards(): encoder_full = lax.all_gather(encoder_rows, 'x', axis=0, tiled=True)]
  transfers between devices with their start and end apart: 17 -> 17, of which waited for: 9 -> 8; matrix products, arithmetic and copies ran while one was open for 3% -> 3% of each run, Pallas kernels for 15% -> 14%
where the time goes in v5:
time: 224 us; the launch traced here: 221 us
  starting transfers between devices  74.3 us (33%)
  waiting for transfers between devices  60.9 us (27%)
  Pallas kernels  33.5 us (15%)
  blocking collectives  26.8 us (12%)
  between operations  15.4 us (7%)
  local copies, waits for them, and re-layouts  8.1 us (4%)
    all_to_all x5, waiting for transfers between devices, exchange(): return lax.all_to_all(x, axes, 0, 0, tiled=True)  49.4 us
    all_to_all x5, starting transfers between devices, exchange(): return lax.all_to_all(x, axes, 0, 0, tiled=True)  47.4 us
    pallas_call x9, Pallas kernels, call(): pl.pallas_call(kernel, out_shape=out_shape, in_specs=specs, out_specs=jax...  33.5 us
    all_to_all x2, blocking collectives, exchange(): return lax.all_to_all(x, axes, 0, 0, tiled=True)  26.8 us
    ppermute x8, starting transfers between devices, swapped(): return lax.ppermute(x, axis, [(i, i ^ by) for i in range(size)])  26.8 us
    ppermute x8, waiting for transfers between devices, swapped(): return lax.ppermute(x, axis, [(i, i ^ by) for i in range(size)])  7.9 us
  transfers between devices with their start and end apart: 17, of which 8 were waited for; matrix products, arithmetic and copies ran while one was open for 3% of the time, Pallas kernels for 14%

profile of v5, /device:TPU:1, one launch (start us, length us, event | category | flops | bytes accessed | tf_op | source)
XLA Modules:
  0.0 221.1 jit_solution(8691913571980131234)
XLA Ops:
  7.2 0.0 all-gather.10.cloned.1.call-start
  7.2 0.7 all-gather.10.cloned.1.call-update
  7.9 2.0 shard_map.149
  9.9 13.6 %all-to-all-start = ((bf16[16,256,128]{2,1,0:T(8,128)(2,1)}), bf16[16,256,128]{2,1,0:T(8,128)(2,1)S(1)}, u32[]{:S(2)}, u32[]{:S(2)}) async-start(bf16[16,256,128]{2,1,0:T(8,128)(2,1)} %shard_map.149), calls=%async_computation | async-start | bytes 2097152 | tf_op jit(solution)/shard_map/all_to_all | solution.py:298
  23.5 0.0 all-gather.14.cloned.1.call-start
  23.5 1.1 dynamic-slice_bitcast_fusion
  24.6 0.8 pad_maximum_fusion.1
  25.5 21.3 %all-to-all-done.x_ref = bf16[16,256,128]{2,1,0:T(8,128)(2,1)S(1)} async-done(((bf16[16,256,128]{2,1,0:T(8,128)(2,1)}), bf16[16,256,128]{2,1,0:T(8,128)(2,1)S(1)}, u32[]{:S(2)}, u32[]{:S(2)}) %all-to-all-start) | async-done | bytes 1048608 | tf_op jit(solution)/shard_map/all_to_all | solution.py:298
  46.8 2.9 %shard_map.150 = (bf16[8,256,128]{2,1,0:T(8,128)(2,1)S(1)}, bf16[2,256,128]{2,1,0:T(8,128)(2,1)S(1)}) custom-call(bf16[16,256,128]{2,1,0:T(8,128)(2,1)S(1)} %all-to-all-done.x_ref, f32[1,2048]{1,0:T(1,128)S(1)} %bitcast.46, bf16[2048,128]{1,0:T(8,128)(2,1)S(1)} %copy-done.1, bf16[2048,128]{1,0:T(8,128)(2,1)S(1)} %copy-done.2, bf16[2048,128]{1,0:T(8,128)(2,1)S(1)} %copy-done.3), custom_call_target="tpu_custom_call" | custom-call | flops 402653184 | bytes 3284992 | tf_op jit(solution)/shard_map/pallas_call | solution.py:33
  49.7 0.8 copy-done.4
  50.5 15.4 %all-to-all-start.1 = ((bf16[8,256,128]{2,1,0:T(8,128)(2,1)}), bf16[8,256,128]{2,1,0:T(8,128)(2,1)S(1)}, u32[]{:S(2)}, u32[]{:S(2)}) async-start(bf16[8,256,128]{2,1,0:T(8,128)(2,1)} %copy-done.4), calls=%async_computation.1 | async-start | bytes 1048576 | tf_op jit(solution)/shard_map/all_to_all | solution.py:298
  66.0 4.2 %collective-permute-start = (bf16[2,256,128]{2,1,0:T(8,128)(2,1)S(1)}, bf16[2,256,128]{2,1,0:T(8,128)(2,1)S(1)}, u32[]{:S(2)}, u32[]{:S(2)}) collective-permute-start(bf16[2,256,128]{2,1,0:T(8,128)(2,1)S(1)} %get-tuple-element.21.refs_0_), channel_id=1, source_target_pairs={{0,64},{64,0},{128,192},{192,128},{1,65},{65,1},{129,193},{193,129... | collective-permute-start | bytes 393224 | tf_op jit(solution)/shard_map/ppermute | solution.py:330
  70.1 4.7 %collective-permute-start.1 = (bf16[2,256,128]{2,1,0:T(8,128)(2,1)S(1)}, bf16[2,256,128]{2,1,0:T(8,128)(2,1)S(1)}, u32[]{:S(2)}, u32[]{:S(2)}) collective-permute-start(bf16[2,256,128]{2,1,0:T(8,128)(2,1)S(1)} %get-tuple-element.21.refs_0_), channel_id=1, source_target_pairs={{0,128},{64,192},{128,0},{192,64},{1,129},{65,193},{129,1},{193,65... | collective-permute-start | bytes 393224 | tf_op jit(solution)/shard_map/ppermute | solution.py:330
  74.9 2.5 %collective-permute-start.2 = (bf16[2,256,128]{2,1,0:T(8,128)(2,1)S(1)}, bf16[2,256,128]{2,1,0:T(8,128)(2,1)S(1)}, u32[]{:S(2)}, u32[]{:S(2)}) collective-permute-start(bf16[2,256,128]{2,1,0:T(8,128)(2,1)S(1)} %get-tuple-element.21.refs_0_), channel_id=1, source_target_pairs={{0,192},{64,128},{128,64},{192,0},{1,193},{65,129},{129,65},{193,1... | collective-permute-start | bytes 393224 | tf_op jit(solution)/shard_map/ppermute | solution.py:330
  77.3 1.0 constant_dynamic-slice_fusion.2
  78.3 2.2 collective-permute-start.3
  80.6 1.9 collective-permute-start.4
  82.5 4.8 %collective-permute-start.5 = (bf16[128,1024]{1,0:T(8,128)(2,1)S(1)}, bf16[128,1024]{1,0:T(8,128)(2,1)}, u32[]{:S(2)}, u32[]{:S(2)}) collective-permute-start(bf16[128,1024]{1,0:T(8,128)(2,1)S(1)} %constant_dynamic-slice_fusion.2), channel_id=1, source_target_pairs={{0,2},{1,3},{2,0},{3,1},{4,6},{5,7},{6,4},{7,5},{8,10},{9,11},{10,... | collective-permute-start | bytes 786440 | tf_op jit(solution)/shard_map/ppermute | solution.py:330
  88.0 0.1 stack.132.info_ref
  88.1 4.4 %shard_map.151 = bf16[8,4,80,128]{3,2,1,0:T(8,128)(2,1)} custom-call(s32[5]{0:T(128)S(1)} %stack.132.info_ref, bf16[8,256,128]{2,1,0:T(8,128)(2,1)S(1)} %all-to-all-done.1.q_ref, bf16[2,256,128]{2,1,0:T(8,128)(2,1)S(1)} %get-tuple-element.21.refs_0_, bf16[2,256,128]{2,1,0:T(8,128)(2,1)S(1)} %collective-permute-done.refs_1_, ...), custom_call_target="tpu_custom_call" | custom-call | flops 2147483648 | bytes 1703956 | tf_op jit(solution)/shard_map/pallas_call | solution.py:33
  92.5 0.7 collective-permute-done.3
  93.2 7.2 %collective-permute-done.4 = bf16[128,1024]{1,0:T(8,128)(2,1)} collective-permute-done((bf16[128,1024]{1,0:T(8,128)(2,1)S(1)}, bf16[128,1024]{1,0:T(8,128)(2,1)}, u32[]{:S(2)}, u32[]{:S(2)}) %collective-permute-start.4) | collective-permute-done | bytes 262176 | tf_op jit(solution)/shard_map/ppermute | solution.py:330
  100.4 5.3 %all-to-all-start.2 = ((bf16[32,80,128]{2,1,0:T(8,128)(2,1)}), bf16[32,80,128]{2,1,0:T(8,128)(2,1)}, u32[]{:S(2)}, u32[]{:S(2)}) async-start(bf16[32,80,128]{2,1,0:T(8,128)(2,1)} %bitcast.23), calls=%async_computation.2 | async-start | bytes 1310720 | tf_op jit(solution)/shard_map/all_to_all | solution.py:298
  105.7 0.0 all-gather.12.cloned.1.call-start
  105.7 1.1 pad_maximum_fusion.mine_ref
  106.8 2.3 %collective-permute-start.6 = (bf16[3,128,1024]{2,1,0:T(8,128)(2,1)S(1)}, bf16[3,128,1024]{2,1,0:T(8,128)(2,1)}, u32[]{:S(2)}, u32[]{:S(2)}) collective-permute-start(bf16[3,128,1024]{2,1,0:T(8,128)(2,1)S(1)} %pad_maximum_fusion.mine_ref), channel_id=1, source_target_pairs={{0,16},{16,0},{1,17},{17,1},{2,18},{18,2},{3,19},{19,3},{4,20},{20... | collective-permute-start | bytes 2359304 | tf_op jit(solution)/shard_map/ppermute | solution.py:330
  109.2 0.6 stack.141.info_ref
  109.8 1.6 copy-done
  111.4 3.7 %shard_map.152 = bf16[512,128]{1,0:T(8,128)(2,1)} custom-call(bf16[16,512,128]{2,1,0:T(8,128)(2,1)S(1)} %bitcast.45, f32[1,2048]{1,0:T(1,128)S(1)} %bitcast.47, bf16[2048,128]{1,0:T(8,128)(2,1)S(1)} %copy-done.5), custom_call_target="tpu_custom_call" | custom-call | flops 268435456 | bytes 2760704 | tf_op jit(solution)/shard_map/pallas_call | solution.py:33
  115.1 2.7 %all-to-all-done.2 = bf16[32,80,128]{2,1,0:T(8,128)(2,1)} async-done(((bf16[32,80,128]{2,1,0:T(8,128)(2,1)}), bf16[32,80,128]{2,1,0:T(8,128)(2,1)}, u32[]{:S(2)}, u32[]{:S(2)}) %all-to-all-start.2) | async-done | bytes 655392 | tf_op jit(solution)/shard_map/all_to_all | solution.py:298
  117.8 3.9 %shard_map.153 = bf16[4,16,2048]{2,1,0:T(8,128)(2,1)} custom-call(s32[5]{0:T(128)} %stack.141.info_ref, bf16[8,4,80,128]{3,2,1,0:T(8,128)(2,1)} %bitcast.32.r_ref, bf16[128,2048]{1,0:T(8,128)(2,1)} %own_ref.1, bf16[3,128,1024]{2,1,0:T(8,128)(2,1)} %copy-done.8, bf16[3,128,1024]{2,1,0:T(8,128)(2,1)} %collective-permute-done.6.theirs_ref), custom_call_target="tpu_custom_call" | custom-call | flops 134217728 | bytes 3014676 | tf_op jit(solution)/shard_map/pallas_call | solution.py:33
  121.8 12.5 %all_to_all.35.r_ref = bf16[4,16,2048]{2,1,0:T(8,128)(2,1)S(1)} all-to-all(bf16[4,16,2048]{2,1,0:T(8,128)(2,1)} %shard_map.153), channel_id=1, replica_groups=mesh['zl'=2,'yh'=4,'yl'=2,'c'=2,'zh'=4,'x'=4] {'zh'}, dimensions={0} | all-to-all | bytes 524288 | tf_op jit(solution)/shard_map/all_to_all | solution.py:298
  134.3 0.9 all-gather.14.cloned.1.call-done
  135.2 4.1 %collective-permute-start.7 = (bf16[4,2,1024,128]{3,2,1,0:T(8,128)(2,1)}, bf16[4,2,1024,128]{3,2,1,0:T(8,128)(2,1)}, u32[]{:S(2)}, u32[]{:S(2)}) collective-permute-start(bf16[4,2,1024,128]{3,2,1,0:T(8,128)(2,1)} %bitcast.50), channel_id=1, source_target_pairs={{0,16},{16,0},{1,17},{17,1},{2,18},{18,2},{3,19},{19,3},{4,20},{20... | collective-permute-start | bytes 6291464 | tf_op jit(solution)/shard_map/ppermute | solution.py:330
  139.4 0.0 all-gather.8.cloned.1.call-start
  139.5 14.3 %all_to_all.36 = bf16[4,16,2048]{2,1,0:T(8,128)(2,1)} all-to-all(bf16[4,16,2048]{2,1,0:T(8,128)(2,1)S(1)} %shard_map.154), channel_id=1, replica_groups=mesh['zl'=2,'yh'=4,'yl'=2,'c'=2,'zh'=4,'x'=4] {'zh'}, dimensions={0} | all-to-all | bytes 524288 | tf_op jit(solution)/shard_map/all_to_all | solution.py:298
  153.8 5.8 %shard_map.155 = bf16[4,4,2,64,128]{4,3,2,1,0:T(8,128)(2,1)} custom-call(s32[5]{0:T(128)} %stack.141.info_ref, bf16[64,2048]{1,0:T(8,128)(2,1)} %bitcast.49, f32[1,2048]{1,0:T(1,128)} %bitcast.56, bf16[4,2,1024,128]{3,2,1,0:T(8,128)(2,1)} %bitcast.51, bf16[4,2,1024,128]{3,2,1,0:T(8,128)(2,1)} %collective-permute-done.7.theirs_ref), custom_call_target="tpu_custom_call" | custom-call | flops 268435456 | bytes 4988948 | tf_op jit(solution)/shard_map/pallas_call | solution.py:33
  159.6 7.7 %all-to-all-start.5 = ((bf16[16,2,64,128]{3,2,1,0:T(8,128)(2,1)}), bf16[16,2,64,128]{3,2,1,0:T(8,128)(2,1)S(1)}, u32[]{:S(2)}, u32[]{:S(2)}) async-start(bf16[16,2,64,128]{3,2,1,0:T(8,128)(2,1)} %bitcast.52), calls=%async_computation.5 | async-start | bytes 1048576 | tf_op jit(solution)/shard_map/all_to_all | solution.py:298
  167.4 0.6 stack.127.info_ref
  168.0 15.2 %all-to-all-done.5 = bf16[16,2,64,128]{3,2,1,0:T(8,128)(2,1)S(1)} async-done(((bf16[16,2,64,128]{3,2,1,0:T(8,128)(2,1)}), bf16[16,2,64,128]{3,2,1,0:T(8,128)(2,1)S(1)}, u32[]{:S(2)}, u32[]{:S(2)}) %all-to-all-start.5) | async-done | bytes 524320 | tf_op jit(solution)/shard_map/all_to_all | solution.py:298
  183.3 0.8 copy-done.9
  184.1 8.9 %shard_map.156 = bf16[8,1,528,128]{3,2,1,0:T(8,128)(2,1)} custom-call(s32[17]{0:T(128)} %stack.127.info_ref, bf16[8,512,128]{2,1,0:T(8,128)(2,1)} %bitcast.57, bf16[4,4,2,64,128]{4,3,2,1,0:T(8,128)(2,1)} %bitcast.54), custom_call_target="tpu_custom_call" | custom-call | flops 4294967296 | bytes 2654276 | tf_op jit(solution)/shard_map/pallas_call | solution.py:33
  193.0 2.0 all-gather.8.cloned.1.call-done
  195.0 5.4 %all-to-all-start.6 = ((bf16[8,528,128]{2,1,0:T(8,128)(2,1)}), bf16[8,528,128]{2,1,0:T(8,128)(2,1)S(1)}, u32[]{:S(2)}, u32[]{:S(2)}) async-start(bf16[8,528,128]{2,1,0:T(8,128)(2,1)} %bitcast.53), calls=%async_computation.6 | async-start | bytes 2162688 | tf_op jit(solution)/shard_map/all_to_all | solution.py:298
  201.1 0.1 pad_add_fusion.info_ref
  201.2 1.5 constant_dynamic-slice_fusion
  202.6 10.1 %all-to-all-done.6.r_ref = bf16[8,528,128]{2,1,0:T(8,128)(2,1)S(1)} async-done(((bf16[8,528,128]{2,1,0:T(8,128)(2,1)}), bf16[8,528,128]{2,1,0:T(8,128)(2,1)S(1)}, u32[]{:S(2)}, u32[]{:S(2)}) %all-to-all-start.6) | async-done | bytes 1081376 | tf_op jit(solution)/shard_map/all_to_all | solution.py:298
  212.7 1.9 shard_map.157
  (31 shorter events, 0.2 us)
Async XLA Ops:
  7.2 102.6 %all-gather.10.cloned.1.call-start = ((), (), s32[]{:S(2)}) async-start(), calls=%async_computation.8 | async-start | bytes 2228224 | tf_op jit(solution)/shard_map/all_gather | solution.py:371
  9.9 36.9 %copy-start.1 = (bf16[2048,128]{1,0:T(8,128)(2,1)S(1)}, bf16[2048,128]{1,0:T(8,128)(2,1)}, u32[]{:S(2)}) copy-start(bf16[2048,128]{1,0:T(8,128)(2,1)} %wq_ref.2) | copy-start | bytes 1572868
  9.9 36.9 %copy-start.2 = (bf16[2048,128]{1,0:T(8,128)(2,1)S(1)}, bf16[2048,128]{1,0:T(8,128)(2,1)}, u32[]{:S(2)}) copy-start(bf16[2048,128]{1,0:T(8,128)(2,1)} %wk_ref.1) | copy-start | bytes 1572868
  9.9 36.9 %copy-start.3 = (bf16[2048,128]{1,0:T(8,128)(2,1)S(1)}, bf16[2048,128]{1,0:T(8,128)(2,1)}, u32[]{:S(2)}) copy-start(bf16[2048,128]{1,0:T(8,128)(2,1)} %wv_ref.1) | copy-start | bytes 1572868
  9.9 36.9 %copy-start.6 = (f32[2048]{0:T(1024)S(1)}, f32[2048]{0:T(1024)}, u32[]{:S(2)}) copy-start(f32[2048]{0:T(1024)} %param.18) | copy-start | bytes 24580
  9.9 36.8 %all-to-all-start = ((bf16[16,256,128]{2,1,0:T(8,128)(2,1)}), bf16[16,256,128]{2,1,0:T(8,128)(2,1)S(1)}, u32[]{:S(2)}, u32[]{:S(2)}) async-start(bf16[16,256,128]{2,1,0:T(8,128)(2,1)} %shard_map.149), calls=%async_computation | async-start | bytes 2097152 | tf_op jit(solution)/shard_map/all_to_all | solution.py:298
  23.5 111.7 %all-gather.14.cloned.1.call-start = ((), (), s32[]{:S(2)}) async-start(), calls=%async_computation.10 | async-start | bytes 2621440 | tf_op jit(solution)/shard_map/all_gather | solution.py:375
  49.7 0.8 copy-start.4
  50.5 27.8 %all-to-all-start.1 = ((bf16[8,256,128]{2,1,0:T(8,128)(2,1)}), bf16[8,256,128]{2,1,0:T(8,128)(2,1)S(1)}, u32[]{:S(2)}, u32[]{:S(2)}) async-start(bf16[8,256,128]{2,1,0:T(8,128)(2,1)} %copy-done.4), calls=%async_computation.1 | async-start | bytes 1048576 | tf_op jit(solution)/shard_map/all_to_all | solution.py:298
  66.0 16.5 %collective-permute-start = (bf16[2,256,128]{2,1,0:T(8,128)(2,1)S(1)}, bf16[2,256,128]{2,1,0:T(8,128)(2,1)S(1)}, u32[]{:S(2)}, u32[]{:S(2)}) collective-permute-start(bf16[2,256,128]{2,1,0:T(8,128)(2,1)S(1)} %get-tuple-element.21.refs_0_), channel_id=1, source_target_pairs={{0,64},{64,0},{128,192},{192,128},{1,65},{65,1},{129,193},{193,129... | collective-permute-start | bytes 393224 | tf_op jit(solution)/shard_map/ppermute | solution.py:330
  70.1 18.0 %collective-permute-start.1 = (bf16[2,256,128]{2,1,0:T(8,128)(2,1)S(1)}, bf16[2,256,128]{2,1,0:T(8,128)(2,1)S(1)}, u32[]{:S(2)}, u32[]{:S(2)}) collective-permute-start(bf16[2,256,128]{2,1,0:T(8,128)(2,1)S(1)} %get-tuple-element.21.refs_0_), channel_id=1, source_target_pairs={{0,128},{64,192},{128,0},{192,64},{1,129},{65,193},{129,1},{193,65... | collective-permute-start | bytes 393224 | tf_op jit(solution)/shard_map/ppermute | solution.py:330
  74.9 13.3 %collective-permute-start.2 = (bf16[2,256,128]{2,1,0:T(8,128)(2,1)S(1)}, bf16[2,256,128]{2,1,0:T(8,128)(2,1)S(1)}, u32[]{:S(2)}, u32[]{:S(2)}) collective-permute-start(bf16[2,256,128]{2,1,0:T(8,128)(2,1)S(1)} %get-tuple-element.21.refs_0_), channel_id=1, source_target_pairs={{0,192},{64,128},{128,64},{192,0},{1,193},{65,129},{129,65},{193,1... | collective-permute-start | bytes 393224 | tf_op jit(solution)/shard_map/ppermute | solution.py:330
  78.3 14.9 %collective-permute-start.3 = (bf16[128,1024]{1,0:T(8,128)(2,1)S(1)}, bf16[128,1024]{1,0:T(8,128)(2,1)S(1)}, u32[]{:S(2)}, u32[]{:S(2)}) collective-permute-start(bf16[128,1024]{1,0:T(8,128)(2,1)S(1)} %constant_dynamic-slice_fusion.2), channel_id=1, source_target_pairs={{0,1},{1,0},{2,3},{3,2},{4,5},{5,4},{6,7},{7,6},{8,9},{9,8},{10,11... | collective-permute-start | bytes 786440 | tf_op jit(solution)/shard_map/ppermute | solution.py:330
  80.6 19.8 %collective-permute-start.4 = (bf16[128,1024]{1,0:T(8,128)(2,1)S(1)}, bf16[128,1024]{1,0:T(8,128)(2,1)}, u32[]{:S(2)}, u32[]{:S(2)}) collective-permute-start(bf16[128,1024]{1,0:T(8,128)(2,1)S(1)} %constant_dynamic-slice_fusion.2), channel_id=1, source_target_pairs={{0,3},{1,2},{2,1},{3,0},{4,7},{5,6},{6,5},{7,4},{8,11},{9,10},{10,... | collective-permute-start | bytes 786440 | tf_op jit(solution)/shard_map/ppermute | solution.py:330
  82.5 17.9 %collective-permute-start.5 = (bf16[128,1024]{1,0:T(8,128)(2,1)S(1)}, bf16[128,1024]{1,0:T(8,128)(2,1)}, u32[]{:S(2)}, u32[]{:S(2)}) collective-permute-start(bf16[128,1024]{1,0:T(8,128)(2,1)S(1)} %constant_dynamic-slice_fusion.2), channel_id=1, source_target_pairs={{0,2},{1,3},{2,0},{3,1},{4,6},{5,7},{6,4},{7,5},{8,10},{9,11},{10,... | collective-permute-start | bytes 786440 | tf_op jit(solution)/shard_map/ppermute | solution.py:330
  92.5 17.3 %copy-start.5 = (bf16[2048,128]{1,0:T(8,128)(2,1)S(1)}, bf16[2048,128]{1,0:T(8,128)(2,1)}, u32[]{:S(2)}) copy-start(bf16[2048,128]{1,0:T(8,128)(2,1)} %wq_ref.3) | copy-start | bytes 1572868
  92.5 17.3 %copy-start.7 = (f32[2048]{0:T(1024)S(1)}, f32[2048]{0:T(1024)}, u32[]{:S(2)}) copy-start(f32[2048]{0:T(1024)} %param.27) | copy-start | bytes 24580
  100.4 17.4 %all-to-all-start.2 = ((bf16[32,80,128]{2,1,0:T(8,128)(2,1)}), bf16[32,80,128]{2,1,0:T(8,128)(2,1)}, u32[]{:S(2)}, u32[]{:S(2)}) async-start(bf16[32,80,128]{2,1,0:T(8,128)(2,1)} %bitcast.23), calls=%async_computation.2 | async-start | bytes 1310720 | tf_op jit(solution)/shard_map/all_to_all | solution.py:298
  105.7 62.4 %all-gather.12.cloned.1.call-start = ((), (), s32[]{:S(2)}) async-start(), calls=%async_computation.9 | async-start | bytes 1179648 | tf_op jit(solution)/shard_map/all_gather | solution.py:466
  106.8 8.3 %copy-start.8 = (bf16[3,128,1024]{2,1,0:T(8,128)(2,1)}, bf16[3,128,1024]{2,1,0:T(8,128)(2,1)S(1)}, u32[]{:S(2)}) copy-start(bf16[3,128,1024]{2,1,0:T(8,128)(2,1)S(1)} %pad_maximum_fusion.mine_ref) | copy-start | bytes 2359300
  106.8 11.0 %collective-permute-start.6 = (bf16[3,128,1024]{2,1,0:T(8,128)(2,1)S(1)}, bf16[3,128,1024]{2,1,0:T(8,128)(2,1)}, u32[]{:S(2)}, u32[]{:S(2)}) collective-permute-start(bf16[3,128,1024]{2,1,0:T(8,128)(2,1)S(1)} %pad_maximum_fusion.mine_ref), channel_id=1, source_target_pairs={{0,16},{16,0},{1,17},{17,1},{2,18},{18,2},{3,19},{19,3},{4,20},{20... | collective-permute-start | bytes 2359304 | tf_op jit(solution)/shard_map/ppermute | solution.py:330
  109.8 1.6 copy-start
  135.2 18.6 %collective-permute-start.7 = (bf16[4,2,1024,128]{3,2,1,0:T(8,128)(2,1)}, bf16[4,2,1024,128]{3,2,1,0:T(8,128)(2,1)}, u32[]{:S(2)}, u32[]{:S(2)}) collective-permute-start(bf16[4,2,1024,128]{3,2,1,0:T(8,128)(2,1)} %bitcast.50), channel_id=1, source_target_pairs={{0,16},{16,0},{1,17},{17,1},{2,18},{18,2},{3,19},{19,3},{4,20},{20... | collective-permute-start | bytes 6291464 | tf_op jit(solution)/shard_map/ppermute | solution.py:330
  139.4 55.6 %all-gather.8.cloned.1.call-start = ((), (), s32[]{:S(2)}) async-start(), calls=%async_computation.7 | async-start | bytes 1310720 | tf_op jit(solution)/shard_map/all_gather | solution.py:464
  159.6 23.6 %all-to-all-start.5 = ((bf16[16,2,64,128]{3,2,1,0:T(8,128)(2,1)}), bf16[16,2,64,128]{3,2,1,0:T(8,128)(2,1)S(1)}, u32[]{:S(2)}, u32[]{:S(2)}) async-start(bf16[16,2,64,128]{3,2,1,0:T(8,128)(2,1)} %bitcast.52), calls=%async_computation.5 | async-start | bytes 1048576 | tf_op jit(solution)/shard_map/all_to_all | solution.py:298
  183.3 0.8 copy-start.9
  195.0 17.7 %all-to-all-start.6 = ((bf16[8,528,128]{2,1,0:T(8,128)(2,1)}), bf16[8,528,128]{2,1,0:T(8,128)(2,1)S(1)}, u32[]{:S(2)}, u32[]{:S(2)}) async-start(bf16[8,528,128]{2,1,0:T(8,128)(2,1)} %bitcast.53), calls=%async_computation.6 | async-start | bytes 2162688 | tf_op jit(solution)/shard_map/all_to_all | solution.py:298
Sparse Core Ops, SparseCore 0:
  11.0 82.4 all-gather.9
  95.6 39.5 all-gather.13
  139.5 25.1 all-gather.11
  166.6 28.3 all-gather.7

commit v6 on v2

--- a/solution.py
+++ b/solution.py
@@ -353,7 +353,6 @@
     target_full = lax.all_gather(target_hidden, HEAD, axis=0)
     source_full = exchange(repeated(source_hidden, 16), HEAD)
     source_full, *out_halves = together(source_full, *out_halves)
-    out_halves.append(swapped(out_halves[0], "x", 4, 3))
     half_weights = jnp.stack([lax.dynamic_slice_in_dim(w, half, D // 2, 0) for w in (cross_key, cross_value)])
     source_full, half_weights = together(source_full, half_weights)
     mine = lax.all_gather(half_weights, "x", axis=0)
@@ -379,10 +378,12 @@
     )
     key_sets = [keys_values] + [swapped(keys_values, "yh", 4, k) for k in (1, 2, 3)]
     queries = exchange(queries, QUERY_GROUP)
-    queries, out_halves[2] = together(queries, out_halves[2])
+    queries, *out_halves = together(queries, *out_halves)
+    out_halves.append(swapped(out_halves[0], "x", 4, 3))
+    partial = attend(queries, key_sets, [(k, ()) for k in range(4)], key_info, quarter, False)
+    partial, *out_halves = together(partial, *out_halves)
     out_mine = jnp.stack(out_halves)
     out_theirs = swapped(out_mine, "c", 2, 1)
-    partial = attend(queries, key_sets, [(k, ()) for k in range(4)], key_info, quarter, False)
     partial = exchange(partial.reshape(32, rows // 4 + 16, 128), QUERY_GROUP + ("x",))
     target_queries = call(
         target_kernel,

time: 218 us -> 220 us (level)
  blocking collectives: 26.5 us -> 29.6 us
  starting transfers between devices: 75.8 us -> 73 us
    all_to_all x5, waiting for transfers between devices: 24 us -> 28.1 us  [exchange(): return lax.all_to_all(x, axes, 0, 0, tiled=True)]
    all_gather x1, waiting for transfers between devices: 5.85 us -> 1.86 us  [shards(): encoder_full = lax.all_gather(encoder_rows, 'x', axis=0, tiled=True)]
    all_to_all x2, blocking collectives: 26.5 us -> 29.6 us  [exchange(): return lax.all_to_all(x, axes, 0, 0, tiled=True)]
    all_gather x1, waiting for transfers between devices: 0.01 us -> 2.45 us  [shards(): mine = lax.all_gather(half_weights, 'x', axis=0)]
    ppermute x8, starting transfers between devices: 27.4 us -> 25 us  [swapped(): return lax.ppermute(x, axis, [(i, i ^ by) for i in range(size)])]
  transfers between devices with their start and end apart: 17 -> 17, of which waited for: 9 -> 10; matrix products, arithmetic and copies ran while one was open for 3% -> 3% of each run, Pallas kernels for 15% -> 15%
where the time goes in v6:
time: 220 us; the launch traced here: 217 us
  starting transfers between devices  73 us (33%)
  waiting for transfers between devices  55.1 us (25%)
  Pallas kernels  33.7 us (15%)
  blocking collectives  29.6 us (13%)
  between operations  15.4 us (7%)
  local copies, waits for them, and re-layouts  8.21 us (4%)
    all_to_all x5, starting transfers between devices, exchange(): return lax.all_to_all(x, axes, 0, 0, tiled=True)  47.8 us
    pallas_call x9, Pallas kernels, call(): pl.pallas_call(kernel, out_shape=out_shape, in_specs=specs, out_specs=jax...  33.7 us
    all_to_all x2, blocking collectives, exchange(): return lax.all_to_all(x, axes, 0, 0, tiled=True)  29.6 us
    all_to_all x5, waiting for transfers between devices, exchange(): return lax.all_to_all(x, axes, 0, 0, tiled=True)  28.1 us
    ppermute x8, starting transfers between devices, swapped(): return lax.ppermute(x, axis, [(i, i ^ by) for i in range(size)])  25 us
    ppermute x8, waiting for transfers between devices, swapped(): return lax.ppermute(x, axis, [(i, i ^ by) for i in range(size)])  22 us
  transfers between devices with their start and end apart: 17, of which 10 were waited for; matrix products, arithmetic and copies ran while one was open for 3% of the time, Pallas kernels for 15%

profile of v6, /device:TPU:1, one launch (start us, length us, event | category | flops | bytes accessed | tf_op | source)
XLA Modules:
  0.0 217.1 jit_solution(3243185206266312497)
XLA Ops:
  7.2 0.7 all-gather.10.cloned.1.call-update
  7.9 2.0 shard_map.149
  9.9 13.4 %all-to-all-start = ((bf16[16,256,128]{2,1,0:T(8,128)(2,1)}), bf16[16,256,128]{2,1,0:T(8,128)(2,1)S(1)}, u32[]{:S(2)}, u32[]{:S(2)}) async-start(bf16[16,256,128]{2,1,0:T(8,128)(2,1)} %shard_map.149), calls=%async_computation | async-start | bytes 2097152 | tf_op jit(solution)/shard_map/all_to_all | solution.py:288
  23.4 0.0 all-gather.14.cloned.1.call-start
  23.4 1.1 constant_dynamic-slice_fusion.2
  24.5 3.3 %collective-permute-start = (bf16[128,1024]{1,0:T(8,128)(2,1)S(1)}, bf16[128,1024]{1,0:T(8,128)(2,1)}, u32[]{:S(2)}, u32[]{:S(2)}) collective-permute-start(bf16[128,1024]{1,0:T(8,128)(2,1)S(1)} %constant_dynamic-slice_fusion.2), channel_id=1, source_target_pairs={{0,1},{1,0},{2,3},{3,2},{4,5},{5,4},{6,7},{7,6},{8,9},{9,8},{10,11... | collective-permute-start | bytes 786440 | tf_op jit(solution)/shard_map/ppermute | solution.py:310
  27.8 3.7 %collective-permute-start.1 = (bf16[128,1024]{1,0:T(8,128)(2,1)S(1)}, bf16[128,1024]{1,0:T(8,128)(2,1)}, u32[]{:S(2)}, u32[]{:S(2)}) collective-permute-start(bf16[128,1024]{1,0:T(8,128)(2,1)S(1)} %constant_dynamic-slice_fusion.2), channel_id=1, source_target_pairs={{0,3},{1,2},{2,1},{3,0},{4,7},{5,6},{6,5},{7,4},{8,11},{9,10},{10,... | collective-permute-start | bytes 786440 | tf_op jit(solution)/shard_map/ppermute | solution.py:310
  31.5 1.1 dynamic-slice_bitcast_fusion
  32.6 0.8 pad_maximum_fusion.1
  33.4 7.7 %collective-permute-done = bf16[128,1024]{1,0:T(8,128)(2,1)} collective-permute-done((bf16[128,1024]{1,0:T(8,128)(2,1)S(1)}, bf16[128,1024]{1,0:T(8,128)(2,1)}, u32[]{:S(2)}, u32[]{:S(2)}) %collective-permute-start) | collective-permute-done | bytes 262176 | tf_op jit(solution)/shard_map/ppermute | solution.py:310
  41.1 5.5 %collective-permute-done.1 = bf16[128,1024]{1,0:T(8,128)(2,1)} collective-permute-done((bf16[128,1024]{1,0:T(8,128)(2,1)S(1)}, bf16[128,1024]{1,0:T(8,128)(2,1)}, u32[]{:S(2)}, u32[]{:S(2)}) %collective-permute-start.1) | collective-permute-done | bytes 262176 | tf_op jit(solution)/shard_map/ppermute | solution.py:310
  46.7 2.9 %shard_map.150 = (bf16[8,256,128]{2,1,0:T(8,128)(2,1)S(1)}, bf16[2,256,128]{2,1,0:T(8,128)(2,1)S(1)}) custom-call(bf16[16,256,128]{2,1,0:T(8,128)(2,1)S(1)} %all-to-all-done.x_ref, f32[1,2048]{1,0:T(1,128)S(1)} %bitcast.46, bf16[2048,128]{1,0:T(8,128)(2,1)S(1)} %copy-done.1, bf16[2048,128]{1,0:T(8,128)(2,1)S(1)} %copy-done.2, bf16[2048,128]{1,0:T(8,128)(2,1)S(1)} %copy-done.3), custom_call_target="tpu_custom_call" | custom-call | flops 402653184 | bytes 3284992 | tf_op jit(solution)/shard_map/pallas_call | solution.py:33
  49.6 0.8 copy-done.4
  50.4 15.4 %all-to-all-start.1 = ((bf16[8,256,128]{2,1,0:T(8,128)(2,1)}), bf16[8,256,128]{2,1,0:T(8,128)(2,1)S(1)}, u32[]{:S(2)}, u32[]{:S(2)}) async-start(bf16[8,256,128]{2,1,0:T(8,128)(2,1)} %copy-done.4), calls=%async_computation.1 | async-start | bytes 1048576 | tf_op jit(solution)/shard_map/all_to_all | solution.py:288
  65.8 4.2 %collective-permute-start.2 = (bf16[2,256,128]{2,1,0:T(8,128)(2,1)S(1)}, bf16[2,256,128]{2,1,0:T(8,128)(2,1)S(1)}, u32[]{:S(2)}, u32[]{:S(2)}) collective-permute-start(bf16[2,256,128]{2,1,0:T(8,128)(2,1)S(1)} %get-tuple-element.28.refs_0_), channel_id=1, source_target_pairs={{0,64},{64,0},{128,192},{192,128},{1,65},{65,1},{129,193},{193,129... | collective-permute-start | bytes 393224 | tf_op jit(solution)/shard_map/ppermute | solution.py:310
  70.0 4.7 %collective-permute-start.3 = (bf16[2,256,128]{2,1,0:T(8,128)(2,1)S(1)}, bf16[2,256,128]{2,1,0:T(8,128)(2,1)S(1)}, u32[]{:S(2)}, u32[]{:S(2)}) collective-permute-start(bf16[2,256,128]{2,1,0:T(8,128)(2,1)S(1)} %get-tuple-element.28.refs_0_), channel_id=1, source_target_pairs={{0,128},{64,192},{128,0},{192,64},{1,129},{65,193},{129,1},{193,65... | collective-permute-start | bytes 393224 | tf_op jit(solution)/shard_map/ppermute | solution.py:310
  74.7 2.5 %collective-permute-start.4 = (bf16[2,256,128]{2,1,0:T(8,128)(2,1)S(1)}, bf16[2,256,128]{2,1,0:T(8,128)(2,1)S(1)}, u32[]{:S(2)}, u32[]{:S(2)}) collective-permute-start(bf16[2,256,128]{2,1,0:T(8,128)(2,1)S(1)} %get-tuple-element.28.refs_0_), channel_id=1, source_target_pairs={{0,192},{64,128},{128,64},{192,0},{1,193},{65,129},{129,65},{193,1... | collective-permute-start | bytes 393224 | tf_op jit(solution)/shard_map/ppermute | solution.py:310
  77.2 1.9 collective-permute-start.5
  79.8 0.1 stack.132.info_ref
  79.9 3.2 %collective-permute-done.3.refs_2_ = bf16[2,256,128]{2,1,0:T(8,128)(2,1)S(1)} collective-permute-done((bf16[2,256,128]{2,1,0:T(8,128)(2,1)S(1)}, bf16[2,256,128]{2,1,0:T(8,128)(2,1)S(1)}, u32[]{:S(2)}, u32[]{:S(2)}) %collective-permute-start.3) | collective-permute-done | bytes 131104 | tf_op jit(solution)/shard_map/ppermute | solution.py:310
  83.1 4.5 %collective-permute-done.4.refs_3_ = bf16[2,256,128]{2,1,0:T(8,128)(2,1)S(1)} collective-permute-done((bf16[2,256,128]{2,1,0:T(8,128)(2,1)S(1)}, bf16[2,256,128]{2,1,0:T(8,128)(2,1)S(1)}, u32[]{:S(2)}, u32[]{:S(2)}) %collective-permute-start.4) | collective-permute-done | bytes 131104 | tf_op jit(solution)/shard_map/ppermute | solution.py:310
  87.6 4.4 %shard_map.151 = bf16[8,4,80,128]{3,2,1,0:T(8,128)(2,1)} custom-call(s32[5]{0:T(128)S(1)} %stack.132.info_ref, bf16[8,256,128]{2,1,0:T(8,128)(2,1)S(1)} %all-to-all-done.1.q_ref, bf16[2,256,128]{2,1,0:T(8,128)(2,1)S(1)} %get-tuple-element.28.refs_0_, bf16[2,256,128]{2,1,0:T(8,128)(2,1)S(1)} %collective-permute-done.2.refs_1_, ...), custom_call_target="tpu_custom_call" | custom-call | flops 2147483648 | bytes 1703956 | tf_op jit(solution)/shard_map/pallas_call | solution.py:33
  92.0 1.0 collective-permute-done.5
  93.0 5.9 %all-to-all-start.2 = ((bf16[32,80,128]{2,1,0:T(8,128)(2,1)}), bf16[32,80,128]{2,1,0:T(8,128)(2,1)}, u32[]{:S(2)}, u32[]{:S(2)}) async-start(bf16[32,80,128]{2,1,0:T(8,128)(2,1)} %bitcast.23), calls=%async_computation.2 | async-start | bytes 1310720 | tf_op jit(solution)/shard_map/all_to_all | solution.py:288
  98.9 0.0 all-gather.12.cloned.1.call-start
  98.9 1.1 pad_maximum_fusion.mine_ref
  100.1 2.2 %collective-permute-start.6 = (bf16[3,128,1024]{2,1,0:T(8,128)(2,1)S(1)}, bf16[3,128,1024]{2,1,0:T(8,128)(2,1)}, u32[]{:S(2)}, u32[]{:S(2)}) collective-permute-start(bf16[3,128,1024]{2,1,0:T(8,128)(2,1)S(1)} %pad_maximum_fusion.mine_ref), channel_id=1, source_target_pairs={{0,16},{16,0},{1,17},{17,1},{2,18},{18,2},{3,19},{19,3},{4,20},{20... | collective-permute-start | bytes 2359304 | tf_op jit(solution)/shard_map/ppermute | solution.py:310
  102.3 0.6 stack.141.info_ref
  102.9 1.6 copy-done
  104.5 3.7 %shard_map.152 = bf16[512,128]{1,0:T(8,128)(2,1)} custom-call(bf16[16,512,128]{2,1,0:T(8,128)(2,1)S(1)} %bitcast.45, f32[1,2048]{1,0:T(1,128)S(1)} %bitcast.47, bf16[2048,128]{1,0:T(8,128)(2,1)S(1)} %copy-done.5), custom_call_target="tpu_custom_call" | custom-call | flops 268435456 | bytes 2760704 | tf_op jit(solution)/shard_map/pallas_call | solution.py:33
  108.2 2.7 %all-to-all-done.2 = bf16[32,80,128]{2,1,0:T(8,128)(2,1)} async-done(((bf16[32,80,128]{2,1,0:T(8,128)(2,1)}), bf16[32,80,128]{2,1,0:T(8,128)(2,1)}, u32[]{:S(2)}, u32[]{:S(2)}) %all-to-all-start.2) | async-done | bytes 655392 | tf_op jit(solution)/shard_map/all_to_all | solution.py:288
  111.0 3.9 %shard_map.153 = bf16[4,16,2048]{2,1,0:T(8,128)(2,1)} custom-call(s32[5]{0:T(128)} %stack.141.info_ref, bf16[8,4,80,128]{3,2,1,0:T(8,128)(2,1)} %bitcast.32.r_ref, bf16[128,2048]{1,0:T(8,128)(2,1)} %own_ref.1, bf16[3,128,1024]{2,1,0:T(8,128)(2,1)} %copy-done.8, bf16[3,128,1024]{2,1,0:T(8,128)(2,1)} %collective-permute-done.6.theirs_ref), custom_call_target="tpu_custom_call" | custom-call | flops 134217728 | bytes 3014676 | tf_op jit(solution)/shard_map/pallas_call | solution.py:33
  114.9 12.7 %all_to_all.35.r_ref = bf16[4,16,2048]{2,1,0:T(8,128)(2,1)S(1)} all-to-all(bf16[4,16,2048]{2,1,0:T(8,128)(2,1)} %shard_map.153), channel_id=1, replica_groups=mesh['zl'=2,'yh'=4,'yl'=2,'c'=2,'zh'=4,'x'=4] {'zh'}, dimensions={0} | all-to-all | bytes 524288 | tf_op jit(solution)/shard_map/all_to_all | solution.py:288
  127.6 2.4 %all-gather.14.cloned.1.call-done = bf16[8,1024,128]{2,1,0:T(8,128)(2,1)} async-done(((bf16[2,1024,128]{2,1,0:T(8,128)(2,1)}), bf16[8,1024,128]{2,1,0:T(8,128)(2,1)}) %all-gather.14.cloned.1.call-update) | async-done | bytes 2097168 | tf_op jit(solution)/shard_map/all_gather | solution.py:358
  130.1 2.6 %collective-permute-start.7 = (bf16[4,2,1024,128]{3,2,1,0:T(8,128)(2,1)}, bf16[4,2,1024,128]{3,2,1,0:T(8,128)(2,1)}, u32[]{:S(2)}, u32[]{:S(2)}) collective-permute-start(bf16[4,2,1024,128]{3,2,1,0:T(8,128)(2,1)} %bitcast.50), channel_id=1, source_target_pairs={{0,16},{16,0},{1,17},{17,1},{2,18},{18,2},{3,19},{19,3},{4,20},{20... | collective-permute-start | bytes 6291464 | tf_op jit(solution)/shard_map/ppermute | solution.py:310
  132.8 16.9 %all_to_all.36 = bf16[4,16,2048]{2,1,0:T(8,128)(2,1)} all-to-all(bf16[4,16,2048]{2,1,0:T(8,128)(2,1)S(1)} %shard_map.154), channel_id=1, replica_groups=mesh['zl'=2,'yh'=4,'yl'=2,'c'=2,'zh'=4,'x'=4] {'zh'}, dimensions={0} | all-to-all | bytes 524288 | tf_op jit(solution)/shard_map/all_to_all | solution.py:288
  149.8 5.8 %shard_map.155 = bf16[4,4,2,64,128]{4,3,2,1,0:T(8,128)(2,1)} custom-call(s32[5]{0:T(128)} %stack.141.info_ref, bf16[64,2048]{1,0:T(8,128)(2,1)} %bitcast.49, f32[1,2048]{1,0:T(1,128)} %bitcast.56, bf16[4,2,1024,128]{3,2,1,0:T(8,128)(2,1)} %bitcast.51, bf16[4,2,1024,128]{3,2,1,0:T(8,128)(2,1)} %collective-permute-done.7.theirs_ref), custom_call_target="tpu_custom_call" | custom-call | flops 268435456 | bytes 4988948 | tf_op jit(solution)/shard_map/pallas_call | solution.py:33
  155.6 7.7 %all-to-all-start.5 = ((bf16[16,2,64,128]{3,2,1,0:T(8,128)(2,1)}), bf16[16,2,64,128]{3,2,1,0:T(8,128)(2,1)S(1)}, u32[]{:S(2)}, u32[]{:S(2)}) async-start(bf16[16,2,64,128]{3,2,1,0:T(8,128)(2,1)} %bitcast.52), calls=%async_computation.5 | async-start | bytes 1048576 | tf_op jit(solution)/shard_map/all_to_all | solution.py:288
  163.3 0.6 stack.127.info_ref
  164.0 15.3 %all-to-all-done.5 = bf16[16,2,64,128]{3,2,1,0:T(8,128)(2,1)S(1)} async-done(((bf16[16,2,64,128]{3,2,1,0:T(8,128)(2,1)}), bf16[16,2,64,128]{3,2,1,0:T(8,128)(2,1)S(1)}, u32[]{:S(2)}, u32[]{:S(2)}) %all-to-all-start.5) | async-done | bytes 524320 | tf_op jit(solution)/shard_map/all_to_all | solution.py:288
  179.3 0.8 copy-done.9
  180.0 9.1 %shard_map.156 = bf16[8,1,528,128]{3,2,1,0:T(8,128)(2,1)} custom-call(s32[17]{0:T(128)} %stack.127.info_ref, bf16[8,512,128]{2,1,0:T(8,128)(2,1)} %bitcast.57, bf16[4,4,2,64,128]{4,3,2,1,0:T(8,128)(2,1)} %bitcast.54), custom_call_target="tpu_custom_call" | custom-call | flops 4294967296 | bytes 2654276 | tf_op jit(solution)/shard_map/pallas_call | solution.py:33
  189.1 1.9 all-gather.8.cloned.1.call-done
  191.0 5.4 %all-to-all-start.6 = ((bf16[8,528,128]{2,1,0:T(8,128)(2,1)}), bf16[8,528,128]{2,1,0:T(8,128)(2,1)S(1)}, u32[]{:S(2)}, u32[]{:S(2)}) async-start(bf16[8,528,128]{2,1,0:T(8,128)(2,1)} %bitcast.53), calls=%async_computation.6 | async-start | bytes 2162688 | tf_op jit(solution)/shard_map/all_to_all | solution.py:288
  197.0 0.1 pad_add_fusion.info_ref
  197.1 1.5 constant_dynamic-slice_fusion
  198.6 10.1 %all-to-all-done.6.r_ref = bf16[8,528,128]{2,1,0:T(8,128)(2,1)S(1)} async-done(((bf16[8,528,128]{2,1,0:T(8,128)(2,1)}), bf16[8,528,128]{2,1,0:T(8,128)(2,1)S(1)}, u32[]{:S(2)}, u32[]{:S(2)}) %all-to-all-start.6) | async-done | bytes 1081376 | tf_op jit(solution)/shard_map/all_to_all | solution.py:288
  208.7 1.9 shard_map.157
  (31 shorter events, 0.3 us)
Async XLA Ops:
  7.2 95.8 %all-gather.10.cloned.1.call-start = ((), (), s32[]{:S(2)}) async-start(), calls=%async_computation.8 | async-start | bytes 2228224 | tf_op jit(solution)/shard_map/all_gather | solution.py:353
  9.9 36.8 %all-to-all-start = ((bf16[16,256,128]{2,1,0:T(8,128)(2,1)}), bf16[16,256,128]{2,1,0:T(8,128)(2,1)S(1)}, u32[]{:S(2)}, u32[]{:S(2)}) async-start(bf16[16,256,128]{2,1,0:T(8,128)(2,1)} %shard_map.149), calls=%async_computation | async-start | bytes 2097152 | tf_op jit(solution)/shard_map/all_to_all | solution.py:288
  23.3 23.3 %copy-start.1 = (bf16[2048,128]{1,0:T(8,128)(2,1)S(1)}, bf16[2048,128]{1,0:T(8,128)(2,1)}, u32[]{:S(2)}) copy-start(bf16[2048,128]{1,0:T(8,128)(2,1)} %wq_ref.2) | copy-start | bytes 1572868
  23.3 23.3 %copy-start.2 = (bf16[2048,128]{1,0:T(8,128)(2,1)S(1)}, bf16[2048,128]{1,0:T(8,128)(2,1)}, u32[]{:S(2)}) copy-start(bf16[2048,128]{1,0:T(8,128)(2,1)} %wk_ref.1) | copy-start | bytes 1572868
  23.3 23.3 %copy-start.3 = (bf16[2048,128]{1,0:T(8,128)(2,1)S(1)}, bf16[2048,128]{1,0:T(8,128)(2,1)}, u32[]{:S(2)}) copy-start(bf16[2048,128]{1,0:T(8,128)(2,1)} %wv_ref.1) | copy-start | bytes 1572868
  23.4 23.3 %copy-start.6 = (f32[2048]{0:T(1024)S(1)}, f32[2048]{0:T(1024)}, u32[]{:S(2)}) copy-start(f32[2048]{0:T(1024)} %param.18) | copy-start | bytes 24580
  23.4 106.7 %all-gather.14.cloned.1.call-start = ((), (), s32[]{:S(2)}) async-start(), calls=%async_computation.10 | async-start | bytes 2621440 | tf_op jit(solution)/shard_map/all_gather | solution.py:358
  24.5 16.7 %collective-permute-start = (bf16[128,1024]{1,0:T(8,128)(2,1)S(1)}, bf16[128,1024]{1,0:T(8,128)(2,1)}, u32[]{:S(2)}, u32[]{:S(2)}) collective-permute-start(bf16[128,1024]{1,0:T(8,128)(2,1)S(1)} %constant_dynamic-slice_fusion.2), channel_id=1, source_target_pairs={{0,1},{1,0},{2,3},{3,2},{4,5},{5,4},{6,7},{7,6},{8,9},{9,8},{10,11... | collective-permute-start | bytes 786440 | tf_op jit(solution)/shard_map/ppermute | solution.py:310
  27.8 18.9 %collective-permute-start.1 = (bf16[128,1024]{1,0:T(8,128)(2,1)S(1)}, bf16[128,1024]{1,0:T(8,128)(2,1)}, u32[]{:S(2)}, u32[]{:S(2)}) collective-permute-start(bf16[128,1024]{1,0:T(8,128)(2,1)S(1)} %constant_dynamic-slice_fusion.2), channel_id=1, source_target_pairs={{0,3},{1,2},{2,1},{3,0},{4,7},{5,6},{6,5},{7,4},{8,11},{9,10},{10,... | collective-permute-start | bytes 786440 | tf_op jit(solution)/shard_map/ppermute | solution.py:310
  49.6 0.8 copy-start.4
  50.4 26.8 %all-to-all-start.1 = ((bf16[8,256,128]{2,1,0:T(8,128)(2,1)}), bf16[8,256,128]{2,1,0:T(8,128)(2,1)S(1)}, u32[]{:S(2)}, u32[]{:S(2)}) async-start(bf16[8,256,128]{2,1,0:T(8,128)(2,1)} %copy-done.4), calls=%async_computation.1 | async-start | bytes 1048576 | tf_op jit(solution)/shard_map/all_to_all | solution.py:288
  65.8 14.1 %collective-permute-start.2 = (bf16[2,256,128]{2,1,0:T(8,128)(2,1)S(1)}, bf16[2,256,128]{2,1,0:T(8,128)(2,1)S(1)}, u32[]{:S(2)}, u32[]{:S(2)}) collective-permute-start(bf16[2,256,128]{2,1,0:T(8,128)(2,1)S(1)} %get-tuple-element.28.refs_0_), channel_id=1, source_target_pairs={{0,64},{64,0},{128,192},{192,128},{1,65},{65,1},{129,193},{193,129... | collective-permute-start | bytes 393224 | tf_op jit(solution)/shard_map/ppermute | solution.py:310
  70.0 13.1 %collective-permute-start.3 = (bf16[2,256,128]{2,1,0:T(8,128)(2,1)S(1)}, bf16[2,256,128]{2,1,0:T(8,128)(2,1)S(1)}, u32[]{:S(2)}, u32[]{:S(2)}) collective-permute-start(bf16[2,256,128]{2,1,0:T(8,128)(2,1)S(1)} %get-tuple-element.28.refs_0_), channel_id=1, source_target_pairs={{0,128},{64,192},{128,0},{192,64},{1,129},{65,193},{129,1},{193,65... | collective-permute-start | bytes 393224 | tf_op jit(solution)/shard_map/ppermute | solution.py:310
  74.7 12.9 %collective-permute-start.4 = (bf16[2,256,128]{2,1,0:T(8,128)(2,1)S(1)}, bf16[2,256,128]{2,1,0:T(8,128)(2,1)S(1)}, u32[]{:S(2)}, u32[]{:S(2)}) collective-permute-start(bf16[2,256,128]{2,1,0:T(8,128)(2,1)S(1)} %get-tuple-element.28.refs_0_), channel_id=1, source_target_pairs={{0,192},{64,128},{128,64},{192,0},{1,193},{65,129},{129,65},{193,1... | collective-permute-start | bytes 393224 | tf_op jit(solution)/shard_map/ppermute | solution.py:310
  77.2 15.8 %collective-permute-start.5 = (bf16[128,1024]{1,0:T(8,128)(2,1)}, bf16[128,1024]{1,0:T(8,128)(2,1)S(1)}, u32[]{:S(2)}, u32[]{:S(2)}) collective-permute-start(bf16[128,1024]{1,0:T(8,128)(2,1)} %collective-permute-done), channel_id=1, source_target_pairs={{0,3},{1,2},{2,1},{3,0},{4,7},{5,6},{6,5},{7,4},{8,11},{9,10},{10,... | collective-permute-start | bytes 786440 | tf_op jit(solution)/shard_map/ppermute | solution.py:310
  92.0 10.9 %copy-start.5 = (bf16[2048,128]{1,0:T(8,128)(2,1)S(1)}, bf16[2048,128]{1,0:T(8,128)(2,1)}, u32[]{:S(2)}) copy-start(bf16[2048,128]{1,0:T(8,128)(2,1)} %wq_ref.3) | copy-start | bytes 1572868
  92.0 10.9 %copy-start.7 = (f32[2048]{0:T(1024)S(1)}, f32[2048]{0:T(1024)}, u32[]{:S(2)}) copy-start(f32[2048]{0:T(1024)} %param.27) | copy-start | bytes 24580
  93.0 18.0 %all-to-all-start.2 = ((bf16[32,80,128]{2,1,0:T(8,128)(2,1)}), bf16[32,80,128]{2,1,0:T(8,128)(2,1)}, u32[]{:S(2)}, u32[]{:S(2)}) async-start(bf16[32,80,128]{2,1,0:T(8,128)(2,1)} %bitcast.23), calls=%async_computation.2 | async-start | bytes 1310720 | tf_op jit(solution)/shard_map/all_to_all | solution.py:288
  98.9 65.1 %all-gather.12.cloned.1.call-start = ((), (), s32[]{:S(2)}) async-start(), calls=%async_computation.9 | async-start | bytes 1179648 | tf_op jit(solution)/shard_map/all_gather | solution.py:448
  100.1 8.2 %copy-start.8 = (bf16[3,128,1024]{2,1,0:T(8,128)(2,1)}, bf16[3,128,1024]{2,1,0:T(8,128)(2,1)S(1)}, u32[]{:S(2)}) copy-start(bf16[3,128,1024]{2,1,0:T(8,128)(2,1)S(1)} %pad_maximum_fusion.mine_ref) | copy-start | bytes 2359300
  100.1 10.9 %collective-permute-start.6 = (bf16[3,128,1024]{2,1,0:T(8,128)(2,1)S(1)}, bf16[3,128,1024]{2,1,0:T(8,128)(2,1)}, u32[]{:S(2)}, u32[]{:S(2)}) collective-permute-start(bf16[3,128,1024]{2,1,0:T(8,128)(2,1)S(1)} %pad_maximum_fusion.mine_ref), channel_id=1, source_target_pairs={{0,16},{16,0},{1,17},{17,1},{2,18},{18,2},{3,19},{19,3},{4,20},{20... | collective-permute-start | bytes 2359304 | tf_op jit(solution)/shard_map/ppermute | solution.py:310
  102.9 1.6 copy-start
  130.1 19.7 %collective-permute-start.7 = (bf16[4,2,1024,128]{3,2,1,0:T(8,128)(2,1)}, bf16[4,2,1024,128]{3,2,1,0:T(8,128)(2,1)}, u32[]{:S(2)}, u32[]{:S(2)}) collective-permute-start(bf16[4,2,1024,128]{3,2,1,0:T(8,128)(2,1)} %bitcast.50), channel_id=1, source_target_pairs={{0,16},{16,0},{1,17},{17,1},{2,18},{18,2},{3,19},{19,3},{4,20},{20... | collective-permute-start | bytes 6291464 | tf_op jit(solution)/shard_map/ppermute | solution.py:310
  132.7 58.3 %all-gather.8.cloned.1.call-start = ((), (), s32[]{:S(2)}) async-start(), calls=%async_computation.7 | async-start | bytes 1310720 | tf_op jit(solution)/shard_map/all_gather | solution.py:446
  155.6 23.6 %all-to-all-start.5 = ((bf16[16,2,64,128]{3,2,1,0:T(8,128)(2,1)}), bf16[16,2,64,128]{3,2,1,0:T(8,128)(2,1)S(1)}, u32[]{:S(2)}, u32[]{:S(2)}) async-start(bf16[16,2,64,128]{3,2,1,0:T(8,128)(2,1)} %bitcast.52), calls=%async_computation.5 | async-start | bytes 1048576 | tf_op jit(solution)/shard_map/all_to_all | solution.py:288
  179.2 0.8 copy-start.9
  191.0 17.7 %all-to-all-start.6 = ((bf16[8,528,128]{2,1,0:T(8,128)(2,1)}), bf16[8,528,128]{2,1,0:T(8,128)(2,1)S(1)}, u32[]{:S(2)}, u32[]{:S(2)}) async-start(bf16[8,528,128]{2,1,0:T(8,128)(2,1)} %bitcast.53), calls=%async_computation.6 | async-start | bytes 2162688 | tf_op jit(solution)/shard_map/all_to_all | solution.py:288
Sparse Core Ops, SparseCore 0:
  11.0 82.0 all-gather.9
  95.2 34.8 all-gather.13
  132.8 27.7 all-gather.11
  162.6 28.3 all-gather.7
